TPU v7x, 32 devices: a whole 2x2x4 slice. The times are simulated.
32 devices in a mesh: seq: 8 (over y, x, core), head: 4 (over z).
Axes of the slice: x: 2, y: 2, z: 4, core: 2. Of those that a mesh axis runs over, the one named last changes fastest.
Arguments:
- queries: bfloat16 [2, 2048, 20, 128], P(None, ('seq', 'head')), may hold values from -96 to 96
- grad_out: bfloat16 [2, 2048, 20, 128], P(None, ('seq', 'head')), may hold values from -6 to 6
- keys: bfloat16 [2048, 4, 128], P('seq', 'head'), may hold values from -6 to 6
- values: bfloat16 [2048, 4, 128], P('seq', 'head'), may hold values from -6 to 6
- doc_start: int32 [2048], replicated, may hold values from 0 to 2047, as said below
Outputs:
- query_grads: bfloat16 [2, 2048, 20, 128], P(None, ('seq', 'head'))
- key_grads: bfloat16 [2048, 4, 128], P('seq', 'head')
- value_grads: bfloat16 [2048, 4, 128], P('seq', 'head')
Inputs may be any that keep to these rules, and one draw needn't show every extreme that they name: doc_start[i] is the first position of token i's document, so doc_start[i] <= i; it is 0 for every token before position 1024, at most four documents begin at or after it, and the last token begins a document of its own.
All inputs are finite; a program needn't handle non-finite values.
Results may differ from a plain program's by a relative error of at most 0.005.
Values may be sent and summed in bfloat16 or wider, within the bound.
No kernel may reach another device: no remote copies, remote signals or barrier semaphores. Data moves between devices by JAX's collectives and lax.ppermute only.
A program may use at most 128 MiB of HBM per device.

v0:
```python
import functools
import math

import jax
import jax.numpy as jnp
from jax import lax
from jax.experimental import pallas as pl
from jax.experimental.pallas import tpu as pltpu
from jax.sharding import PartitionSpec as P

NEG = -1e30
KEY_BLOCK = 256
VMEM_LIMIT = 48 * 1024 * 1024
SCORE_BYTES = 24 * 1024 * 1024


def attention_kernel(column_count, group_lanes, merged, doc_ref, doc_rows_ref, *refs):
    chunk_refs = refs[:2]
    kv_refs = refs[2 : 2 + column_count]
    kv_other = refs[2 + column_count : 2 + 2 * column_count]
    if merged:
        kv_other = [refs[2 + column_count].at[d] for d in range(column_count)]
    (
        dq_own, dq_send, kept_ref, sent_ref,
        q_rows, g_rows, q_cols, g_cols, keys, values,
        e_scr, d_scr, m_scr, max_scr, sum_scr, weight_scr, dqt, dk_acc, dv_acc,
    ) = refs[-19:]
    layers, group, tokens, width = dq_own.shape
    block_tokens = kv_refs[0].shape[1]
    pair = 2 * tokens
    heads = layers * group
    lanes = heads * pair
    wide = 2 * pair
    scale = 1.0 / math.sqrt(width)
    exp_scale = scale * math.log2(math.e)
    s = lax.axis_index("seq")
    z = lax.axis_index("head")
    column, core, z_pair, z_bit = s // 2, s % 2, z // 2, z % 2

    first = (column * 2 + core) * block_tokens + z_pair * pair
    last = first + pair - 1
    low = doc_ref[first] // KEY_BLOCK
    high = last // KEY_BLOCK + 1
    open_from = doc_ref[last]
    starts = doc_rows_ref[pl.ds(first // pair, 1), :]
    places = first + lax.broadcasted_iota(jnp.int32, (1, pair), 1)

    for d in range(column_count):
        for b in range(2):
            start = pl.multiple_of(((column ^ d) * 2 + (core ^ b)) * block_tokens, block_tokens)

            @pl.when((start <= last) & (start + block_tokens > low * KEY_BLOCK))
            def _():
                block = kv_other[d] if b else kv_refs[d]
                keys[pl.ds(start, block_tokens), :] = block[0]
                values[pl.ds(start, block_tokens), :] = block[1]

    dk_acc[...] = jnp.zeros_like(dk_acc)
    dv_acc[...] = jnp.zeros_like(dv_acc)
    for layer in range(layers):
        for h in range(group):
            n = layer * group + h
            for dz in range(2):
                at = pl.multiple_of((z_bit ^ dz) * tokens, tokens)
                q_rows[n, pl.ds(at, tokens), :] = chunk_refs[dz][0, layer, h]
                g_rows[n, pl.ds(at, tokens), :] = chunk_refs[dz][1, layer, h]
            q_cols[:, n * pair : (n + 1) * pair] = q_rows[n].T
            g_cols[:, n * pair : (n + 1) * pair] = g_rows[n].T

    for left in range(0, lanes, group_lanes):
        max_scr[...] = jnp.full_like(max_scr, NEG)
        sum_scr[...] = jnp.zeros_like(sum_scr)
        weight_scr[...] = jnp.zeros_like(weight_scr)

        def stats(j, _):
            key_start = pl.multiple_of(j * KEY_BLOCK, KEY_BLOCK)
            rows = pl.ds(key_start, KEY_BLOCK)
            key_block = keys[rows, :]
            value_block = values[rows, :]

            def run(masked):
                if masked:
                    at = key_start + lax.broadcasted_iota(jnp.int32, (KEY_BLOCK, pair), 0)
                    allowed = (at >= starts) & (at <= places)
                    allowed = jnp.concatenate([allowed, allowed], axis=1)
                for base in range(0, group_lanes, wide):
                    cols = slice(base, base + wide)
                    from_cols = slice(left + base, left + base + wide)
                    scores = jnp.dot(
                        key_block, q_cols[:, from_cols], preferred_element_type=jnp.float32
                    )
                    grads = jnp.dot(
                        value_block, g_cols[:, from_cols], preferred_element_type=jnp.float32
                    )
                    if masked:
                        scores = jnp.where(allowed, scores, NEG)
                    old = max_scr[:, cols]
                    new = jnp.maximum(old, jnp.max(scores, axis=0, keepdims=True))
                    weights = jnp.exp2((scores - new) * exp_scale)
                    rescale = jnp.exp2((old - new) * exp_scale)
                    max_scr[:, cols] = new
                    m_scr[pl.ds(j, 1), cols] = new
                    sum_scr[:, cols] = sum_scr[:, cols] * rescale + jnp.sum(
                        weights, axis=0, keepdims=True
                    )
                    weight_scr[:, cols] = weight_scr[:, cols] * rescale + jnp.sum(
                        weights * grads, axis=0, keepdims=True
                    )
                    e_scr[rows, cols] = weights
                    d_scr[rows, cols] = grads

            whole = (key_start + KEY_BLOCK - 1 <= first) & (key_start >= open_from)

            @pl.when(whole)
            def _():
                run(False)

            @pl.when(jnp.logical_not(whole))
            def _():
                run(True)

            return 0

        lax.fori_loop(low, high, stats, 0)
        inverse = 1.0 / sum_scr[...]
        weight_scr[...] = weight_scr[...] * inverse
        sum_scr[...] = inverse
        here = slice(left, left + group_lanes)
        dqt[:, here] = jnp.zeros((width, group_lanes), jnp.float32)

        def grads_step(j, _):
            key_start = pl.multiple_of(j * KEY_BLOCK, KEY_BLOCK)
            rows = pl.ds(key_start, KEY_BLOCK)
            factor = jnp.exp2((m_scr[pl.ds(j, 1), :] - max_scr[...]) * exp_scale) * sum_scr[...]
            probs_parts, grad_parts = [], []
            for base in range(0, group_lanes, wide):
                cols = slice(base, base + wide)
                probs = e_scr[rows, cols] * factor[:, cols]
                grad_scores = probs * (d_scr[rows, cols] - weight_scr[:, cols])
                probs_parts.append(probs.astype(jnp.bfloat16))
                grad_parts.append(grad_scores.astype(jnp.bfloat16))
            probs_low = jnp.concatenate(probs_parts, axis=1)
            grad_low = jnp.concatenate(grad_parts, axis=1)
            mine = slice(left // pair, (left + group_lanes) // pair)
            g_all = g_rows[mine].reshape(group_lanes, width)
            q_all = q_rows[mine].reshape(group_lanes, width)
            dv_acc[rows, :] += jnp.dot(probs_low, g_all, preferred_element_type=jnp.float32)
            dk_acc[rows, :] += jnp.dot(grad_low, q_all, preferred_element_type=jnp.float32)
            dqt[:, here] += jnp.dot(keys[rows, :].T, grad_low, preferred_element_type=jnp.float32)
            return 0

        lax.fori_loop(low, high, grads_step, 0)

    for n in range(heads):
        q_rows[n] = (dqt[:, n * pair : (n + 1) * pair] * scale).T.astype(jnp.bfloat16)
        for dz, out in enumerate((dq_own, dq_send)):
            at = pl.multiple_of((z_bit ^ dz) * tokens, tokens)
            out[n // group, n % group] = q_rows[n, pl.ds(at, tokens), :]

    for d in range(column_count):
        for b, out in enumerate((kept_ref, sent_ref)):
            start = pl.multiple_of(((column ^ d) * 2 + (core ^ b)) * block_tokens, block_tokens)
            rows = pl.ds(start, block_tokens)
            out[d, 0] = (dk_acc[rows, :] * scale).astype(out.dtype)
            out[d, 1] = dv_acc[rows, :].astype(out.dtype)


def attention(name, doc_start, chunks, kv_own, kv_other, after=()):
    _, layers, group, tokens, width = chunks[0].shape
    column_count = len(kv_own)
    merged = len(kv_other) == 1
    block_tokens = kv_own[0].shape[1]
    total = column_count * 2 * block_tokens
    pair = 2 * tokens
    lanes = layers * group * pair
    wide = 2 * pair
    group_lanes = lanes
    while 8 * total * group_lanes > SCORE_BYTES and group_lanes > wide:
        group_lanes = max(k for k in range(wide, group_lanes, wide) if lanes % k == 0)
    smem = pl.BlockSpec(memory_space=pltpu.SMEM)
    vmem = pl.BlockSpec(memory_space=pltpu.VMEM)
    f32, bf16 = jnp.float32, jnp.bfloat16
    outs = [jax.ShapeDtypeStruct((layers, group, tokens, width), bf16)] * 2
    outs.append(jax.ShapeDtypeStruct((column_count, 2, block_tokens, width), f32))
    outs.append(jax.ShapeDtypeStruct((column_count, 2, block_tokens, width), bf16))
    return pl.pallas_call(
        functools.partial(attention_kernel, column_count, group_lanes, merged),
        out_shape=outs,
        in_specs=[smem] + [vmem] * (1 + 2 + column_count + len(kv_other))
        + [pl.BlockSpec(memory_space=pl.ANY)] * len(after),
        out_specs=[vmem] * len(outs),
        scratch_shapes=[
            pltpu.VMEM((layers * group, pair, width), bf16),
            pltpu.VMEM((layers * group, pair, width), bf16),
            pltpu.VMEM((width, lanes), bf16),
            pltpu.VMEM((width, lanes), bf16),
            pltpu.VMEM((total, width), bf16),
            pltpu.VMEM((total, width), bf16),
            pltpu.VMEM((total, group_lanes), f32),
            pltpu.VMEM((total, group_lanes), f32),
            pltpu.VMEM((total // KEY_BLOCK, group_lanes), f32),
            pltpu.VMEM((1, group_lanes), f32),
            pltpu.VMEM((1, group_lanes), f32),
            pltpu.VMEM((1, group_lanes), f32),
            pltpu.VMEM((width, lanes), f32),
            pltpu.VMEM((total, width), f32),
            pltpu.VMEM((total, width), f32),
        ],
        compiler_params=pltpu.CompilerParams(vmem_limit_bytes=VMEM_LIMIT),
        cost_estimate=pl.CostEstimate(
            flops=10 * lanes * total * width,
            bytes_accessed=16 * total * width,
            transcendentals=lanes * total,
        ),
        name=name,
    )(doc_start, doc_start.reshape(-1, pair), *chunks, *kv_own, *kv_other, *after)


def per_device(seq_count, head_count, queries, grad_out, keys, values, doc_start):
    layers, tokens, all_heads, width = queries.shape
    group = all_heads // head_count
    column_count = seq_count // 2
    columns = range(column_count)

    def swap(x, flip_seq, flip_head):
        pairs = [
            (s * head_count + z, (s ^ flip_seq) * head_count + (z ^ flip_head))
            for s in range(seq_count)
            for z in range(head_count)
        ]
        return lax.ppermute(x, ("seq", "head"), pairs)

    z = lax.axis_index("head")

    own = jnp.stack([keys[:, 0], values[:, 0]])
    far_own = swap(own, 0, 2)
    near = [own] + [swap(own, 2 * d, 0) for d in columns[1:]]
    far = [far_own] + [swap(far_own, 2 * d, 0) for d in columns[1:]]
    near_other = [swap(jnp.stack(near), 1, 0)]
    far_other = [swap(x, 1, 0) for x in far]

    both = jnp.stack([queries, grad_out]).reshape(2, layers, tokens, head_count, group, width)
    both = jnp.transpose(both, (3, 0, 1, 4, 2, 5))

    def piece(flip):
        return lax.dynamic_index_in_dim(both, z ^ flip, 0, keepdims=False)

    near_chunks = (piece(0), swap(piece(1), 0, 1))
    far_chunks = (piece(2), swap(piece(3), 0, 1))

    near_dq, near_dq_send, near_kept, near_sent = attention(
        "attention_near", doc_start, near_chunks, near, near_other
    )
    far_dq, far_dq_send, far_kept, far_sent = attention(
        "attention_far", doc_start, far_chunks, far, far_other
    )

    def add_cores(kept, sent):
        sums = kept + swap(sent, 1, 0).astype(jnp.float32)
        return sums[0], [sums[d].astype(jnp.bfloat16) for d in columns[1:]]

    def add_columns(mine, parts):
        for d, part in zip(columns[1:], parts):
            mine = mine + swap(part, 2 * d, 0).astype(jnp.float32)
        return mine

    far_total = add_columns(*add_cores(far_kept, far_sent))
    far_low = far_total.astype(jnp.bfloat16)
    near_total = add_columns(*add_cores(near_kept, near_sent))
    final = near_total + swap(far_low, 0, 2).astype(jnp.float32)
    final = final.astype(jnp.bfloat16)[:, :, None, :]

    pieces = jnp.stack([near_dq, swap(near_dq_send, 0, 1), far_dq, swap(far_dq_send, 0, 1)])
    ordered = [
        lax.dynamic_index_in_dim(pieces, z ^ head, 0, keepdims=False) for head in range(head_count)
    ]
    query_grads = jnp.transpose(jnp.stack(ordered), (1, 3, 0, 2, 4))
    query_grads = query_grads.reshape(layers, tokens, all_heads, width)
    return query_grads, final[0], final[1]


def solution(mesh):
    tokens_spec = P(None, ("seq", "head"), None, None)
    keys_spec = P("seq", "head", None)
    return jax.shard_map(
        functools.partial(per_device, mesh.shape["seq"], mesh.shape["head"]),
        mesh=mesh,
        in_specs=(tokens_spec, tokens_spec, keys_spec, keys_spec, P()),
        out_specs=(tokens_spec, keys_spec, keys_spec),
        check_vma=False,
    )
```

profile of v0, /device:TPU:0, one launch (start us, length us, event | category | flops | bytes accessed | tf_op | source)
XLA Modules:
  0.0 63.6 jit_solution(9505075065211691435)
XLA Ops:
  0.6 0.9 %fusion.17 = (bf16[1,2,256,128]{3,2,1,0:T(8,128)(2,1)S(1)}, bf16[2,256,128]{2,1,0:T(8,128)(2,1)S(1)}) fusion(bf16[1,256,128]{2,1,0:T(8,128)(2,1)} %bitcast.91, bf16[1,256,128]{2,1,0:T(8,128)(2,1)} %bitcast.92), kind=kLoop, calls=%fused_computation.45 | loop fusion | flops 65536 | bytes 393216 | tf_op jit(solution)/shard_map/stack | solution.py:239
  1.5 4.1 %collective-permute-start.7 = (bf16[2,256,128]{2,1,0:T(8,128)(2,1)S(1)}, bf16[2,256,128]{2,1,0:T(8,128)(2,1)S(1)}, u32[]{:S(2)}, u32[]{:S(2)}) collective-permute-start(bf16[2,256,128]{2,1,0:T(8,128)(2,1)S(1)} %get-tuple-element.40.refs_2_), channel_id=1, source_target_pairs={{0,2},{1,3},{2,0},{3,1},{4,6},{5,7},{6,4},{7,5},{8,10},{9,11},{10,... | collective-permute-start | bytes 393224 | tf_op jit(solution)/shard_map/ppermute | solution.py:231
  5.6 1.5 %collective-permute-start.1 = (bf16[2,256,128]{2,1,0:T(8,128)(2,1)S(1)}, bf16[2,256,128]{2,1,0:T(8,128)(2,1)S(1)}, u32[]{:S(2)}, u32[]{:S(2)}) collective-permute-start(bf16[2,256,128]{2,1,0:T(8,128)(2,1)S(1)} %get-tuple-element.40.refs_2_), channel_id=1, source_target_pairs={{0,8},{1,9},{2,10},{3,11},{4,12},{5,13},{6,14},{7,15},{8,0},{9,1},... | collective-permute-start | bytes 393224 | tf_op jit(solution)/shard_map/ppermute | solution.py:231
  7.1 1.5 %collective-permute-start.2 = (bf16[2,256,128]{2,1,0:T(8,128)(2,1)S(1)}, bf16[2,256,128]{2,1,0:T(8,128)(2,1)S(1)}, u32[]{:S(2)}, u32[]{:S(2)}) collective-permute-start(bf16[2,256,128]{2,1,0:T(8,128)(2,1)S(1)} %get-tuple-element.40.refs_2_), channel_id=1, source_target_pairs={{0,16},{1,17},{2,18},{3,19},{4,20},{5,21},{6,22},{7,23},{8,24},{9,... | collective-permute-start | bytes 393224 | tf_op jit(solution)/shard_map/ppermute | solution.py:231
  8.6 1.5 %fusion.5 = (bf16[2,2,5,64,128]{4,3,2,1,0:T(8,128)(2,1)S(1)}, bf16[2,2,5,64,128]{4,3,2,1,0:T(8,128)(2,1)S(1)}, bf16[2,2,5,64,128]{4,3,2,1,0:T(8,128)(2,1)S(1)}, bf16[2,2,5,64,128]{4,3,2,1,0:T(8,128)(2,1)S(1)}) fusion(s32[]{:T(128)S(6)} %select_n.19, bf16[1,2,64,4,5,128]{5,2,4,3,1,0:T(8,128)(2,1)} %bitcast.87, bf16[1,2,64,4,5,128]{5,2,4,3,1,0:T(8,128)(2,1)} %bitcast.88, ...), kind=kLoop, calls=%fused_computation.18 | loop fusion | flops 655360 | bytes 2621456 | tf_op jit(solution)/shard_map/jit(dynamic_index_in_dim)/squeeze | solution.py:246
  10.1 0.0 copy-start
  10.2 1.6 %collective-permute-start.6 = (bf16[2,2,5,64,128]{4,3,2,1,0:T(8,128)(2,1)S(1)}, bf16[2,2,5,64,128]{4,3,2,1,0:T(8,128)(2,1)S(1)}, u32[]{:S(2)}, u32[]{:S(2)}) collective-permute-start(bf16[2,2,5,64,128]{4,3,2,1,0:T(8,128)(2,1)S(1)} %get-tuple-element.26), channel_id=1, source_target_pairs={{0,1},{1,0},{2,3},{3,2},{4,5},{5,4},{6,7},{7,6},{8,9},{9,8},{10,11... | collective-permute-start | bytes 983048 | tf_op jit(solution)/shard_map/ppermute | solution.py:231
  11.8 0.5 collective-permute-start.3
  12.3 0.0 collective-permute-done.7.refs_2_
  12.3 1.5 %collective-permute-start.8 = (bf16[2,256,128]{2,1,0:T(8,128)(2,1)S(1)}, bf16[2,256,128]{2,1,0:T(8,128)(2,1)S(1)}, u32[]{:S(2)}, u32[]{:S(2)}) collective-permute-start(bf16[2,256,128]{2,1,0:T(8,128)(2,1)S(1)} %collective-permute-done.7.refs_2_), channel_id=1, source_target_pairs={{0,8},{1,9},{2,10},{3,11},{4,12},{5,13},{6,14},{7,15},{8,0},{9,1},... | collective-permute-start | bytes 393224 | tf_op jit(solution)/shard_map/ppermute | solution.py:231
  13.8 0.0 collective-permute-done.1.refs_3_
  13.8 1.5 %collective-permute-start.9 = (bf16[2,256,128]{2,1,0:T(8,128)(2,1)S(1)}, bf16[2,256,128]{2,1,0:T(8,128)(2,1)S(1)}, u32[]{:S(2)}, u32[]{:S(2)}) collective-permute-start(bf16[2,256,128]{2,1,0:T(8,128)(2,1)S(1)} %collective-permute-done.7.refs_2_), channel_id=1, source_target_pairs={{0,16},{1,17},{2,18},{3,19},{4,20},{5,21},{6,22},{7,23},{8,24},{9,... | collective-permute-start | bytes 393224 | tf_op jit(solution)/shard_map/ppermute | solution.py:231
  15.3 0.0 collective-permute-done.2.refs_4_
  15.3 0.5 collective-permute-start.10
  15.8 3.5 %collective-permute-done.3.refs_5_ = bf16[2,256,128]{2,1,0:T(8,128)(2,1)S(1)} collective-permute-done((bf16[2,256,128]{2,1,0:T(8,128)(2,1)S(1)}, bf16[2,256,128]{2,1,0:T(8,128)(2,1)S(1)}, u32[]{:S(2)}, u32[]{:S(2)}) %collective-permute-start.3) | collective-permute-done | bytes 131104 | tf_op jit(solution)/shard_map/ppermute | solution.py:231
  19.2 0.0 collective-permute-start.11
  19.2 0.9 %collective-permute-done.8.refs_3_ = bf16[2,256,128]{2,1,0:T(8,128)(2,1)S(1)} collective-permute-done((bf16[2,256,128]{2,1,0:T(8,128)(2,1)S(1)}, bf16[2,256,128]{2,1,0:T(8,128)(2,1)S(1)}, u32[]{:S(2)}, u32[]{:S(2)}) %collective-permute-start.8) | collective-permute-done | bytes 131104 | tf_op jit(solution)/shard_map/ppermute | solution.py:231
  20.1 0.0 collective-permute-start.12
  20.1 0.9 %collective-permute-done.9.refs_4_ = bf16[2,256,128]{2,1,0:T(8,128)(2,1)S(1)} collective-permute-done((bf16[2,256,128]{2,1,0:T(8,128)(2,1)S(1)}, bf16[2,256,128]{2,1,0:T(8,128)(2,1)S(1)}, u32[]{:S(2)}, u32[]{:S(2)}) %collective-permute-start.9) | collective-permute-done | bytes 131104 | tf_op jit(solution)/shard_map/ppermute | solution.py:231
  21.0 0.0 collective-permute-start.13
  21.0 1.4 %collective-permute-done.10.refs_5_ = bf16[2,256,128]{2,1,0:T(8,128)(2,1)S(1)} collective-permute-done((bf16[2,256,128]{2,1,0:T(8,128)(2,1)S(1)}, bf16[2,256,128]{2,1,0:T(8,128)(2,1)S(1)}, u32[]{:S(2)}, u32[]{:S(2)}) %collective-permute-start.10) | collective-permute-done | bytes 131104 | tf_op jit(solution)/shard_map/ppermute | solution.py:231
  22.5 0.0 collective-permute-start.14
  22.5 0.1 pad_maximum_fusion.1
  22.5 0.0 collective-permute-done.11.refs_6_
  22.6 1.7 %collective-permute-start = (bf16[2,2,5,64,128]{4,3,2,1,0:T(8,128)(2,1)S(1)}, bf16[2,2,5,64,128]{4,3,2,1,0:T(8,128)(2,1)S(1)}, u32[]{:S(2)}, u32[]{:S(2)}) collective-permute-start(bf16[2,2,5,64,128]{4,3,2,1,0:T(8,128)(2,1)S(1)} %get-tuple-element.23), channel_id=1, source_target_pairs={{0,1},{1,0},{2,3},{3,2},{4,5},{5,4},{6,7},{7,6},{8,9},{9,8},{10,11... | collective-permute-start | bytes 983048 | tf_op jit(solution)/shard_map/ppermute | solution.py:231
  24.2 0.0 collective-permute-done.6.refs_1_
  24.2 0.0 collective-permute-start.4
  24.2 0.0 collective-permute-done.12.refs_7_
  24.2 0.0 collective-permute-done.13.refs_8_
  24.2 0.0 collective-permute-done.14.refs_9_
  24.3 2.8 %attention_far.1 = (bf16[2,5,64,128]{3,2,1,0:T(8,128)(2,1)S(1)}, bf16[2,5,64,128]{3,2,1,0:T(8,128)(2,1)S(1)}, f32[4,2,256,128]{3,2,1,0:T(8,128)S(1)}, bf16[4,2,256,128]{3,2,1,0:T(8,128)(2,1)S(1)}) custom-call(s32[2048]{0:T(1024)S(1)} %copy-done, s32[16,128]{1,0:T(8,128)S(1)} %bitcast.84, bf16[2,2,5,64,128]{4,3,2,1,0:T(8,128)(2,1)S(1)} %get-tuple-element.25.refs_0_, ...), custom_call_target="tpu_custom_call" | custom-call | flops 3355443200 | bytes 4194304 | tf_op jit(solution)/shard_map/attention_far/pallas_call | solution.py:186
  27.1 1.8 %collective-permute-start.20 = (bf16[4,2,256,128]{3,2,1,0:T(8,128)(2,1)S(1)}, bf16[4,2,256,128]{3,2,1,0:T(8,128)(2,1)S(1)}, u32[]{:S(2)}, u32[]{:S(2)}) collective-permute-start(bf16[4,2,256,128]{3,2,1,0:T(8,128)(2,1)S(1)} %get-tuple-element.18), channel_id=1, source_target_pairs={{0,4},{1,5},{2,6},{3,7},{4,0},{5,1},{6,2},{7,3},{8,12},{9,13},{10,... | collective-permute-start | bytes 1572872 | tf_op jit(solution)/shard_map/ppermute | solution.py:231
  28.9 0.7 %collective-permute-start.15 = (bf16[2,5,64,128]{3,2,1,0:T(8,128)(2,1)S(1)}, bf16[2,5,64,128]{3,2,1,0:T(8,128)(2,1)S(1)}, u32[]{:S(2)}, u32[]{:S(2)}) collective-permute-start(bf16[2,5,64,128]{3,2,1,0:T(8,128)(2,1)S(1)} %get-tuple-element.14), channel_id=1, source_target_pairs={{0,1},{1,0},{2,3},{3,2},{4,5},{5,4},{6,7},{7,6},{8,9},{9,8},{10,11... | collective-permute-start | bytes 491528 | tf_op jit(solution)/shard_map/ppermute | solution.py:231
  29.6 3.5 %collective-permute-done.refs_1_ = bf16[2,2,5,64,128]{4,3,2,1,0:T(8,128)(2,1)S(1)} collective-permute-done((bf16[2,2,5,64,128]{4,3,2,1,0:T(8,128)(2,1)S(1)}, bf16[2,2,5,64,128]{4,3,2,1,0:T(8,128)(2,1)S(1)}, u32[]{:S(2)}, u32[]{:S(2)}) %collective-permute-start) | collective-permute-done | bytes 327712 | tf_op jit(solution)/shard_map/ppermute | solution.py:231
  33.1 0.0 collective-permute-done.4.refs_6_
  33.1 2.8 %attention_near.1 = (bf16[2,5,64,128]{3,2,1,0:T(8,128)(2,1)S(1)}, bf16[2,5,64,128]{3,2,1,0:T(8,128)(2,1)S(1)}, f32[4,2,256,128]{3,2,1,0:T(8,128)S(1)}, bf16[4,2,256,128]{3,2,1,0:T(8,128)(2,1)S(1)}) custom-call(s32[2048]{0:T(1024)S(1)} %copy-done, s32[16,128]{1,0:T(8,128)S(1)} %bitcast.85, bf16[2,2,5,64,128]{4,3,2,1,0:T(8,128)(2,1)S(1)} %get-tuple-element.24.refs_0_, ...), custom_call_target="tpu_custom_call" | custom-call | flops 3355443200 | bytes 4194304 | tf_op jit(solution)/shard_map/attention_near/pallas_call | solution.py:186
  36.0 0.7 %collective-permute-start.16 = (bf16[4,2,256,128]{3,2,1,0:T(8,128)(2,1)S(1)}, bf16[4,2,256,128]{3,2,1,0:T(8,128)(2,1)S(1)}, u32[]{:S(2)}, u32[]{:S(2)}) collective-permute-start(bf16[4,2,256,128]{3,2,1,0:T(8,128)(2,1)S(1)} %get-tuple-element.16), channel_id=1, source_target_pairs={{0,4},{1,5},{2,6},{3,7},{4,0},{5,1},{6,2},{7,3},{8,12},{9,13},{10,... | collective-permute-start | bytes 1572872 | tf_op jit(solution)/shard_map/ppermute | solution.py:231
  36.6 1.1 %collective-permute-start.5 = (bf16[2,5,64,128]{3,2,1,0:T(8,128)(2,1)S(1)}, bf16[2,5,64,128]{3,2,1,0:T(8,128)(2,1)S(1)}, u32[]{:S(2)}, u32[]{:S(2)}) collective-permute-start(bf16[2,5,64,128]{3,2,1,0:T(8,128)(2,1)S(1)} %get-tuple-element.12), channel_id=1, source_target_pairs={{0,1},{1,0},{2,3},{3,2},{4,5},{5,4},{6,7},{7,6},{8,9},{9,8},{10,11... | collective-permute-start | bytes 491528 | tf_op jit(solution)/shard_map/ppermute | solution.py:231
  37.8 0.0 collective-permute-done.20
  37.8 0.2 fusion.19
  38.0 3.3 %collective-permute-start.21 = (bf16[2,256,128]{2,1,0:T(8,128)(2,1)S(1)}, bf16[2,256,128]{2,1,0:T(8,128)(2,1)S(1)}, u32[]{:S(2)}, u32[]{:S(2)}) collective-permute-start(bf16[2,256,128]{2,1,0:T(8,128)(2,1)S(1)} %get-tuple-element.34), channel_id=1, source_target_pairs={{0,8},{1,9},{2,10},{3,11},{4,12},{5,13},{6,14},{7,15},{8,0},{9,1},... | collective-permute-start | bytes 393224 | tf_op jit(solution)/shard_map/ppermute | solution.py:231
  41.3 5.4 %collective-permute-start.22 = (bf16[2,256,128]{2,1,0:T(8,128)(2,1)S(1)}, bf16[2,256,128]{2,1,0:T(8,128)(2,1)S(1)}, u32[]{:S(2)}, u32[]{:S(2)}) collective-permute-start(bf16[2,256,128]{2,1,0:T(8,128)(2,1)S(1)} %get-tuple-element.36), channel_id=1, source_target_pairs={{0,16},{1,17},{2,18},{3,19},{4,20},{5,21},{6,22},{7,23},{8,24},{9,... | collective-permute-start | bytes 393224 | tf_op jit(solution)/shard_map/ppermute | solution.py:231
  46.7 0.0 collective-permute-done.15
  46.7 1.4 %collective-permute-start.23 = (bf16[2,256,128]{2,1,0:T(8,128)(2,1)S(1)}, bf16[2,256,128]{2,1,0:T(8,128)(2,1)S(1)}, u32[]{:S(2)}, u32[]{:S(2)}) collective-permute-start(bf16[2,256,128]{2,1,0:T(8,128)(2,1)S(1)} %get-tuple-element.35), channel_id=1, source_target_pairs={{0,24},{1,25},{2,26},{3,27},{4,28},{5,29},{6,30},{7,31},{8,16},{9,... | collective-permute-start | bytes 393224 | tf_op jit(solution)/shard_map/ppermute | solution.py:231
  48.1 0.0 collective-permute-done.5
  48.1 0.1 pad_maximum_fusion
  48.1 0.0 collective-permute-done.21
  48.2 4.0 %collective-permute-done.22 = bf16[2,256,128]{2,1,0:T(8,128)(2,1)S(1)} collective-permute-done((bf16[2,256,128]{2,1,0:T(8,128)(2,1)S(1)}, bf16[2,256,128]{2,1,0:T(8,128)(2,1)S(1)}, u32[]{:S(2)}, u32[]{:S(2)}) %collective-permute-start.22) | collective-permute-done | bytes 131104 | tf_op jit(solution)/shard_map/ppermute | solution.py:231
  52.2 1.8 %collective-permute-done.23 = bf16[2,256,128]{2,1,0:T(8,128)(2,1)S(1)} collective-permute-done((bf16[2,256,128]{2,1,0:T(8,128)(2,1)S(1)}, bf16[2,256,128]{2,1,0:T(8,128)(2,1)S(1)}, u32[]{:S(2)}, u32[]{:S(2)}) %collective-permute-start.23) | collective-permute-done | bytes 131104 | tf_op jit(solution)/shard_map/ppermute | solution.py:231
  54.0 0.1 fusion.11
  54.1 0.1 collective-permute-start.24
  54.2 0.0 collective-permute-done.16
  54.2 0.2 fusion.18
  54.4 0.6 %collective-permute-start.17 = (bf16[2,256,128]{2,1,0:T(8,128)(2,1)S(1)}, bf16[2,256,128]{2,1,0:T(8,128)(2,1)S(1)}, u32[]{:S(2)}, u32[]{:S(2)}) collective-permute-start(bf16[2,256,128]{2,1,0:T(8,128)(2,1)S(1)} %get-tuple-element.31), channel_id=1, source_target_pairs={{0,8},{1,9},{2,10},{3,11},{4,12},{5,13},{6,14},{7,15},{8,0},{9,1},... | collective-permute-start | bytes 393224 | tf_op jit(solution)/shard_map/ppermute | solution.py:231
  55.1 1.7 %collective-permute-start.18 = (bf16[2,256,128]{2,1,0:T(8,128)(2,1)S(1)}, bf16[2,256,128]{2,1,0:T(8,128)(2,1)S(1)}, u32[]{:S(2)}, u32[]{:S(2)}) collective-permute-start(bf16[2,256,128]{2,1,0:T(8,128)(2,1)S(1)} %get-tuple-element.33), channel_id=1, source_target_pairs={{0,16},{1,17},{2,18},{3,19},{4,20},{5,21},{6,22},{7,23},{8,24},{9,... | collective-permute-start | bytes 393224 | tf_op jit(solution)/shard_map/ppermute | solution.py:231
  56.8 1.2 %collective-permute-start.19 = (bf16[2,256,128]{2,1,0:T(8,128)(2,1)S(1)}, bf16[2,256,128]{2,1,0:T(8,128)(2,1)S(1)}, u32[]{:S(2)}, u32[]{:S(2)}) collective-permute-start(bf16[2,256,128]{2,1,0:T(8,128)(2,1)S(1)} %get-tuple-element.32), channel_id=1, source_target_pairs={{0,24},{1,25},{2,26},{3,27},{4,28},{5,29},{6,30},{7,31},{8,16},{9,... | collective-permute-start | bytes 393224 | tf_op jit(solution)/shard_map/ppermute | solution.py:231
  58.0 0.1 maximum_bitcast_fusion
  58.1 0.9 %copy.10 = bf16[2,64,4,5,128]{4,1,3,2,0:T(8,128)(2,1)} copy(bf16[2,64,4,5,128]{4,1,3,0,2:T(8,128)(2,1)S(1)} %maximum_bitcast_fusion) | data formatting | bytes 1310720 | tf_op jit(solution)/shard_map/transpose | solution.py:277
  59.0 3.2 %collective-permute-done.24 = bf16[2,256,128]{2,1,0:T(8,128)(2,1)S(1)} collective-permute-done((bf16[2,256,128]{2,1,0:T(8,128)(2,1)S(1)}, bf16[2,256,128]{2,1,0:T(8,128)(2,1)S(1)}, u32[]{:S(2)}, u32[]{:S(2)}) %collective-permute-start.24) | collective-permute-done | bytes 131104 | tf_op jit(solution)/shard_map/ppermute | solution.py:231
  62.2 0.0 collective-permute-done.17
  62.2 0.6 %collective-permute-done.18 = bf16[2,256,128]{2,1,0:T(8,128)(2,1)S(1)} collective-permute-done((bf16[2,256,128]{2,1,0:T(8,128)(2,1)S(1)}, bf16[2,256,128]{2,1,0:T(8,128)(2,1)S(1)}, u32[]{:S(2)}, u32[]{:S(2)}) %collective-permute-start.18) | collective-permute-done | bytes 131104 | tf_op jit(solution)/shard_map/ppermute | solution.py:231
  62.9 0.0 collective-permute-done.19
  62.9 0.1 fusion.16
  62.9 0.7 %slice_bitcast_fusion.8 = (bf16[256,1,128]{2,0,1:T(8,128)(2,1)}, bf16[256,1,128]{2,0,1:T(8,128)(2,1)}) fusion(bf16[2,256,128]{2,1,0:T(8,128)(2,1)S(1)} %fusion.16), kind=kLoop, calls=%fused_computation.39 | loop fusion | bytes 262144 | tf_op jit(solution)/shard_map/squeeze | solution.py:279
  (4 shorter events, 0.1 us)
Async XLA Ops:
  1.5 10.8 %collective-permute-start.7 = (bf16[2,256,128]{2,1,0:T(8,128)(2,1)S(1)}, bf16[2,256,128]{2,1,0:T(8,128)(2,1)S(1)}, u32[]{:S(2)}, u32[]{:S(2)}) collective-permute-start(bf16[2,256,128]{2,1,0:T(8,128)(2,1)S(1)} %get-tuple-element.40.refs_2_), channel_id=1, source_target_pairs={{0,2},{1,3},{2,0},{3,1},{4,6},{5,7},{6,4},{7,5},{8,10},{9,11},{10,... | collective-permute-start | bytes 393224 | tf_op jit(solution)/shard_map/ppermute | solution.py:231
  5.6 8.2 %collective-permute-start.1 = (bf16[2,256,128]{2,1,0:T(8,128)(2,1)S(1)}, bf16[2,256,128]{2,1,0:T(8,128)(2,1)S(1)}, u32[]{:S(2)}, u32[]{:S(2)}) collective-permute-start(bf16[2,256,128]{2,1,0:T(8,128)(2,1)S(1)} %get-tuple-element.40.refs_2_), channel_id=1, source_target_pairs={{0,8},{1,9},{2,10},{3,11},{4,12},{5,13},{6,14},{7,15},{8,0},{9,1},... | collective-permute-start | bytes 393224 | tf_op jit(solution)/shard_map/ppermute | solution.py:231
  7.1 8.2 %collective-permute-start.2 = (bf16[2,256,128]{2,1,0:T(8,128)(2,1)S(1)}, bf16[2,256,128]{2,1,0:T(8,128)(2,1)S(1)}, u32[]{:S(2)}, u32[]{:S(2)}) collective-permute-start(bf16[2,256,128]{2,1,0:T(8,128)(2,1)S(1)} %get-tuple-element.40.refs_2_), channel_id=1, source_target_pairs={{0,16},{1,17},{2,18},{3,19},{4,20},{5,21},{6,22},{7,23},{8,24},{9,... | collective-permute-start | bytes 393224 | tf_op jit(solution)/shard_map/ppermute | solution.py:231
  10.1 14.1 %copy-start = (s32[2048]{0:T(1024)S(1)}, s32[2048]{0:T(1024)}, u32[]{:S(2)}) copy-start(s32[2048]{0:T(1024)} %doc_ref.3) | copy-start | bytes 24580
  10.2 14.1 %collective-permute-start.6 = (bf16[2,2,5,64,128]{4,3,2,1,0:T(8,128)(2,1)S(1)}, bf16[2,2,5,64,128]{4,3,2,1,0:T(8,128)(2,1)S(1)}, u32[]{:S(2)}, u32[]{:S(2)}) collective-permute-start(bf16[2,2,5,64,128]{4,3,2,1,0:T(8,128)(2,1)S(1)} %get-tuple-element.26), channel_id=1, source_target_pairs={{0,1},{1,0},{2,3},{3,2},{4,5},{5,4},{6,7},{7,6},{8,9},{9,8},{10,11... | collective-permute-start | bytes 983048 | tf_op jit(solution)/shard_map/ppermute | solution.py:231
  11.8 7.4 %collective-permute-start.3 = (bf16[2,256,128]{2,1,0:T(8,128)(2,1)S(1)}, bf16[2,256,128]{2,1,0:T(8,128)(2,1)S(1)}, u32[]{:S(2)}, u32[]{:S(2)}) collective-permute-start(bf16[2,256,128]{2,1,0:T(8,128)(2,1)S(1)} %get-tuple-element.40.refs_2_), channel_id=1, source_target_pairs={{0,24},{1,25},{2,26},{3,27},{4,28},{5,29},{6,30},{7,31},{8,16},{9,... | collective-permute-start | bytes 393224 | tf_op jit(solution)/shard_map/ppermute | solution.py:231
  12.3 7.8 %collective-permute-start.8 = (bf16[2,256,128]{2,1,0:T(8,128)(2,1)S(1)}, bf16[2,256,128]{2,1,0:T(8,128)(2,1)S(1)}, u32[]{:S(2)}, u32[]{:S(2)}) collective-permute-start(bf16[2,256,128]{2,1,0:T(8,128)(2,1)S(1)} %collective-permute-done.7.refs_2_), channel_id=1, source_target_pairs={{0,8},{1,9},{2,10},{3,11},{4,12},{5,13},{6,14},{7,15},{8,0},{9,1},... | collective-permute-start | bytes 393224 | tf_op jit(solution)/shard_map/ppermute | solution.py:231
  13.8 7.3 %collective-permute-start.9 = (bf16[2,256,128]{2,1,0:T(8,128)(2,1)S(1)}, bf16[2,256,128]{2,1,0:T(8,128)(2,1)S(1)}, u32[]{:S(2)}, u32[]{:S(2)}) collective-permute-start(bf16[2,256,128]{2,1,0:T(8,128)(2,1)S(1)} %collective-permute-done.7.refs_2_), channel_id=1, source_target_pairs={{0,16},{1,17},{2,18},{3,19},{4,20},{5,21},{6,22},{7,23},{8,24},{9,... | collective-permute-start | bytes 393224 | tf_op jit(solution)/shard_map/ppermute | solution.py:231
  15.3 7.2 %collective-permute-start.10 = (bf16[2,256,128]{2,1,0:T(8,128)(2,1)S(1)}, bf16[2,256,128]{2,1,0:T(8,128)(2,1)S(1)}, u32[]{:S(2)}, u32[]{:S(2)}) collective-permute-start(bf16[2,256,128]{2,1,0:T(8,128)(2,1)S(1)} %collective-permute-done.7.refs_2_), channel_id=1, source_target_pairs={{0,24},{1,25},{2,26},{3,27},{4,28},{5,29},{6,30},{7,31},{8,16},{9,... | collective-permute-start | bytes 393224 | tf_op jit(solution)/shard_map/ppermute | solution.py:231
  19.2 3.3 %collective-permute-start.11 = (bf16[2,256,128]{2,1,0:T(8,128)(2,1)S(1)}, bf16[2,256,128]{2,1,0:T(8,128)(2,1)S(1)}, u32[]{:S(2)}, u32[]{:S(2)}) collective-permute-start(bf16[2,256,128]{2,1,0:T(8,128)(2,1)S(1)} %collective-permute-done.7.refs_2_), channel_id=1, source_target_pairs={{0,4},{1,5},{2,6},{3,7},{4,0},{5,1},{6,2},{7,3},{8,12},{9,13},{10,... | collective-permute-start | bytes 393224 | tf_op jit(solution)/shard_map/ppermute | solution.py:231
  20.1 4.1 %collective-permute-start.12 = (bf16[2,256,128]{2,1,0:T(8,128)(2,1)S(1)}, bf16[2,256,128]{2,1,0:T(8,128)(2,1)S(1)}, u32[]{:S(2)}, u32[]{:S(2)}) collective-permute-start(bf16[2,256,128]{2,1,0:T(8,128)(2,1)S(1)} %collective-permute-done.8.refs_3_), channel_id=1, source_target_pairs={{0,4},{1,5},{2,6},{3,7},{4,0},{5,1},{6,2},{7,3},{8,12},{9,13},{10,... | collective-permute-start | bytes 393224 | tf_op jit(solution)/shard_map/ppermute | solution.py:231
  21.0 3.2 %collective-permute-start.13 = (bf16[2,256,128]{2,1,0:T(8,128)(2,1)S(1)}, bf16[2,256,128]{2,1,0:T(8,128)(2,1)S(1)}, u32[]{:S(2)}, u32[]{:S(2)}) collective-permute-start(bf16[2,256,128]{2,1,0:T(8,128)(2,1)S(1)} %collective-permute-done.9.refs_4_), channel_id=1, source_target_pairs={{0,4},{1,5},{2,6},{3,7},{4,0},{5,1},{6,2},{7,3},{8,12},{9,13},{10,... | collective-permute-start | bytes 393224 | tf_op jit(solution)/shard_map/ppermute | solution.py:231
  22.5 1.8 %collective-permute-start.14 = (bf16[2,256,128]{2,1,0:T(8,128)(2,1)S(1)}, bf16[2,256,128]{2,1,0:T(8,128)(2,1)S(1)}, u32[]{:S(2)}, u32[]{:S(2)}) collective-permute-start(bf16[2,256,128]{2,1,0:T(8,128)(2,1)S(1)} %collective-permute-done.10.refs_5_), channel_id=1, source_target_pairs={{0,4},{1,5},{2,6},{3,7},{4,0},{5,1},{6,2},{7,3},{8,12},{9,13},{10,... | collective-permute-start | bytes 393224 | tf_op jit(solution)/shard_map/ppermute | solution.py:231
  22.6 10.6 %collective-permute-start = (bf16[2,2,5,64,128]{4,3,2,1,0:T(8,128)(2,1)S(1)}, bf16[2,2,5,64,128]{4,3,2,1,0:T(8,128)(2,1)S(1)}, u32[]{:S(2)}, u32[]{:S(2)}) collective-permute-start(bf16[2,2,5,64,128]{4,3,2,1,0:T(8,128)(2,1)S(1)} %get-tuple-element.23), channel_id=1, source_target_pairs={{0,1},{1,0},{2,3},{3,2},{4,5},{5,4},{6,7},{7,6},{8,9},{9,8},{10,11... | collective-permute-start | bytes 983048 | tf_op jit(solution)/shard_map/ppermute | solution.py:231
  24.2 8.9 %collective-permute-start.4 = (bf16[4,2,256,128]{3,2,1,0:T(8,128)(2,1)S(1)}, bf16[4,2,256,128]{3,2,1,0:T(8,128)(2,1)S(1)}, u32[]{:S(2)}, u32[]{:S(2)}) collective-permute-start(bf16[4,2,256,128]{3,2,1,0:T(8,128)(2,1)S(1)} %pad_maximum_fusion.1), channel_id=1, source_target_pairs={{0,4},{1,5},{2,6},{3,7},{4,0},{5,1},{6,2},{7,3},{8,12},{9,13},{10,... | collective-permute-start | bytes 1572872 | tf_op jit(solution)/shard_map/ppermute | solution.py:231
  27.1 10.7 %collective-permute-start.20 = (bf16[4,2,256,128]{3,2,1,0:T(8,128)(2,1)S(1)}, bf16[4,2,256,128]{3,2,1,0:T(8,128)(2,1)S(1)}, u32[]{:S(2)}, u32[]{:S(2)}) collective-permute-start(bf16[4,2,256,128]{3,2,1,0:T(8,128)(2,1)S(1)} %get-tuple-element.18), channel_id=1, source_target_pairs={{0,4},{1,5},{2,6},{3,7},{4,0},{5,1},{6,2},{7,3},{8,12},{9,13},{10,... | collective-permute-start | bytes 1572872 | tf_op jit(solution)/shard_map/ppermute | solution.py:231
  28.9 17.7 %collective-permute-start.15 = (bf16[2,5,64,128]{3,2,1,0:T(8,128)(2,1)S(1)}, bf16[2,5,64,128]{3,2,1,0:T(8,128)(2,1)S(1)}, u32[]{:S(2)}, u32[]{:S(2)}) collective-permute-start(bf16[2,5,64,128]{3,2,1,0:T(8,128)(2,1)S(1)} %get-tuple-element.14), channel_id=1, source_target_pairs={{0,1},{1,0},{2,3},{3,2},{4,5},{5,4},{6,7},{7,6},{8,9},{9,8},{10,11... | collective-permute-start | bytes 491528 | tf_op jit(solution)/shard_map/ppermute | solution.py:231
  36.0 18.3 %collective-permute-start.16 = (bf16[4,2,256,128]{3,2,1,0:T(8,128)(2,1)S(1)}, bf16[4,2,256,128]{3,2,1,0:T(8,128)(2,1)S(1)}, u32[]{:S(2)}, u32[]{:S(2)}) collective-permute-start(bf16[4,2,256,128]{3,2,1,0:T(8,128)(2,1)S(1)} %get-tuple-element.16), channel_id=1, source_target_pairs={{0,4},{1,5},{2,6},{3,7},{4,0},{5,1},{6,2},{7,3},{8,12},{9,13},{10,... | collective-permute-start | bytes 1572872 | tf_op jit(solution)/shard_map/ppermute | solution.py:231
  36.6 11.4 %collective-permute-start.5 = (bf16[2,5,64,128]{3,2,1,0:T(8,128)(2,1)S(1)}, bf16[2,5,64,128]{3,2,1,0:T(8,128)(2,1)S(1)}, u32[]{:S(2)}, u32[]{:S(2)}) collective-permute-start(bf16[2,5,64,128]{3,2,1,0:T(8,128)(2,1)S(1)} %get-tuple-element.12), channel_id=1, source_target_pairs={{0,1},{1,0},{2,3},{3,2},{4,5},{5,4},{6,7},{7,6},{8,9},{9,8},{10,11... | collective-permute-start | bytes 491528 | tf_op jit(solution)/shard_map/ppermute | solution.py:231
  38.0 10.2 %collective-permute-start.21 = (bf16[2,256,128]{2,1,0:T(8,128)(2,1)S(1)}, bf16[2,256,128]{2,1,0:T(8,128)(2,1)S(1)}, u32[]{:S(2)}, u32[]{:S(2)}) collective-permute-start(bf16[2,256,128]{2,1,0:T(8,128)(2,1)S(1)} %get-tuple-element.34), channel_id=1, source_target_pairs={{0,8},{1,9},{2,10},{3,11},{4,12},{5,13},{6,14},{7,15},{8,0},{9,1},... | collective-permute-start | bytes 393224 | tf_op jit(solution)/shard_map/ppermute | solution.py:231
  41.3 10.9 %collective-permute-start.22 = (bf16[2,256,128]{2,1,0:T(8,128)(2,1)S(1)}, bf16[2,256,128]{2,1,0:T(8,128)(2,1)S(1)}, u32[]{:S(2)}, u32[]{:S(2)}) collective-permute-start(bf16[2,256,128]{2,1,0:T(8,128)(2,1)S(1)} %get-tuple-element.36), channel_id=1, source_target_pairs={{0,16},{1,17},{2,18},{3,19},{4,20},{5,21},{6,22},{7,23},{8,24},{9,... | collective-permute-start | bytes 393224 | tf_op jit(solution)/shard_map/ppermute | solution.py:231
  46.7 7.4 %collective-permute-start.23 = (bf16[2,256,128]{2,1,0:T(8,128)(2,1)S(1)}, bf16[2,256,128]{2,1,0:T(8,128)(2,1)S(1)}, u32[]{:S(2)}, u32[]{:S(2)}) collective-permute-start(bf16[2,256,128]{2,1,0:T(8,128)(2,1)S(1)} %get-tuple-element.35), channel_id=1, source_target_pairs={{0,24},{1,25},{2,26},{3,27},{4,28},{5,29},{6,30},{7,31},{8,16},{9,... | collective-permute-start | bytes 393224 | tf_op jit(solution)/shard_map/ppermute | solution.py:231
  54.1 8.1 %collective-permute-start.24 = (bf16[2,256,128]{2,1,0:T(8,128)(2,1)S(1)}, bf16[2,256,128]{2,1,0:T(8,128)(2,1)S(1)}, u32[]{:S(2)}, u32[]{:S(2)}) collective-permute-start(bf16[2,256,128]{2,1,0:T(8,128)(2,1)S(1)} %fusion.11), channel_id=1, source_target_pairs={{0,2},{1,3},{2,0},{3,1},{4,6},{5,7},{6,4},{7,5},{8,10},{9,11},{10,... | collective-permute-start | bytes 393224 | tf_op jit(solution)/shard_map/ppermute | solution.py:231
  54.4 7.8 %collective-permute-start.17 = (bf16[2,256,128]{2,1,0:T(8,128)(2,1)S(1)}, bf16[2,256,128]{2,1,0:T(8,128)(2,1)S(1)}, u32[]{:S(2)}, u32[]{:S(2)}) collective-permute-start(bf16[2,256,128]{2,1,0:T(8,128)(2,1)S(1)} %get-tuple-element.31), channel_id=1, source_target_pairs={{0,8},{1,9},{2,10},{3,11},{4,12},{5,13},{6,14},{7,15},{8,0},{9,1},... | collective-permute-start | bytes 393224 | tf_op jit(solution)/shard_map/ppermute | solution.py:231
  55.1 7.8 %collective-permute-start.18 = (bf16[2,256,128]{2,1,0:T(8,128)(2,1)S(1)}, bf16[2,256,128]{2,1,0:T(8,128)(2,1)S(1)}, u32[]{:S(2)}, u32[]{:S(2)}) collective-permute-start(bf16[2,256,128]{2,1,0:T(8,128)(2,1)S(1)} %get-tuple-element.33), channel_id=1, source_target_pairs={{0,16},{1,17},{2,18},{3,19},{4,20},{5,21},{6,22},{7,23},{8,24},{9,... | collective-permute-start | bytes 393224 | tf_op jit(solution)/shard_map/ppermute | solution.py:231
  56.8 6.0 %collective-permute-start.19 = (bf16[2,256,128]{2,1,0:T(8,128)(2,1)S(1)}, bf16[2,256,128]{2,1,0:T(8,128)(2,1)S(1)}, u32[]{:S(2)}, u32[]{:S(2)}) collective-permute-start(bf16[2,256,128]{2,1,0:T(8,128)(2,1)S(1)} %get-tuple-element.32), channel_id=1, source_target_pairs={{0,24},{1,25},{2,26},{3,27},{4,28},{5,29},{6,30},{7,31},{8,16},{9,... | collective-permute-start | bytes 393224 | tf_op jit(solution)/shard_map/ppermute | solution.py:231
where the time goes:
time: 63.8 us; the launch traced here: 63.6 us
  starting transfers between devices  32.4 us (51%)
  waiting for transfers between devices  19.9 us (31%)
  Pallas kernels  5.66 us (9%)
  other arithmetic  3.14 us (5%)
  local copies, waits for them, and re-layouts  1.65 us (3%)
  between operations  0.78 us (1%)
    ppermute x25, starting transfers between devices, swap(): return lax.ppermute(x, ('seq', 'head'), pairs)  32.4 us
    ppermute x25, waiting for transfers between devices, swap(): return lax.ppermute(x, ('seq', 'head'), pairs)  19.9 us
    pallas_call x2, Pallas kernels, attention(): pl.pallas_call(functools.partial(attention_kernel, column_count, group_la...  5.66 us
    squeeze x1, other arithmetic, piece(): return lax.dynamic_index_in_dim(both, z ^ flip, 0, keepdims=False)  1.51 us
  transfers between devices with their start and end apart: 25, of which 9 were waited for; matrix products, arithmetic and copies ran while one was open for 5% of the time, Pallas kernels for 9%

commit v1 on v0

--- a/solution.py
+++ b/solution.py
@@ -55,8 +55,9 @@
                 keys[pl.ds(start, block_tokens), :] = block[0]
                 values[pl.ds(start, block_tokens), :] = block[1]
 
-    dk_acc[...] = jnp.zeros_like(dk_acc)
-    dv_acc[...] = jnp.zeros_like(dv_acc)
+    if group_lanes != lanes:
+        dk_acc[...] = jnp.zeros_like(dk_acc)
+        dv_acc[...] = jnp.zeros_like(dv_acc)
     for layer in range(layers):
         for h in range(group):
             n = layer * group + h
@@ -67,36 +68,52 @@
             q_cols[:, n * pair : (n + 1) * pair] = q_rows[n].T
             g_cols[:, n * pair : (n + 1) * pair] = g_rows[n].T
 
+    def over_keys(step):
+        def two(i, _):
+            step(low + 2 * i, 2 * KEY_BLOCK)
+            return 0
+
+        lax.fori_loop(0, (high - low) // 2, two, 0)
+
+        @pl.when((high - low) % 2 == 1)
+        def _():
+            step(high - 1, KEY_BLOCK)
+
     for left in range(0, lanes, group_lanes):
         max_scr[...] = jnp.full_like(max_scr, NEG)
         sum_scr[...] = jnp.zeros_like(sum_scr)
         weight_scr[...] = jnp.zeros_like(weight_scr)
 
-        def stats(j, _):
+        def stats(j, size):
             key_start = pl.multiple_of(j * KEY_BLOCK, KEY_BLOCK)
-            rows = pl.ds(key_start, KEY_BLOCK)
+            rows = pl.ds(key_start, size)
             key_block = keys[rows, :]
             value_block = values[rows, :]
 
             def run(masked):
                 if masked:
-                    at = key_start + lax.broadcasted_iota(jnp.int32, (KEY_BLOCK, pair), 0)
+                    at = key_start + lax.broadcasted_iota(jnp.int32, (size, pair), 0)
                     allowed = (at >= starts) & (at <= places)
                     allowed = jnp.concatenate([allowed, allowed], axis=1)
+                news = []
                 for base in range(0, group_lanes, wide):
                     cols = slice(base, base + wide)
                     from_cols = slice(left + base, left + base + wide)
                     scores = jnp.dot(
                         key_block, q_cols[:, from_cols], preferred_element_type=jnp.float32
                     )
+                    if masked:
+                        scores = jnp.where(allowed, scores, NEG)
+                    e_scr[rows, cols] = scores
+                    news.append(jnp.maximum(max_scr[:, cols], jnp.max(scores, axis=0, keepdims=True)))
+                for base in range(0, group_lanes, wide):
+                    cols = slice(base, base + wide)
+                    from_cols = slice(left + base, left + base + wide)
                     grads = jnp.dot(
                         value_block, g_cols[:, from_cols], preferred_element_type=jnp.float32
                     )
-                    if masked:
-                        scores = jnp.where(allowed, scores, NEG)
-                    old = max_scr[:, cols]
-                    new = jnp.maximum(old, jnp.max(scores, axis=0, keepdims=True))
-                    weights = jnp.exp2((scores - new) * exp_scale)
+                    old, new = max_scr[:, cols], news[base // wide]
+                    weights = jnp.exp2((e_scr[rows, cols] - new) * exp_scale)
                     rescale = jnp.exp2((old - new) * exp_scale)
                     max_scr[:, cols] = new
                     m_scr[pl.ds(j, 1), cols] = new
@@ -109,7 +126,7 @@
                     e_scr[rows, cols] = weights
                     d_scr[rows, cols] = grads
 
-            whole = (key_start + KEY_BLOCK - 1 <= first) & (key_start >= open_from)
+            whole = (key_start + size - 1 <= first) & (key_start >= open_from)
 
             @pl.when(whole)
             def _():
@@ -119,18 +136,16 @@
             def _():
                 run(True)
 
-            return 0
-
-        lax.fori_loop(low, high, stats, 0)
+        over_keys(stats)
         inverse = 1.0 / sum_scr[...]
         weight_scr[...] = weight_scr[...] * inverse
         sum_scr[...] = inverse
         here = slice(left, left + group_lanes)
         dqt[:, here] = jnp.zeros((width, group_lanes), jnp.float32)
 
-        def grads_step(j, _):
+        def grads_step(j, size):
             key_start = pl.multiple_of(j * KEY_BLOCK, KEY_BLOCK)
-            rows = pl.ds(key_start, KEY_BLOCK)
+            rows = pl.ds(key_start, size)
             factor = jnp.exp2((m_scr[pl.ds(j, 1), :] - max_scr[...]) * exp_scale) * sum_scr[...]
             probs_parts, grad_parts = [], []
             for base in range(0, group_lanes, wide):
@@ -144,12 +159,17 @@
             mine = slice(left // pair, (left + group_lanes) // pair)
             g_all = g_rows[mine].reshape(group_lanes, width)
             q_all = q_rows[mine].reshape(group_lanes, width)
-            dv_acc[rows, :] += jnp.dot(probs_low, g_all, preferred_element_type=jnp.float32)
-            dk_acc[rows, :] += jnp.dot(grad_low, q_all, preferred_element_type=jnp.float32)
+            dv_part = jnp.dot(probs_low, g_all, preferred_element_type=jnp.float32)
+            dk_part = jnp.dot(grad_low, q_all, preferred_element_type=jnp.float32)
+            if group_lanes == lanes:
+                dv_acc[rows, :] = dv_part
+                dk_acc[rows, :] = dk_part
+            else:
+                dv_acc[rows, :] += dv_part
+                dk_acc[rows, :] += dk_part
             dqt[:, here] += jnp.dot(keys[rows, :].T, grad_low, preferred_element_type=jnp.float32)
-            return 0
-
-        lax.fori_loop(low, high, grads_step, 0)
+
+        over_keys(grads_step)
 
     for n in range(heads):
         q_rows[n] = (dqt[:, n * pair : (n + 1) * pair] * scale).T.astype(jnp.bfloat16)
@@ -161,8 +181,16 @@
         for b, out in enumerate((kept_ref, sent_ref)):
             start = pl.multiple_of(((column ^ d) * 2 + (core ^ b)) * block_tokens, block_tokens)
             rows = pl.ds(start, block_tokens)
-            out[d, 0] = (dk_acc[rows, :] * scale).astype(out.dtype)
-            out[d, 1] = dv_acc[rows, :].astype(out.dtype)
+            seen = (start >= low * KEY_BLOCK) & (start < high * KEY_BLOCK)
+
+            @pl.when(seen)
+            def _():
+                out[d, 0] = (dk_acc[rows, :] * scale).astype(out.dtype)
+                out[d, 1] = dv_acc[rows, :].astype(out.dtype)
+
+            @pl.when(jnp.logical_not(seen))
+            def _():
+                out[d] = jnp.zeros(out.shape[1:], out.dtype)
 
 
 def attention(name, doc_start, chunks, kv_own, kv_other, after=()):

time: 63.8 us -> 62.4 us (0.978)
  starting transfers between devices: 32.4 us -> 30.1 us
  waiting for transfers between devices: 19.9 us -> 20.8 us
    ppermute x25, starting transfers between devices: 32.4 us -> 30.1 us  [swap(): return lax.ppermute(x, ('seq', 'head'), pairs)]
    ppermute x25, waiting for transfers between devices: 19.9 us -> 20.8 us  [swap(): return lax.ppermute(x, ('seq', 'head'), pairs)]
  transfers between devices with their start and end apart: 25 -> 25, of which waited for: 9 -> 11; matrix products, arithmetic and copies ran while one was open for 5% -> 5% of each run, Pallas kernels for 9% -> 9%
where the time goes in v1:
time: 62.4 us; the launch traced here: 61.9 us
  starting transfers between devices  30.1 us (48%)
  waiting for transfers between devices  20.8 us (33%)
  Pallas kernels  5.47 us (9%)
  other arithmetic  3.14 us (5%)
  local copies, waits for them, and re-layouts  1.65 us (3%)
  between operations  0.78 us (1%)
    ppermute x25, starting transfers between devices, swap(): return lax.ppermute(x, ('seq', 'head'), pairs)  30.1 us
    ppermute x25, waiting for transfers between devices, swap(): return lax.ppermute(x, ('seq', 'head'), pairs)  20.8 us
    pallas_call x2, Pallas kernels, attention(): pl.pallas_call(functools.partial(attention_kernel, column_count, group_la...  5.47 us
    squeeze x1, other arithmetic, piece(): return lax.dynamic_index_in_dim(both, z ^ flip, 0, keepdims=False)  1.51 us
  transfers between devices with their start and end apart: 25, of which 11 were waited for; matrix products, arithmetic and copies ran while one was open for 5% of the time, Pallas kernels for 9%

profile of v1, /device:TPU:0, one launch (start us, length us, event | category | flops | bytes accessed | tf_op | source)
XLA Modules:
  0.0 61.9 jit_solution(5953201603917455908)
XLA Ops:
  0.6 0.9 %fusion.17 = (bf16[1,2,256,128]{3,2,1,0:T(8,128)(2,1)S(1)}, bf16[2,256,128]{2,1,0:T(8,128)(2,1)S(1)}) fusion(bf16[1,256,128]{2,1,0:T(8,128)(2,1)} %bitcast.91, bf16[1,256,128]{2,1,0:T(8,128)(2,1)} %bitcast.92), kind=kLoop, calls=%fused_computation.45 | loop fusion | flops 65536 | bytes 393216 | tf_op jit(solution)/shard_map/stack | solution.py:267
  1.5 4.1 %collective-permute-start.7 = (bf16[2,256,128]{2,1,0:T(8,128)(2,1)S(1)}, bf16[2,256,128]{2,1,0:T(8,128)(2,1)S(1)}, u32[]{:S(2)}, u32[]{:S(2)}) collective-permute-start(bf16[2,256,128]{2,1,0:T(8,128)(2,1)S(1)} %get-tuple-element.40.refs_2_), channel_id=1, source_target_pairs={{0,2},{1,3},{2,0},{3,1},{4,6},{5,7},{6,4},{7,5},{8,10},{9,11},{10,... | collective-permute-start | bytes 393224 | tf_op jit(solution)/shard_map/ppermute | solution.py:259
  5.6 1.5 %collective-permute-start.1 = (bf16[2,256,128]{2,1,0:T(8,128)(2,1)S(1)}, bf16[2,256,128]{2,1,0:T(8,128)(2,1)S(1)}, u32[]{:S(2)}, u32[]{:S(2)}) collective-permute-start(bf16[2,256,128]{2,1,0:T(8,128)(2,1)S(1)} %get-tuple-element.40.refs_2_), channel_id=1, source_target_pairs={{0,8},{1,9},{2,10},{3,11},{4,12},{5,13},{6,14},{7,15},{8,0},{9,1},... | collective-permute-start | bytes 393224 | tf_op jit(solution)/shard_map/ppermute | solution.py:259
  7.1 1.5 %collective-permute-start.2 = (bf16[2,256,128]{2,1,0:T(8,128)(2,1)S(1)}, bf16[2,256,128]{2,1,0:T(8,128)(2,1)S(1)}, u32[]{:S(2)}, u32[]{:S(2)}) collective-permute-start(bf16[2,256,128]{2,1,0:T(8,128)(2,1)S(1)} %get-tuple-element.40.refs_2_), channel_id=1, source_target_pairs={{0,16},{1,17},{2,18},{3,19},{4,20},{5,21},{6,22},{7,23},{8,24},{9,... | collective-permute-start | bytes 393224 | tf_op jit(solution)/shard_map/ppermute | solution.py:259
  8.6 1.5 %fusion.5 = (bf16[2,2,5,64,128]{4,3,2,1,0:T(8,128)(2,1)S(1)}, bf16[2,2,5,64,128]{4,3,2,1,0:T(8,128)(2,1)S(1)}, bf16[2,2,5,64,128]{4,3,2,1,0:T(8,128)(2,1)S(1)}, bf16[2,2,5,64,128]{4,3,2,1,0:T(8,128)(2,1)S(1)}) fusion(s32[]{:T(128)S(6)} %select_n.19, bf16[1,2,64,4,5,128]{5,2,4,3,1,0:T(8,128)(2,1)} %bitcast.87, bf16[1,2,64,4,5,128]{5,2,4,3,1,0:T(8,128)(2,1)} %bitcast.88, ...), kind=kLoop, calls=%fused_computation.18 | loop fusion | flops 655360 | bytes 2621456 | tf_op jit(solution)/shard_map/jit(dynamic_index_in_dim)/squeeze | solution.py:274
  10.1 0.0 copy-start
  10.2 1.6 %collective-permute-start.6 = (bf16[2,2,5,64,128]{4,3,2,1,0:T(8,128)(2,1)S(1)}, bf16[2,2,5,64,128]{4,3,2,1,0:T(8,128)(2,1)S(1)}, u32[]{:S(2)}, u32[]{:S(2)}) collective-permute-start(bf16[2,2,5,64,128]{4,3,2,1,0:T(8,128)(2,1)S(1)} %get-tuple-element.26), channel_id=1, source_target_pairs={{0,1},{1,0},{2,3},{3,2},{4,5},{5,4},{6,7},{7,6},{8,9},{9,8},{10,11... | collective-permute-start | bytes 983048 | tf_op jit(solution)/shard_map/ppermute | solution.py:259
  11.8 0.5 collective-permute-start.3
  12.3 0.0 collective-permute-done.7.refs_2_
  12.3 1.5 %collective-permute-start.8 = (bf16[2,256,128]{2,1,0:T(8,128)(2,1)S(1)}, bf16[2,256,128]{2,1,0:T(8,128)(2,1)S(1)}, u32[]{:S(2)}, u32[]{:S(2)}) collective-permute-start(bf16[2,256,128]{2,1,0:T(8,128)(2,1)S(1)} %collective-permute-done.7.refs_2_), channel_id=1, source_target_pairs={{0,8},{1,9},{2,10},{3,11},{4,12},{5,13},{6,14},{7,15},{8,0},{9,1},... | collective-permute-start | bytes 393224 | tf_op jit(solution)/shard_map/ppermute | solution.py:259
  13.8 0.0 collective-permute-done.1.refs_3_
  13.8 1.5 %collective-permute-start.9 = (bf16[2,256,128]{2,1,0:T(8,128)(2,1)S(1)}, bf16[2,256,128]{2,1,0:T(8,128)(2,1)S(1)}, u32[]{:S(2)}, u32[]{:S(2)}) collective-permute-start(bf16[2,256,128]{2,1,0:T(8,128)(2,1)S(1)} %collective-permute-done.7.refs_2_), channel_id=1, source_target_pairs={{0,16},{1,17},{2,18},{3,19},{4,20},{5,21},{6,22},{7,23},{8,24},{9,... | collective-permute-start | bytes 393224 | tf_op jit(solution)/shard_map/ppermute | solution.py:259
  15.3 0.0 collective-permute-done.2.refs_4_
  15.3 0.5 collective-permute-start.10
  15.8 3.5 %collective-permute-done.3.refs_5_ = bf16[2,256,128]{2,1,0:T(8,128)(2,1)S(1)} collective-permute-done((bf16[2,256,128]{2,1,0:T(8,128)(2,1)S(1)}, bf16[2,256,128]{2,1,0:T(8,128)(2,1)S(1)}, u32[]{:S(2)}, u32[]{:S(2)}) %collective-permute-start.3) | collective-permute-done | bytes 131104 | tf_op jit(solution)/shard_map/ppermute | solution.py:259
  19.2 0.0 collective-permute-start.11
  19.2 0.9 %collective-permute-done.8.refs_3_ = bf16[2,256,128]{2,1,0:T(8,128)(2,1)S(1)} collective-permute-done((bf16[2,256,128]{2,1,0:T(8,128)(2,1)S(1)}, bf16[2,256,128]{2,1,0:T(8,128)(2,1)S(1)}, u32[]{:S(2)}, u32[]{:S(2)}) %collective-permute-start.8) | collective-permute-done | bytes 131104 | tf_op jit(solution)/shard_map/ppermute | solution.py:259
  20.1 0.0 collective-permute-start.12
  20.1 0.9 %collective-permute-done.9.refs_4_ = bf16[2,256,128]{2,1,0:T(8,128)(2,1)S(1)} collective-permute-done((bf16[2,256,128]{2,1,0:T(8,128)(2,1)S(1)}, bf16[2,256,128]{2,1,0:T(8,128)(2,1)S(1)}, u32[]{:S(2)}, u32[]{:S(2)}) %collective-permute-start.9) | collective-permute-done | bytes 131104 | tf_op jit(solution)/shard_map/ppermute | solution.py:259
  21.0 0.0 collective-permute-start.13
  21.0 1.4 %collective-permute-done.10.refs_5_ = bf16[2,256,128]{2,1,0:T(8,128)(2,1)S(1)} collective-permute-done((bf16[2,256,128]{2,1,0:T(8,128)(2,1)S(1)}, bf16[2,256,128]{2,1,0:T(8,128)(2,1)S(1)}, u32[]{:S(2)}, u32[]{:S(2)}) %collective-permute-start.10) | collective-permute-done | bytes 131104 | tf_op jit(solution)/shard_map/ppermute | solution.py:259
  22.5 0.0 collective-permute-start.14
  22.5 0.1 pad_maximum_fusion.1
  22.5 0.0 collective-permute-done.11.refs_6_
  22.6 1.7 %collective-permute-start = (bf16[2,2,5,64,128]{4,3,2,1,0:T(8,128)(2,1)S(1)}, bf16[2,2,5,64,128]{4,3,2,1,0:T(8,128)(2,1)S(1)}, u32[]{:S(2)}, u32[]{:S(2)}) collective-permute-start(bf16[2,2,5,64,128]{4,3,2,1,0:T(8,128)(2,1)S(1)} %get-tuple-element.23), channel_id=1, source_target_pairs={{0,1},{1,0},{2,3},{3,2},{4,5},{5,4},{6,7},{7,6},{8,9},{9,8},{10,11... | collective-permute-start | bytes 983048 | tf_op jit(solution)/shard_map/ppermute | solution.py:259
  24.2 0.0 collective-permute-done.6.refs_1_
  24.2 0.0 collective-permute-start.4
  24.2 0.0 collective-permute-done.12.refs_7_
  24.2 0.0 collective-permute-done.13.refs_8_
  24.2 0.0 collective-permute-done.14.refs_9_
  24.3 2.7 %attention_far.1 = (bf16[2,5,64,128]{3,2,1,0:T(8,128)(2,1)S(1)}, bf16[2,5,64,128]{3,2,1,0:T(8,128)(2,1)S(1)}, f32[4,2,256,128]{3,2,1,0:T(8,128)S(1)}, bf16[4,2,256,128]{3,2,1,0:T(8,128)(2,1)S(1)}) custom-call(s32[2048]{0:T(1024)S(1)} %copy-done, s32[16,128]{1,0:T(8,128)S(1)} %bitcast.84, bf16[2,2,5,64,128]{4,3,2,1,0:T(8,128)(2,1)S(1)} %get-tuple-element.25.refs_0_, ...), custom_call_target="tpu_custom_call" | custom-call | flops 3355443200 | bytes 4194304 | tf_op jit(solution)/shard_map/attention_far/pallas_call | solution.py:214
  27.0 1.4 %collective-permute-start.20 = (bf16[4,2,256,128]{3,2,1,0:T(8,128)(2,1)S(1)}, bf16[4,2,256,128]{3,2,1,0:T(8,128)(2,1)S(1)}, u32[]{:S(2)}, u32[]{:S(2)}) collective-permute-start(bf16[4,2,256,128]{3,2,1,0:T(8,128)(2,1)S(1)} %get-tuple-element.18), channel_id=1, source_target_pairs={{0,4},{1,5},{2,6},{3,7},{4,0},{5,1},{6,2},{7,3},{8,12},{9,13},{10,... | collective-permute-start | bytes 1572872 | tf_op jit(solution)/shard_map/ppermute | solution.py:259
  28.4 0.7 %collective-permute-start.15 = (bf16[2,5,64,128]{3,2,1,0:T(8,128)(2,1)S(1)}, bf16[2,5,64,128]{3,2,1,0:T(8,128)(2,1)S(1)}, u32[]{:S(2)}, u32[]{:S(2)}) collective-permute-start(bf16[2,5,64,128]{3,2,1,0:T(8,128)(2,1)S(1)} %get-tuple-element.14), channel_id=1, source_target_pairs={{0,1},{1,0},{2,3},{3,2},{4,5},{5,4},{6,7},{7,6},{8,9},{9,8},{10,11... | collective-permute-start | bytes 491528 | tf_op jit(solution)/shard_map/ppermute | solution.py:259
  29.1 4.0 %collective-permute-done.refs_1_ = bf16[2,2,5,64,128]{4,3,2,1,0:T(8,128)(2,1)S(1)} collective-permute-done((bf16[2,2,5,64,128]{4,3,2,1,0:T(8,128)(2,1)S(1)}, bf16[2,2,5,64,128]{4,3,2,1,0:T(8,128)(2,1)S(1)}, u32[]{:S(2)}, u32[]{:S(2)}) %collective-permute-start) | collective-permute-done | bytes 327712 | tf_op jit(solution)/shard_map/ppermute | solution.py:259
  33.1 0.0 collective-permute-done.4.refs_6_
  33.1 2.7 %attention_near.1 = (bf16[2,5,64,128]{3,2,1,0:T(8,128)(2,1)S(1)}, bf16[2,5,64,128]{3,2,1,0:T(8,128)(2,1)S(1)}, f32[4,2,256,128]{3,2,1,0:T(8,128)S(1)}, bf16[4,2,256,128]{3,2,1,0:T(8,128)(2,1)S(1)}) custom-call(s32[2048]{0:T(1024)S(1)} %copy-done, s32[16,128]{1,0:T(8,128)S(1)} %bitcast.85, bf16[2,2,5,64,128]{4,3,2,1,0:T(8,128)(2,1)S(1)} %get-tuple-element.24.refs_0_, ...), custom_call_target="tpu_custom_call" | custom-call | flops 3355443200 | bytes 4194304 | tf_op jit(solution)/shard_map/attention_near/pallas_call | solution.py:214
  35.9 0.3 collective-permute-start.16
  36.1 1.6 %collective-permute-start.5 = (bf16[2,5,64,128]{3,2,1,0:T(8,128)(2,1)S(1)}, bf16[2,5,64,128]{3,2,1,0:T(8,128)(2,1)S(1)}, u32[]{:S(2)}, u32[]{:S(2)}) collective-permute-start(bf16[2,5,64,128]{3,2,1,0:T(8,128)(2,1)S(1)} %get-tuple-element.12), channel_id=1, source_target_pairs={{0,1},{1,0},{2,3},{3,2},{4,5},{5,4},{6,7},{7,6},{8,9},{9,8},{10,11... | collective-permute-start | bytes 491528 | tf_op jit(solution)/shard_map/ppermute | solution.py:259
  37.7 0.0 collective-permute-done.20
  37.7 0.2 fusion.19
  37.9 2.3 %collective-permute-start.21 = (bf16[2,256,128]{2,1,0:T(8,128)(2,1)S(1)}, bf16[2,256,128]{2,1,0:T(8,128)(2,1)S(1)}, u32[]{:S(2)}, u32[]{:S(2)}) collective-permute-start(bf16[2,256,128]{2,1,0:T(8,128)(2,1)S(1)} %get-tuple-element.34), channel_id=1, source_target_pairs={{0,8},{1,9},{2,10},{3,11},{4,12},{5,13},{6,14},{7,15},{8,0},{9,1},... | collective-permute-start | bytes 393224 | tf_op jit(solution)/shard_map/ppermute | solution.py:259
  40.2 1.9 %collective-permute-start.22 = (bf16[2,256,128]{2,1,0:T(8,128)(2,1)S(1)}, bf16[2,256,128]{2,1,0:T(8,128)(2,1)S(1)}, u32[]{:S(2)}, u32[]{:S(2)}) collective-permute-start(bf16[2,256,128]{2,1,0:T(8,128)(2,1)S(1)} %get-tuple-element.36), channel_id=1, source_target_pairs={{0,16},{1,17},{2,18},{3,19},{4,20},{5,21},{6,22},{7,23},{8,24},{9,... | collective-permute-start | bytes 393224 | tf_op jit(solution)/shard_map/ppermute | solution.py:259
  42.1 0.0 collective-permute-done.15
  42.1 1.4 %collective-permute-start.23 = (bf16[2,256,128]{2,1,0:T(8,128)(2,1)S(1)}, bf16[2,256,128]{2,1,0:T(8,128)(2,1)S(1)}, u32[]{:S(2)}, u32[]{:S(2)}) collective-permute-start(bf16[2,256,128]{2,1,0:T(8,128)(2,1)S(1)} %get-tuple-element.35), channel_id=1, source_target_pairs={{0,24},{1,25},{2,26},{3,27},{4,28},{5,29},{6,30},{7,31},{8,16},{9,... | collective-permute-start | bytes 393224 | tf_op jit(solution)/shard_map/ppermute | solution.py:259
  43.5 0.0 collective-permute-done.5
  43.5 0.1 pad_maximum_fusion
  43.6 0.3 collective-permute-done.21
  43.9 4.1 %collective-permute-done.22 = bf16[2,256,128]{2,1,0:T(8,128)(2,1)S(1)} collective-permute-done((bf16[2,256,128]{2,1,0:T(8,128)(2,1)S(1)}, bf16[2,256,128]{2,1,0:T(8,128)(2,1)S(1)}, u32[]{:S(2)}, u32[]{:S(2)}) %collective-permute-start.22) | collective-permute-done | bytes 131104 | tf_op jit(solution)/shard_map/ppermute | solution.py:259
  48.0 1.8 %collective-permute-done.23 = bf16[2,256,128]{2,1,0:T(8,128)(2,1)S(1)} collective-permute-done((bf16[2,256,128]{2,1,0:T(8,128)(2,1)S(1)}, bf16[2,256,128]{2,1,0:T(8,128)(2,1)S(1)}, u32[]{:S(2)}, u32[]{:S(2)}) %collective-permute-start.23) | collective-permute-done | bytes 131104 | tf_op jit(solution)/shard_map/ppermute | solution.py:259
  49.8 0.1 fusion.11
  49.9 2.6 %collective-permute-start.24 = (bf16[2,256,128]{2,1,0:T(8,128)(2,1)S(1)}, bf16[2,256,128]{2,1,0:T(8,128)(2,1)S(1)}, u32[]{:S(2)}, u32[]{:S(2)}) collective-permute-start(bf16[2,256,128]{2,1,0:T(8,128)(2,1)S(1)} %fusion.11), channel_id=1, source_target_pairs={{0,2},{1,3},{2,0},{3,1},{4,6},{5,7},{6,4},{7,5},{8,10},{9,11},{10,... | collective-permute-start | bytes 393224 | tf_op jit(solution)/shard_map/ppermute | solution.py:259
  52.6 0.0 collective-permute-done.16
  52.6 0.2 fusion.18
  52.8 0.6 %collective-permute-start.17 = (bf16[2,256,128]{2,1,0:T(8,128)(2,1)S(1)}, bf16[2,256,128]{2,1,0:T(8,128)(2,1)S(1)}, u32[]{:S(2)}, u32[]{:S(2)}) collective-permute-start(bf16[2,256,128]{2,1,0:T(8,128)(2,1)S(1)} %get-tuple-element.31), channel_id=1, source_target_pairs={{0,8},{1,9},{2,10},{3,11},{4,12},{5,13},{6,14},{7,15},{8,0},{9,1},... | collective-permute-start | bytes 393224 | tf_op jit(solution)/shard_map/ppermute | solution.py:259
  53.4 1.7 %collective-permute-start.18 = (bf16[2,256,128]{2,1,0:T(8,128)(2,1)S(1)}, bf16[2,256,128]{2,1,0:T(8,128)(2,1)S(1)}, u32[]{:S(2)}, u32[]{:S(2)}) collective-permute-start(bf16[2,256,128]{2,1,0:T(8,128)(2,1)S(1)} %get-tuple-element.33), channel_id=1, source_target_pairs={{0,16},{1,17},{2,18},{3,19},{4,20},{5,21},{6,22},{7,23},{8,24},{9,... | collective-permute-start | bytes 393224 | tf_op jit(solution)/shard_map/ppermute | solution.py:259
  55.2 1.2 %collective-permute-start.19 = (bf16[2,256,128]{2,1,0:T(8,128)(2,1)S(1)}, bf16[2,256,128]{2,1,0:T(8,128)(2,1)S(1)}, u32[]{:S(2)}, u32[]{:S(2)}) collective-permute-start(bf16[2,256,128]{2,1,0:T(8,128)(2,1)S(1)} %get-tuple-element.32), channel_id=1, source_target_pairs={{0,24},{1,25},{2,26},{3,27},{4,28},{5,29},{6,30},{7,31},{8,16},{9,... | collective-permute-start | bytes 393224 | tf_op jit(solution)/shard_map/ppermute | solution.py:259
  56.4 0.1 maximum_bitcast_fusion
  56.5 0.9 %copy.10 = bf16[2,64,4,5,128]{4,1,3,2,0:T(8,128)(2,1)} copy(bf16[2,64,4,5,128]{4,1,3,0,2:T(8,128)(2,1)S(1)} %maximum_bitcast_fusion) | data formatting | bytes 1310720 | tf_op jit(solution)/shard_map/transpose | solution.py:305
  57.4 1.1 %collective-permute-done.24 = bf16[2,256,128]{2,1,0:T(8,128)(2,1)S(1)} collective-permute-done((bf16[2,256,128]{2,1,0:T(8,128)(2,1)S(1)}, bf16[2,256,128]{2,1,0:T(8,128)(2,1)S(1)}, u32[]{:S(2)}, u32[]{:S(2)}) %collective-permute-start.24) | collective-permute-done | bytes 131104 | tf_op jit(solution)/shard_map/ppermute | solution.py:259
  58.4 0.3 collective-permute-done.17
  58.7 2.4 %collective-permute-done.18 = bf16[2,256,128]{2,1,0:T(8,128)(2,1)S(1)} collective-permute-done((bf16[2,256,128]{2,1,0:T(8,128)(2,1)S(1)}, bf16[2,256,128]{2,1,0:T(8,128)(2,1)S(1)}, u32[]{:S(2)}, u32[]{:S(2)}) %collective-permute-start.18) | collective-permute-done | bytes 131104 | tf_op jit(solution)/shard_map/ppermute | solution.py:259
  61.1 0.0 collective-permute-done.19
  61.1 0.1 fusion.16
  61.2 0.7 %slice_bitcast_fusion.8 = (bf16[256,1,128]{2,0,1:T(8,128)(2,1)}, bf16[256,1,128]{2,0,1:T(8,128)(2,1)}) fusion(bf16[2,256,128]{2,1,0:T(8,128)(2,1)S(1)} %fusion.16), kind=kLoop, calls=%fused_computation.39 | loop fusion | bytes 262144 | tf_op jit(solution)/shard_map/squeeze | solution.py:307
  (4 shorter events, 0.1 us)
Async XLA Ops:
  1.5 10.8 %collective-permute-start.7 = (bf16[2,256,128]{2,1,0:T(8,128)(2,1)S(1)}, bf16[2,256,128]{2,1,0:T(8,128)(2,1)S(1)}, u32[]{:S(2)}, u32[]{:S(2)}) collective-permute-start(bf16[2,256,128]{2,1,0:T(8,128)(2,1)S(1)} %get-tuple-element.40.refs_2_), channel_id=1, source_target_pairs={{0,2},{1,3},{2,0},{3,1},{4,6},{5,7},{6,4},{7,5},{8,10},{9,11},{10,... | collective-permute-start | bytes 393224 | tf_op jit(solution)/shard_map/ppermute | solution.py:259
  5.6 8.2 %collective-permute-start.1 = (bf16[2,256,128]{2,1,0:T(8,128)(2,1)S(1)}, bf16[2,256,128]{2,1,0:T(8,128)(2,1)S(1)}, u32[]{:S(2)}, u32[]{:S(2)}) collective-permute-start(bf16[2,256,128]{2,1,0:T(8,128)(2,1)S(1)} %get-tuple-element.40.refs_2_), channel_id=1, source_target_pairs={{0,8},{1,9},{2,10},{3,11},{4,12},{5,13},{6,14},{7,15},{8,0},{9,1},... | collective-permute-start | bytes 393224 | tf_op jit(solution)/shard_map/ppermute | solution.py:259
  7.1 8.2 %collective-permute-start.2 = (bf16[2,256,128]{2,1,0:T(8,128)(2,1)S(1)}, bf16[2,256,128]{2,1,0:T(8,128)(2,1)S(1)}, u32[]{:S(2)}, u32[]{:S(2)}) collective-permute-start(bf16[2,256,128]{2,1,0:T(8,128)(2,1)S(1)} %get-tuple-element.40.refs_2_), channel_id=1, source_target_pairs={{0,16},{1,17},{2,18},{3,19},{4,20},{5,21},{6,22},{7,23},{8,24},{9,... | collective-permute-start | bytes 393224 | tf_op jit(solution)/shard_map/ppermute | solution.py:259
  10.1 14.1 %copy-start = (s32[2048]{0:T(1024)S(1)}, s32[2048]{0:T(1024)}, u32[]{:S(2)}) copy-start(s32[2048]{0:T(1024)} %doc_ref.3) | copy-start | bytes 24580
  10.2 14.1 %collective-permute-start.6 = (bf16[2,2,5,64,128]{4,3,2,1,0:T(8,128)(2,1)S(1)}, bf16[2,2,5,64,128]{4,3,2,1,0:T(8,128)(2,1)S(1)}, u32[]{:S(2)}, u32[]{:S(2)}) collective-permute-start(bf16[2,2,5,64,128]{4,3,2,1,0:T(8,128)(2,1)S(1)} %get-tuple-element.26), channel_id=1, source_target_pairs={{0,1},{1,0},{2,3},{3,2},{4,5},{5,4},{6,7},{7,6},{8,9},{9,8},{10,11... | collective-permute-start | bytes 983048 | tf_op jit(solution)/shard_map/ppermute | solution.py:259
  11.8 7.4 %collective-permute-start.3 = (bf16[2,256,128]{2,1,0:T(8,128)(2,1)S(1)}, bf16[2,256,128]{2,1,0:T(8,128)(2,1)S(1)}, u32[]{:S(2)}, u32[]{:S(2)}) collective-permute-start(bf16[2,256,128]{2,1,0:T(8,128)(2,1)S(1)} %get-tuple-element.40.refs_2_), channel_id=1, source_target_pairs={{0,24},{1,25},{2,26},{3,27},{4,28},{5,29},{6,30},{7,31},{8,16},{9,... | collective-permute-start | bytes 393224 | tf_op jit(solution)/shard_map/ppermute | solution.py:259
  12.3 7.8 %collective-permute-start.8 = (bf16[2,256,128]{2,1,0:T(8,128)(2,1)S(1)}, bf16[2,256,128]{2,1,0:T(8,128)(2,1)S(1)}, u32[]{:S(2)}, u32[]{:S(2)}) collective-permute-start(bf16[2,256,128]{2,1,0:T(8,128)(2,1)S(1)} %collective-permute-done.7.refs_2_), channel_id=1, source_target_pairs={{0,8},{1,9},{2,10},{3,11},{4,12},{5,13},{6,14},{7,15},{8,0},{9,1},... | collective-permute-start | bytes 393224 | tf_op jit(solution)/shard_map/ppermute | solution.py:259
  13.8 7.3 %collective-permute-start.9 = (bf16[2,256,128]{2,1,0:T(8,128)(2,1)S(1)}, bf16[2,256,128]{2,1,0:T(8,128)(2,1)S(1)}, u32[]{:S(2)}, u32[]{:S(2)}) collective-permute-start(bf16[2,256,128]{2,1,0:T(8,128)(2,1)S(1)} %collective-permute-done.7.refs_2_), channel_id=1, source_target_pairs={{0,16},{1,17},{2,18},{3,19},{4,20},{5,21},{6,22},{7,23},{8,24},{9,... | collective-permute-start | bytes 393224 | tf_op jit(solution)/shard_map/ppermute | solution.py:259
  15.3 7.2 %collective-permute-start.10 = (bf16[2,256,128]{2,1,0:T(8,128)(2,1)S(1)}, bf16[2,256,128]{2,1,0:T(8,128)(2,1)S(1)}, u32[]{:S(2)}, u32[]{:S(2)}) collective-permute-start(bf16[2,256,128]{2,1,0:T(8,128)(2,1)S(1)} %collective-permute-done.7.refs_2_), channel_id=1, source_target_pairs={{0,24},{1,25},{2,26},{3,27},{4,28},{5,29},{6,30},{7,31},{8,16},{9,... | collective-permute-start | bytes 393224 | tf_op jit(solution)/shard_map/ppermute | solution.py:259
  19.2 3.3 %collective-permute-start.11 = (bf16[2,256,128]{2,1,0:T(8,128)(2,1)S(1)}, bf16[2,256,128]{2,1,0:T(8,128)(2,1)S(1)}, u32[]{:S(2)}, u32[]{:S(2)}) collective-permute-start(bf16[2,256,128]{2,1,0:T(8,128)(2,1)S(1)} %collective-permute-done.7.refs_2_), channel_id=1, source_target_pairs={{0,4},{1,5},{2,6},{3,7},{4,0},{5,1},{6,2},{7,3},{8,12},{9,13},{10,... | collective-permute-start | bytes 393224 | tf_op jit(solution)/shard_map/ppermute | solution.py:259
  20.1 4.1 %collective-permute-start.12 = (bf16[2,256,128]{2,1,0:T(8,128)(2,1)S(1)}, bf16[2,256,128]{2,1,0:T(8,128)(2,1)S(1)}, u32[]{:S(2)}, u32[]{:S(2)}) collective-permute-start(bf16[2,256,128]{2,1,0:T(8,128)(2,1)S(1)} %collective-permute-done.8.refs_3_), channel_id=1, source_target_pairs={{0,4},{1,5},{2,6},{3,7},{4,0},{5,1},{6,2},{7,3},{8,12},{9,13},{10,... | collective-permute-start | bytes 393224 | tf_op jit(solution)/shard_map/ppermute | solution.py:259
  21.0 3.2 %collective-permute-start.13 = (bf16[2,256,128]{2,1,0:T(8,128)(2,1)S(1)}, bf16[2,256,128]{2,1,0:T(8,128)(2,1)S(1)}, u32[]{:S(2)}, u32[]{:S(2)}) collective-permute-start(bf16[2,256,128]{2,1,0:T(8,128)(2,1)S(1)} %collective-permute-done.9.refs_4_), channel_id=1, source_target_pairs={{0,4},{1,5},{2,6},{3,7},{4,0},{5,1},{6,2},{7,3},{8,12},{9,13},{10,... | collective-permute-start | bytes 393224 | tf_op jit(solution)/shard_map/ppermute | solution.py:259
  22.5 1.8 %collective-permute-start.14 = (bf16[2,256,128]{2,1,0:T(8,128)(2,1)S(1)}, bf16[2,256,128]{2,1,0:T(8,128)(2,1)S(1)}, u32[]{:S(2)}, u32[]{:S(2)}) collective-permute-start(bf16[2,256,128]{2,1,0:T(8,128)(2,1)S(1)} %collective-permute-done.10.refs_5_), channel_id=1, source_target_pairs={{0,4},{1,5},{2,6},{3,7},{4,0},{5,1},{6,2},{7,3},{8,12},{9,13},{10,... | collective-permute-start | bytes 393224 | tf_op jit(solution)/shard_map/ppermute | solution.py:259
  22.6 10.6 %collective-permute-start = (bf16[2,2,5,64,128]{4,3,2,1,0:T(8,128)(2,1)S(1)}, bf16[2,2,5,64,128]{4,3,2,1,0:T(8,128)(2,1)S(1)}, u32[]{:S(2)}, u32[]{:S(2)}) collective-permute-start(bf16[2,2,5,64,128]{4,3,2,1,0:T(8,128)(2,1)S(1)} %get-tuple-element.23), channel_id=1, source_target_pairs={{0,1},{1,0},{2,3},{3,2},{4,5},{5,4},{6,7},{7,6},{8,9},{9,8},{10,11... | collective-permute-start | bytes 983048 | tf_op jit(solution)/shard_map/ppermute | solution.py:259
  24.2 8.9 %collective-permute-start.4 = (bf16[4,2,256,128]{3,2,1,0:T(8,128)(2,1)S(1)}, bf16[4,2,256,128]{3,2,1,0:T(8,128)(2,1)S(1)}, u32[]{:S(2)}, u32[]{:S(2)}) collective-permute-start(bf16[4,2,256,128]{3,2,1,0:T(8,128)(2,1)S(1)} %pad_maximum_fusion.1), channel_id=1, source_target_pairs={{0,4},{1,5},{2,6},{3,7},{4,0},{5,1},{6,2},{7,3},{8,12},{9,13},{10,... | collective-permute-start | bytes 1572872 | tf_op jit(solution)/shard_map/ppermute | solution.py:259
  27.0 10.7 %collective-permute-start.20 = (bf16[4,2,256,128]{3,2,1,0:T(8,128)(2,1)S(1)}, bf16[4,2,256,128]{3,2,1,0:T(8,128)(2,1)S(1)}, u32[]{:S(2)}, u32[]{:S(2)}) collective-permute-start(bf16[4,2,256,128]{3,2,1,0:T(8,128)(2,1)S(1)} %get-tuple-element.18), channel_id=1, source_target_pairs={{0,4},{1,5},{2,6},{3,7},{4,0},{5,1},{6,2},{7,3},{8,12},{9,13},{10,... | collective-permute-start | bytes 1572872 | tf_op jit(solution)/shard_map/ppermute | solution.py:259
  28.4 13.7 %collective-permute-start.15 = (bf16[2,5,64,128]{3,2,1,0:T(8,128)(2,1)S(1)}, bf16[2,5,64,128]{3,2,1,0:T(8,128)(2,1)S(1)}, u32[]{:S(2)}, u32[]{:S(2)}) collective-permute-start(bf16[2,5,64,128]{3,2,1,0:T(8,128)(2,1)S(1)} %get-tuple-element.14), channel_id=1, source_target_pairs={{0,1},{1,0},{2,3},{3,2},{4,5},{5,4},{6,7},{7,6},{8,9},{9,8},{10,11... | collective-permute-start | bytes 491528 | tf_op jit(solution)/shard_map/ppermute | solution.py:259
  35.9 16.7 %collective-permute-start.16 = (bf16[4,2,256,128]{3,2,1,0:T(8,128)(2,1)S(1)}, bf16[4,2,256,128]{3,2,1,0:T(8,128)(2,1)S(1)}, u32[]{:S(2)}, u32[]{:S(2)}) collective-permute-start(bf16[4,2,256,128]{3,2,1,0:T(8,128)(2,1)S(1)} %get-tuple-element.16), channel_id=1, source_target_pairs={{0,4},{1,5},{2,6},{3,7},{4,0},{5,1},{6,2},{7,3},{8,12},{9,13},{10,... | collective-permute-start | bytes 1572872 | tf_op jit(solution)/shard_map/ppermute | solution.py:259
  36.1 7.4 %collective-permute-start.5 = (bf16[2,5,64,128]{3,2,1,0:T(8,128)(2,1)S(1)}, bf16[2,5,64,128]{3,2,1,0:T(8,128)(2,1)S(1)}, u32[]{:S(2)}, u32[]{:S(2)}) collective-permute-start(bf16[2,5,64,128]{3,2,1,0:T(8,128)(2,1)S(1)} %get-tuple-element.12), channel_id=1, source_target_pairs={{0,1},{1,0},{2,3},{3,2},{4,5},{5,4},{6,7},{7,6},{8,9},{9,8},{10,11... | collective-permute-start | bytes 491528 | tf_op jit(solution)/shard_map/ppermute | solution.py:259
  37.9 6.0 %collective-permute-start.21 = (bf16[2,256,128]{2,1,0:T(8,128)(2,1)S(1)}, bf16[2,256,128]{2,1,0:T(8,128)(2,1)S(1)}, u32[]{:S(2)}, u32[]{:S(2)}) collective-permute-start(bf16[2,256,128]{2,1,0:T(8,128)(2,1)S(1)} %get-tuple-element.34), channel_id=1, source_target_pairs={{0,8},{1,9},{2,10},{3,11},{4,12},{5,13},{6,14},{7,15},{8,0},{9,1},... | collective-permute-start | bytes 393224 | tf_op jit(solution)/shard_map/ppermute | solution.py:259
  40.2 7.8 %collective-permute-start.22 = (bf16[2,256,128]{2,1,0:T(8,128)(2,1)S(1)}, bf16[2,256,128]{2,1,0:T(8,128)(2,1)S(1)}, u32[]{:S(2)}, u32[]{:S(2)}) collective-permute-start(bf16[2,256,128]{2,1,0:T(8,128)(2,1)S(1)} %get-tuple-element.36), channel_id=1, source_target_pairs={{0,16},{1,17},{2,18},{3,19},{4,20},{5,21},{6,22},{7,23},{8,24},{9,... | collective-permute-start | bytes 393224 | tf_op jit(solution)/shard_map/ppermute | solution.py:259
  42.1 7.7 %collective-permute-start.23 = (bf16[2,256,128]{2,1,0:T(8,128)(2,1)S(1)}, bf16[2,256,128]{2,1,0:T(8,128)(2,1)S(1)}, u32[]{:S(2)}, u32[]{:S(2)}) collective-permute-start(bf16[2,256,128]{2,1,0:T(8,128)(2,1)S(1)} %get-tuple-element.35), channel_id=1, source_target_pairs={{0,24},{1,25},{2,26},{3,27},{4,28},{5,29},{6,30},{7,31},{8,16},{9,... | collective-permute-start | bytes 393224 | tf_op jit(solution)/shard_map/ppermute | solution.py:259
  49.9 8.5 %collective-permute-start.24 = (bf16[2,256,128]{2,1,0:T(8,128)(2,1)S(1)}, bf16[2,256,128]{2,1,0:T(8,128)(2,1)S(1)}, u32[]{:S(2)}, u32[]{:S(2)}) collective-permute-start(bf16[2,256,128]{2,1,0:T(8,128)(2,1)S(1)} %fusion.11), channel_id=1, source_target_pairs={{0,2},{1,3},{2,0},{3,1},{4,6},{5,7},{6,4},{7,5},{8,10},{9,11},{10,... | collective-permute-start | bytes 393224 | tf_op jit(solution)/shard_map/ppermute | solution.py:259
  52.8 5.9 %collective-permute-start.17 = (bf16[2,256,128]{2,1,0:T(8,128)(2,1)S(1)}, bf16[2,256,128]{2,1,0:T(8,128)(2,1)S(1)}, u32[]{:S(2)}, u32[]{:S(2)}) collective-permute-start(bf16[2,256,128]{2,1,0:T(8,128)(2,1)S(1)} %get-tuple-element.31), channel_id=1, source_target_pairs={{0,8},{1,9},{2,10},{3,11},{4,12},{5,13},{6,14},{7,15},{8,0},{9,1},... | collective-permute-start | bytes 393224 | tf_op jit(solution)/shard_map/ppermute | solution.py:259
  53.4 7.7 %collective-permute-start.18 = (bf16[2,256,128]{2,1,0:T(8,128)(2,1)S(1)}, bf16[2,256,128]{2,1,0:T(8,128)(2,1)S(1)}, u32[]{:S(2)}, u32[]{:S(2)}) collective-permute-start(bf16[2,256,128]{2,1,0:T(8,128)(2,1)S(1)} %get-tuple-element.33), channel_id=1, source_target_pairs={{0,16},{1,17},{2,18},{3,19},{4,20},{5,21},{6,22},{7,23},{8,24},{9,... | collective-permute-start | bytes 393224 | tf_op jit(solution)/shard_map/ppermute | solution.py:259
  55.2 6.0 %collective-permute-start.19 = (bf16[2,256,128]{2,1,0:T(8,128)(2,1)S(1)}, bf16[2,256,128]{2,1,0:T(8,128)(2,1)S(1)}, u32[]{:S(2)}, u32[]{:S(2)}) collective-permute-start(bf16[2,256,128]{2,1,0:T(8,128)(2,1)S(1)} %get-tuple-element.32), channel_id=1, source_target_pairs={{0,24},{1,25},{2,26},{3,27},{4,28},{5,29},{6,30},{7,31},{8,16},{9,... | collective-permute-start | bytes 393224 | tf_op jit(solution)/shard_map/ppermute | solution.py:259

commit v2 on v1

--- a/solution.py
+++ b/solution.py
@@ -292,13 +292,25 @@
             mine = mine + swap(part, 2 * d, 0).astype(jnp.float32)
         return mine
 
-    far_total = add_columns(*add_cores(far_kept, far_sent))
+    far_kept_total, far_sent_total = far_kept[0], far_sent[0].astype(jnp.float32)
+    for d in columns[1:]:
+        both_cores = swap(jnp.stack([far_kept[d].astype(jnp.bfloat16), far_sent[d]]), 2 * d, 0)
+        both_cores = both_cores.astype(jnp.float32)
+        far_kept_total = far_kept_total + both_cores[0]
+        far_sent_total = far_sent_total + both_cores[1]
+    far_back, far_sent_low = lax.optimization_barrier(
+        (swap(far_dq_send, 0, 1), far_sent_total.astype(jnp.bfloat16))
+    )
+    far_by_core = swap(far_sent_low, 1, 0)
+    far_total = far_kept_total + far_by_core.astype(jnp.float32)
     far_low = far_total.astype(jnp.bfloat16)
-    near_total = add_columns(*add_cores(near_kept, near_sent))
+    near_sums = add_cores(near_kept, near_sent)
+    near_total = add_columns(*near_sums)
     final = near_total + swap(far_low, 0, 2).astype(jnp.float32)
     final = final.astype(jnp.bfloat16)[:, :, None, :]
 
-    pieces = jnp.stack([near_dq, swap(near_dq_send, 0, 1), far_dq, swap(far_dq_send, 0, 1)])
+    near_back, _ = lax.optimization_barrier((swap(near_dq_send, 0, 1), near_sums[1][0]))
+    pieces = jnp.stack([near_dq, near_back, far_dq, far_back])
     ordered = [
         lax.dynamic_index_in_dim(pieces, z ^ head, 0, keepdims=False) for head in range(head_count)
     ]

time: 62.4 us -> 59.2 us (0.949); the launches traced: 61.9 us -> 60.2 us
  waiting for transfers between devices: 20.8 us -> 18.5 us
    ppermute x25, waiting for transfers between devices: 20.8 us -> 18.5 us  [swap(): return lax.ppermute(x, ('seq', 'head'), pairs)]
  transfers between devices with their start and end apart: 25 -> 25, of which waited for: 11 -> 9; matrix products, arithmetic and copies ran while one was open for 5% -> 6% of each run, Pallas kernels for 9% -> 9%
where the time goes in v2:
time: 59.2 us; the launch traced here: 60.2 us
  starting transfers between devices  30.2 us (51%)
  waiting for transfers between devices  18.5 us (31%)
  Pallas kernels  5.65 us (10%)
  other arithmetic  3.28 us (6%)
  local copies, waits for them, and re-layouts  1.69 us (3%)
  between operations  0.82 us (1%)
    ppermute x25, starting transfers between devices, swap(): return lax.ppermute(x, ('seq', 'head'), pairs)  30.2 us
    ppermute x25, waiting for transfers between devices, swap(): return lax.ppermute(x, ('seq', 'head'), pairs)  18.5 us
    pallas_call x2, Pallas kernels, attention(): pl.pallas_call(functools.partial(attention_kernel, column_count, group_la...  5.65 us
    squeeze x1, other arithmetic, piece(): return lax.dynamic_index_in_dim(both, z ^ flip, 0, keepdims=False)  1.51 us
  transfers between devices with their start and end apart: 25, of which 9 were waited for; matrix products, arithmetic and copies ran while one was open for 6% of the time, Pallas kernels for 9%

profile of v2, /device:TPU:0, one launch (start us, length us, event | category | flops | bytes accessed | tf_op | source)
XLA Modules:
  0.0 60.2 jit_solution(6251598805815495960)
XLA Ops:
  0.6 0.9 %fusion.18 = (bf16[1,2,256,128]{3,2,1,0:T(8,128)(2,1)S(1)}, bf16[2,256,128]{2,1,0:T(8,128)(2,1)S(1)}) fusion(bf16[1,256,128]{2,1,0:T(8,128)(2,1)} %bitcast.83, bf16[1,256,128]{2,1,0:T(8,128)(2,1)} %bitcast.84), kind=kLoop, calls=%fused_computation.50 | loop fusion | flops 65536 | bytes 393216 | tf_op jit(solution)/shard_map/stack | solution.py:267
  1.5 4.1 %collective-permute-start.8 = (bf16[2,256,128]{2,1,0:T(8,128)(2,1)S(1)}, bf16[2,256,128]{2,1,0:T(8,128)(2,1)S(1)}, u32[]{:S(2)}, u32[]{:S(2)}) collective-permute-start(bf16[2,256,128]{2,1,0:T(8,128)(2,1)S(1)} %get-tuple-element.47.refs_2_), channel_id=1, source_target_pairs={{0,2},{1,3},{2,0},{3,1},{4,6},{5,7},{6,4},{7,5},{8,10},{9,11},{10,... | collective-permute-start | bytes 393224 | tf_op jit(solution)/shard_map/ppermute | solution.py:259
  5.6 1.5 %collective-permute-start.1 = (bf16[2,256,128]{2,1,0:T(8,128)(2,1)S(1)}, bf16[2,256,128]{2,1,0:T(8,128)(2,1)S(1)}, u32[]{:S(2)}, u32[]{:S(2)}) collective-permute-start(bf16[2,256,128]{2,1,0:T(8,128)(2,1)S(1)} %get-tuple-element.47.refs_2_), channel_id=1, source_target_pairs={{0,8},{1,9},{2,10},{3,11},{4,12},{5,13},{6,14},{7,15},{8,0},{9,1},... | collective-permute-start | bytes 393224 | tf_op jit(solution)/shard_map/ppermute | solution.py:259
  7.1 1.5 %collective-permute-start.2 = (bf16[2,256,128]{2,1,0:T(8,128)(2,1)S(1)}, bf16[2,256,128]{2,1,0:T(8,128)(2,1)S(1)}, u32[]{:S(2)}, u32[]{:S(2)}) collective-permute-start(bf16[2,256,128]{2,1,0:T(8,128)(2,1)S(1)} %get-tuple-element.47.refs_2_), channel_id=1, source_target_pairs={{0,16},{1,17},{2,18},{3,19},{4,20},{5,21},{6,22},{7,23},{8,24},{9,... | collective-permute-start | bytes 393224 | tf_op jit(solution)/shard_map/ppermute | solution.py:259
  8.6 1.5 %fusion.5 = (bf16[2,2,5,64,128]{4,3,2,1,0:T(8,128)(2,1)S(1)}, bf16[2,2,5,64,128]{4,3,2,1,0:T(8,128)(2,1)S(1)}, bf16[2,2,5,64,128]{4,3,2,1,0:T(8,128)(2,1)S(1)}, bf16[2,2,5,64,128]{4,3,2,1,0:T(8,128)(2,1)S(1)}) fusion(s32[]{:T(128)S(6)} %select_n.19, bf16[1,2,64,4,5,128]{5,2,4,3,1,0:T(8,128)(2,1)} %bitcast.79, bf16[1,2,64,4,5,128]{5,2,4,3,1,0:T(8,128)(2,1)} %bitcast.80, ...), kind=kLoop, calls=%fused_computation.17 | loop fusion | flops 655360 | bytes 2621456 | tf_op jit(solution)/shard_map/jit(dynamic_index_in_dim)/squeeze | solution.py:274
  10.1 0.0 copy-start
  10.2 1.6 %collective-permute-start.7 = (bf16[2,2,5,64,128]{4,3,2,1,0:T(8,128)(2,1)S(1)}, bf16[2,2,5,64,128]{4,3,2,1,0:T(8,128)(2,1)S(1)}, u32[]{:S(2)}, u32[]{:S(2)}) collective-permute-start(bf16[2,2,5,64,128]{4,3,2,1,0:T(8,128)(2,1)S(1)} %get-tuple-element.30), channel_id=1, source_target_pairs={{0,1},{1,0},{2,3},{3,2},{4,5},{5,4},{6,7},{7,6},{8,9},{9,8},{10,11... | collective-permute-start | bytes 983048 | tf_op jit(solution)/shard_map/ppermute | solution.py:259
  11.8 0.5 collective-permute-start.3
  12.3 0.0 collective-permute-done.8.refs_2_
  12.3 1.5 %collective-permute-start.9 = (bf16[2,256,128]{2,1,0:T(8,128)(2,1)S(1)}, bf16[2,256,128]{2,1,0:T(8,128)(2,1)S(1)}, u32[]{:S(2)}, u32[]{:S(2)}) collective-permute-start(bf16[2,256,128]{2,1,0:T(8,128)(2,1)S(1)} %collective-permute-done.8.refs_2_), channel_id=1, source_target_pairs={{0,8},{1,9},{2,10},{3,11},{4,12},{5,13},{6,14},{7,15},{8,0},{9,1},... | collective-permute-start | bytes 393224 | tf_op jit(solution)/shard_map/ppermute | solution.py:259
  13.8 0.0 collective-permute-done.1.refs_3_
  13.8 1.5 %collective-permute-start.10 = (bf16[2,256,128]{2,1,0:T(8,128)(2,1)S(1)}, bf16[2,256,128]{2,1,0:T(8,128)(2,1)S(1)}, u32[]{:S(2)}, u32[]{:S(2)}) collective-permute-start(bf16[2,256,128]{2,1,0:T(8,128)(2,1)S(1)} %collective-permute-done.8.refs_2_), channel_id=1, source_target_pairs={{0,16},{1,17},{2,18},{3,19},{4,20},{5,21},{6,22},{7,23},{8,24},{9,... | collective-permute-start | bytes 393224 | tf_op jit(solution)/shard_map/ppermute | solution.py:259
  15.3 0.0 collective-permute-done.2.refs_4_
  15.3 0.5 collective-permute-start.11
  15.8 3.5 %collective-permute-done.3.refs_5_ = bf16[2,256,128]{2,1,0:T(8,128)(2,1)S(1)} collective-permute-done((bf16[2,256,128]{2,1,0:T(8,128)(2,1)S(1)}, bf16[2,256,128]{2,1,0:T(8,128)(2,1)S(1)}, u32[]{:S(2)}, u32[]{:S(2)}) %collective-permute-start.3) | collective-permute-done | bytes 131104 | tf_op jit(solution)/shard_map/ppermute | solution.py:259
  19.2 0.0 collective-permute-start.12
  19.2 0.9 %collective-permute-done.9.refs_3_ = bf16[2,256,128]{2,1,0:T(8,128)(2,1)S(1)} collective-permute-done((bf16[2,256,128]{2,1,0:T(8,128)(2,1)S(1)}, bf16[2,256,128]{2,1,0:T(8,128)(2,1)S(1)}, u32[]{:S(2)}, u32[]{:S(2)}) %collective-permute-start.9) | collective-permute-done | bytes 131104 | tf_op jit(solution)/shard_map/ppermute | solution.py:259
  20.1 0.0 collective-permute-start.13
  20.1 0.9 %collective-permute-done.10.refs_4_ = bf16[2,256,128]{2,1,0:T(8,128)(2,1)S(1)} collective-permute-done((bf16[2,256,128]{2,1,0:T(8,128)(2,1)S(1)}, bf16[2,256,128]{2,1,0:T(8,128)(2,1)S(1)}, u32[]{:S(2)}, u32[]{:S(2)}) %collective-permute-start.10) | collective-permute-done | bytes 131104 | tf_op jit(solution)/shard_map/ppermute | solution.py:259
  21.0 0.0 collective-permute-start.14
  21.0 1.4 %collective-permute-done.11.refs_5_ = bf16[2,256,128]{2,1,0:T(8,128)(2,1)S(1)} collective-permute-done((bf16[2,256,128]{2,1,0:T(8,128)(2,1)S(1)}, bf16[2,256,128]{2,1,0:T(8,128)(2,1)S(1)}, u32[]{:S(2)}, u32[]{:S(2)}) %collective-permute-start.11) | collective-permute-done | bytes 131104 | tf_op jit(solution)/shard_map/ppermute | solution.py:259
  22.5 0.0 collective-permute-start.15
  22.5 0.1 pad_maximum_fusion.1
  22.5 0.0 collective-permute-done.12.refs_6_
  22.6 1.7 %collective-permute-start = (bf16[2,2,5,64,128]{4,3,2,1,0:T(8,128)(2,1)S(1)}, bf16[2,2,5,64,128]{4,3,2,1,0:T(8,128)(2,1)S(1)}, u32[]{:S(2)}, u32[]{:S(2)}) collective-permute-start(bf16[2,2,5,64,128]{4,3,2,1,0:T(8,128)(2,1)S(1)} %get-tuple-element.27), channel_id=1, source_target_pairs={{0,1},{1,0},{2,3},{3,2},{4,5},{5,4},{6,7},{7,6},{8,9},{9,8},{10,11... | collective-permute-start | bytes 983048 | tf_op jit(solution)/shard_map/ppermute | solution.py:259
  24.2 0.0 collective-permute-done.7.refs_1_
  24.2 0.0 collective-permute-start.4
  24.2 0.0 collective-permute-done.13.refs_7_
  24.2 0.0 collective-permute-done.14.refs_8_
  24.2 0.0 collective-permute-done.15.refs_9_
  24.3 2.7 %attention_far.1 = (bf16[2,5,64,128]{3,2,1,0:T(8,128)(2,1)S(1)}, bf16[2,5,64,128]{3,2,1,0:T(8,128)(2,1)S(1)}, f32[4,2,256,128]{3,2,1,0:T(8,128)S(1)}, bf16[4,2,256,128]{3,2,1,0:T(8,128)(2,1)S(1)}) custom-call(s32[2048]{0:T(1024)S(1)} %copy-done, s32[16,128]{1,0:T(8,128)S(1)} %bitcast.76, bf16[2,2,5,64,128]{4,3,2,1,0:T(8,128)(2,1)S(1)} %get-tuple-element.29.refs_0_, ...), custom_call_target="tpu_custom_call" | custom-call | flops 3355443200 | bytes 4194304 | tf_op jit(solution)/shard_map/attention_far/pallas_call | solution.py:214
  27.0 0.1 convert.14
  27.2 2.5 %collective-permute-start.17 = (bf16[2,2,256,128]{3,2,1,0:T(8,128)(2,1)S(1)}, bf16[2,2,256,128]{3,2,1,0:T(8,128)(2,1)S(1)}, u32[]{:S(2)}, u32[]{:S(2)}) collective-permute-start(bf16[2,2,256,128]{3,2,1,0:T(8,128)(2,1)S(1)} %pad_maximum_fusion.2), channel_id=1, source_target_pairs={{0,8},{1,9},{2,10},{3,11},{4,12},{5,13},{6,14},{7,15},{8,0},{9,1},... | collective-permute-start | bytes 786440 | tf_op jit(solution)/shard_map/ppermute | solution.py:259
  29.7 2.7 %collective-permute-start.18 = (bf16[2,2,256,128]{3,2,1,0:T(8,128)(2,1)S(1)}, bf16[2,2,256,128]{3,2,1,0:T(8,128)(2,1)S(1)}, u32[]{:S(2)}, u32[]{:S(2)}) collective-permute-start(bf16[2,2,256,128]{3,2,1,0:T(8,128)(2,1)S(1)} %pad_maximum_fusion.3), channel_id=1, source_target_pairs={{0,16},{1,17},{2,18},{3,19},{4,20},{5,21},{6,22},{7,23},{8,24},{9,... | collective-permute-start | bytes 786440 | tf_op jit(solution)/shard_map/ppermute | solution.py:259
  32.4 1.5 %collective-permute-start.19 = (bf16[2,2,256,128]{3,2,1,0:T(8,128)(2,1)S(1)}, bf16[2,2,256,128]{3,2,1,0:T(8,128)(2,1)S(1)}, u32[]{:S(2)}, u32[]{:S(2)}) collective-permute-start(bf16[2,2,256,128]{3,2,1,0:T(8,128)(2,1)S(1)} %pad_maximum_fusion.4), channel_id=1, source_target_pairs={{0,24},{1,25},{2,26},{3,27},{4,28},{5,29},{6,30},{7,31},{8,16},{9,... | collective-permute-start | bytes 786440 | tf_op jit(solution)/shard_map/ppermute | solution.py:259
  33.9 0.0 collective-permute-done.refs_1_
  33.9 0.9 %collective-permute-start.16 = (bf16[2,5,64,128]{3,2,1,0:T(8,128)(2,1)S(1)}, bf16[2,5,64,128]{3,2,1,0:T(8,128)(2,1)S(1)}, u32[]{:S(2)}, u32[]{:S(2)}) collective-permute-start(bf16[2,5,64,128]{3,2,1,0:T(8,128)(2,1)S(1)} %get-tuple-element.20), channel_id=1, source_target_pairs={{0,1},{1,0},{2,3},{3,2},{4,5},{5,4},{6,7},{7,6},{8,9},{9,8},{10,11... | collective-permute-start | bytes 491528 | tf_op jit(solution)/shard_map/ppermute | solution.py:259
  34.8 0.0 collective-permute-done.4.refs_6_
  34.8 2.9 %attention_near.1 = (bf16[2,5,64,128]{3,2,1,0:T(8,128)(2,1)S(1)}, bf16[2,5,64,128]{3,2,1,0:T(8,128)(2,1)S(1)}, f32[4,2,256,128]{3,2,1,0:T(8,128)S(1)}, bf16[4,2,256,128]{3,2,1,0:T(8,128)(2,1)S(1)}) custom-call(s32[2048]{0:T(1024)S(1)} %copy-done, s32[16,128]{1,0:T(8,128)S(1)} %bitcast.77, bf16[2,2,5,64,128]{4,3,2,1,0:T(8,128)(2,1)S(1)} %get-tuple-element.28.refs_0_, ...), custom_call_target="tpu_custom_call" | custom-call | flops 3355443200 | bytes 4194304 | tf_op jit(solution)/shard_map/attention_near/pallas_call | solution.py:214
  37.7 1.3 %collective-permute-start.6 = (bf16[4,2,256,128]{3,2,1,0:T(8,128)(2,1)S(1)}, bf16[4,2,256,128]{3,2,1,0:T(8,128)(2,1)S(1)}, u32[]{:S(2)}, u32[]{:S(2)}) collective-permute-start(bf16[4,2,256,128]{3,2,1,0:T(8,128)(2,1)S(1)} %get-tuple-element.17), channel_id=1, source_target_pairs={{0,4},{1,5},{2,6},{3,7},{4,0},{5,1},{6,2},{7,3},{8,12},{9,13},{10,... | collective-permute-start | bytes 1572872 | tf_op jit(solution)/shard_map/ppermute | solution.py:259
  39.0 0.0 collective-permute-done.17
  39.1 5.3 %collective-permute-done.18 = bf16[2,2,256,128]{3,2,1,0:T(8,128)(2,1)S(1)} collective-permute-done((bf16[2,2,256,128]{3,2,1,0:T(8,128)(2,1)S(1)}, bf16[2,2,256,128]{3,2,1,0:T(8,128)(2,1)S(1)}, u32[]{:S(2)}, u32[]{:S(2)}) %collective-permute-start.18) | collective-permute-done | bytes 262176 | tf_op jit(solution)/shard_map/ppermute | solution.py:259
  44.4 1.8 %collective-permute-done.19 = bf16[2,2,256,128]{3,2,1,0:T(8,128)(2,1)S(1)} collective-permute-done((bf16[2,2,256,128]{3,2,1,0:T(8,128)(2,1)S(1)}, bf16[2,2,256,128]{3,2,1,0:T(8,128)(2,1)S(1)}, u32[]{:S(2)}, u32[]{:S(2)}) %collective-permute-start.19) | collective-permute-done | bytes 262176 | tf_op jit(solution)/shard_map/ppermute | solution.py:259
  46.2 0.1 fusion.17
  46.3 0.0 collective-permute-done.16
  46.3 0.2 collective-permute-start.23
  46.5 0.9 %collective-permute-start.5 = (bf16[2,5,64,128]{3,2,1,0:T(8,128)(2,1)S(1)}, bf16[2,5,64,128]{3,2,1,0:T(8,128)(2,1)S(1)}, u32[]{:S(2)}, u32[]{:S(2)}) collective-permute-start(bf16[2,5,64,128]{3,2,1,0:T(8,128)(2,1)S(1)} %get-tuple-element.15), channel_id=1, source_target_pairs={{0,1},{1,0},{2,3},{3,2},{4,5},{5,4},{6,7},{7,6},{8,9},{9,8},{10,11... | collective-permute-start | bytes 491528 | tf_op jit(solution)/shard_map/ppermute | solution.py:259
  47.4 0.3 collective-permute-done.23
  47.7 0.1 fusion.10
  47.8 2.3 %collective-permute-start.24 = (bf16[2,256,128]{2,1,0:T(8,128)(2,1)S(1)}, bf16[2,256,128]{2,1,0:T(8,128)(2,1)S(1)}, u32[]{:S(2)}, u32[]{:S(2)}) collective-permute-start(bf16[2,256,128]{2,1,0:T(8,128)(2,1)S(1)} %fusion.10), channel_id=1, source_target_pairs={{0,2},{1,3},{2,0},{3,1},{4,6},{5,7},{6,4},{7,5},{8,10},{9,11},{10,... | collective-permute-start | bytes 393224 | tf_op jit(solution)/shard_map/ppermute | solution.py:259
  50.1 0.0 collective-permute-done.6
  50.2 0.2 fusion.19
  50.4 0.8 %collective-permute-start.20 = (bf16[2,256,128]{2,1,0:T(8,128)(2,1)S(1)}, bf16[2,256,128]{2,1,0:T(8,128)(2,1)S(1)}, u32[]{:S(2)}, u32[]{:S(2)}) collective-permute-start(bf16[2,256,128]{2,1,0:T(8,128)(2,1)S(1)} %get-tuple-element.37), channel_id=1, source_target_pairs={{0,8},{1,9},{2,10},{3,11},{4,12},{5,13},{6,14},{7,15},{8,0},{9,1},... | collective-permute-start | bytes 393224 | tf_op jit(solution)/shard_map/ppermute | solution.py:259
  51.2 2.2 %collective-permute-start.21 = (bf16[2,256,128]{2,1,0:T(8,128)(2,1)S(1)}, bf16[2,256,128]{2,1,0:T(8,128)(2,1)S(1)}, u32[]{:S(2)}, u32[]{:S(2)}) collective-permute-start(bf16[2,256,128]{2,1,0:T(8,128)(2,1)S(1)} %get-tuple-element.35), channel_id=1, source_target_pairs={{0,16},{1,17},{2,18},{3,19},{4,20},{5,21},{6,22},{7,23},{8,24},{9,... | collective-permute-start | bytes 393224 | tf_op jit(solution)/shard_map/ppermute | solution.py:259
  53.4 0.5 collective-permute-start.22
  53.9 1.9 %collective-permute-done.5 = bf16[2,5,64,128]{3,2,1,0:T(8,128)(2,1)S(1)} collective-permute-done((bf16[2,5,64,128]{3,2,1,0:T(8,128)(2,1)S(1)}, bf16[2,5,64,128]{3,2,1,0:T(8,128)(2,1)S(1)}, u32[]{:S(2)}, u32[]{:S(2)}) %collective-permute-start.5) | collective-permute-done | bytes 163872 | tf_op jit(solution)/shard_map/ppermute | solution.py:259
  55.8 0.1 pad_maximum_fusion
  55.9 0.1 constant_dynamic-slice_fusion.3
  56.0 0.1 maximum_bitcast_fusion
  56.1 0.9 %copy.10 = bf16[2,64,4,5,128]{4,1,3,2,0:T(8,128)(2,1)} copy(bf16[2,64,4,5,128]{4,1,3,0,2:T(8,128)(2,1)S(1)} %maximum_bitcast_fusion) | data formatting | bytes 1310720 | tf_op jit(solution)/shard_map/transpose | solution.py:317
  56.9 2.5 %collective-permute-done.21 = bf16[2,256,128]{2,1,0:T(8,128)(2,1)S(1)} collective-permute-done((bf16[2,256,128]{2,1,0:T(8,128)(2,1)S(1)}, bf16[2,256,128]{2,1,0:T(8,128)(2,1)S(1)}, u32[]{:S(2)}, u32[]{:S(2)}) %collective-permute-start.21) | collective-permute-done | bytes 131104 | tf_op jit(solution)/shard_map/ppermute | solution.py:259
  59.4 0.0 collective-permute-done.22
  59.4 0.1 fusion.15
  59.5 0.7 %slice_bitcast_fusion.4 = (bf16[256,1,128]{2,0,1:T(8,128)(2,1)}, bf16[256,1,128]{2,0,1:T(8,128)(2,1)}) fusion(bf16[2,256,128]{2,1,0:T(8,128)(2,1)S(1)} %fusion.15), kind=kLoop, calls=%fused_computation.44 | loop fusion | bytes 262144 | tf_op jit(solution)/shard_map/squeeze | solution.py:319
  (12 shorter events, 0.3 us)
Async XLA Ops:
  1.5 10.8 %collective-permute-start.8 = (bf16[2,256,128]{2,1,0:T(8,128)(2,1)S(1)}, bf16[2,256,128]{2,1,0:T(8,128)(2,1)S(1)}, u32[]{:S(2)}, u32[]{:S(2)}) collective-permute-start(bf16[2,256,128]{2,1,0:T(8,128)(2,1)S(1)} %get-tuple-element.47.refs_2_), channel_id=1, source_target_pairs={{0,2},{1,3},{2,0},{3,1},{4,6},{5,7},{6,4},{7,5},{8,10},{9,11},{10,... | collective-permute-start | bytes 393224 | tf_op jit(solution)/shard_map/ppermute | solution.py:259
  5.6 8.2 %collective-permute-start.1 = (bf16[2,256,128]{2,1,0:T(8,128)(2,1)S(1)}, bf16[2,256,128]{2,1,0:T(8,128)(2,1)S(1)}, u32[]{:S(2)}, u32[]{:S(2)}) collective-permute-start(bf16[2,256,128]{2,1,0:T(8,128)(2,1)S(1)} %get-tuple-element.47.refs_2_), channel_id=1, source_target_pairs={{0,8},{1,9},{2,10},{3,11},{4,12},{5,13},{6,14},{7,15},{8,0},{9,1},... | collective-permute-start | bytes 393224 | tf_op jit(solution)/shard_map/ppermute | solution.py:259
  7.1 8.2 %collective-permute-start.2 = (bf16[2,256,128]{2,1,0:T(8,128)(2,1)S(1)}, bf16[2,256,128]{2,1,0:T(8,128)(2,1)S(1)}, u32[]{:S(2)}, u32[]{:S(2)}) collective-permute-start(bf16[2,256,128]{2,1,0:T(8,128)(2,1)S(1)} %get-tuple-element.47.refs_2_), channel_id=1, source_target_pairs={{0,16},{1,17},{2,18},{3,19},{4,20},{5,21},{6,22},{7,23},{8,24},{9,... | collective-permute-start | bytes 393224 | tf_op jit(solution)/shard_map/ppermute | solution.py:259
  10.1 14.1 %copy-start = (s32[2048]{0:T(1024)S(1)}, s32[2048]{0:T(1024)}, u32[]{:S(2)}) copy-start(s32[2048]{0:T(1024)} %doc_ref.3) | copy-start | bytes 24580
  10.2 14.1 %collective-permute-start.7 = (bf16[2,2,5,64,128]{4,3,2,1,0:T(8,128)(2,1)S(1)}, bf16[2,2,5,64,128]{4,3,2,1,0:T(8,128)(2,1)S(1)}, u32[]{:S(2)}, u32[]{:S(2)}) collective-permute-start(bf16[2,2,5,64,128]{4,3,2,1,0:T(8,128)(2,1)S(1)} %get-tuple-element.30), channel_id=1, source_target_pairs={{0,1},{1,0},{2,3},{3,2},{4,5},{5,4},{6,7},{7,6},{8,9},{9,8},{10,11... | collective-permute-start | bytes 983048 | tf_op jit(solution)/shard_map/ppermute | solution.py:259
  11.8 7.4 %collective-permute-start.3 = (bf16[2,256,128]{2,1,0:T(8,128)(2,1)S(1)}, bf16[2,256,128]{2,1,0:T(8,128)(2,1)S(1)}, u32[]{:S(2)}, u32[]{:S(2)}) collective-permute-start(bf16[2,256,128]{2,1,0:T(8,128)(2,1)S(1)} %get-tuple-element.47.refs_2_), channel_id=1, source_target_pairs={{0,24},{1,25},{2,26},{3,27},{4,28},{5,29},{6,30},{7,31},{8,16},{9,... | collective-permute-start | bytes 393224 | tf_op jit(solution)/shard_map/ppermute | solution.py:259
  12.3 7.8 %collective-permute-start.9 = (bf16[2,256,128]{2,1,0:T(8,128)(2,1)S(1)}, bf16[2,256,128]{2,1,0:T(8,128)(2,1)S(1)}, u32[]{:S(2)}, u32[]{:S(2)}) collective-permute-start(bf16[2,256,128]{2,1,0:T(8,128)(2,1)S(1)} %collective-permute-done.8.refs_2_), channel_id=1, source_target_pairs={{0,8},{1,9},{2,10},{3,11},{4,12},{5,13},{6,14},{7,15},{8,0},{9,1},... | collective-permute-start | bytes 393224 | tf_op jit(solution)/shard_map/ppermute | solution.py:259
  13.8 7.3 %collective-permute-start.10 = (bf16[2,256,128]{2,1,0:T(8,128)(2,1)S(1)}, bf16[2,256,128]{2,1,0:T(8,128)(2,1)S(1)}, u32[]{:S(2)}, u32[]{:S(2)}) collective-permute-start(bf16[2,256,128]{2,1,0:T(8,128)(2,1)S(1)} %collective-permute-done.8.refs_2_), channel_id=1, source_target_pairs={{0,16},{1,17},{2,18},{3,19},{4,20},{5,21},{6,22},{7,23},{8,24},{9,... | collective-permute-start | bytes 393224 | tf_op jit(solution)/shard_map/ppermute | solution.py:259
  15.3 7.2 %collective-permute-start.11 = (bf16[2,256,128]{2,1,0:T(8,128)(2,1)S(1)}, bf16[2,256,128]{2,1,0:T(8,128)(2,1)S(1)}, u32[]{:S(2)}, u32[]{:S(2)}) collective-permute-start(bf16[2,256,128]{2,1,0:T(8,128)(2,1)S(1)} %collective-permute-done.8.refs_2_), channel_id=1, source_target_pairs={{0,24},{1,25},{2,26},{3,27},{4,28},{5,29},{6,30},{7,31},{8,16},{9,... | collective-permute-start | bytes 393224 | tf_op jit(solution)/shard_map/ppermute | solution.py:259
  19.2 3.3 %collective-permute-start.12 = (bf16[2,256,128]{2,1,0:T(8,128)(2,1)S(1)}, bf16[2,256,128]{2,1,0:T(8,128)(2,1)S(1)}, u32[]{:S(2)}, u32[]{:S(2)}) collective-permute-start(bf16[2,256,128]{2,1,0:T(8,128)(2,1)S(1)} %collective-permute-done.8.refs_2_), channel_id=1, source_target_pairs={{0,4},{1,5},{2,6},{3,7},{4,0},{5,1},{6,2},{7,3},{8,12},{9,13},{10,... | collective-permute-start | bytes 393224 | tf_op jit(solution)/shard_map/ppermute | solution.py:259
  20.1 4.1 %collective-permute-start.13 = (bf16[2,256,128]{2,1,0:T(8,128)(2,1)S(1)}, bf16[2,256,128]{2,1,0:T(8,128)(2,1)S(1)}, u32[]{:S(2)}, u32[]{:S(2)}) collective-permute-start(bf16[2,256,128]{2,1,0:T(8,128)(2,1)S(1)} %collective-permute-done.9.refs_3_), channel_id=1, source_target_pairs={{0,4},{1,5},{2,6},{3,7},{4,0},{5,1},{6,2},{7,3},{8,12},{9,13},{10,... | collective-permute-start | bytes 393224 | tf_op jit(solution)/shard_map/ppermute | solution.py:259
  21.0 3.2 %collective-permute-start.14 = (bf16[2,256,128]{2,1,0:T(8,128)(2,1)S(1)}, bf16[2,256,128]{2,1,0:T(8,128)(2,1)S(1)}, u32[]{:S(2)}, u32[]{:S(2)}) collective-permute-start(bf16[2,256,128]{2,1,0:T(8,128)(2,1)S(1)} %collective-permute-done.10.refs_4_), channel_id=1, source_target_pairs={{0,4},{1,5},{2,6},{3,7},{4,0},{5,1},{6,2},{7,3},{8,12},{9,13},{10,... | collective-permute-start | bytes 393224 | tf_op jit(solution)/shard_map/ppermute | solution.py:259
  22.5 1.8 %collective-permute-start.15 = (bf16[2,256,128]{2,1,0:T(8,128)(2,1)S(1)}, bf16[2,256,128]{2,1,0:T(8,128)(2,1)S(1)}, u32[]{:S(2)}, u32[]{:S(2)}) collective-permute-start(bf16[2,256,128]{2,1,0:T(8,128)(2,1)S(1)} %collective-permute-done.11.refs_5_), channel_id=1, source_target_pairs={{0,4},{1,5},{2,6},{3,7},{4,0},{5,1},{6,2},{7,3},{8,12},{9,13},{10,... | collective-permute-start | bytes 393224 | tf_op jit(solution)/shard_map/ppermute | solution.py:259
  22.6 11.4 %collective-permute-start = (bf16[2,2,5,64,128]{4,3,2,1,0:T(8,128)(2,1)S(1)}, bf16[2,2,5,64,128]{4,3,2,1,0:T(8,128)(2,1)S(1)}, u32[]{:S(2)}, u32[]{:S(2)}) collective-permute-start(bf16[2,2,5,64,128]{4,3,2,1,0:T(8,128)(2,1)S(1)} %get-tuple-element.27), channel_id=1, source_target_pairs={{0,1},{1,0},{2,3},{3,2},{4,5},{5,4},{6,7},{7,6},{8,9},{9,8},{10,11... | collective-permute-start | bytes 983048 | tf_op jit(solution)/shard_map/ppermute | solution.py:259
  24.2 10.6 %collective-permute-start.4 = (bf16[4,2,256,128]{3,2,1,0:T(8,128)(2,1)S(1)}, bf16[4,2,256,128]{3,2,1,0:T(8,128)(2,1)S(1)}, u32[]{:S(2)}, u32[]{:S(2)}) collective-permute-start(bf16[4,2,256,128]{3,2,1,0:T(8,128)(2,1)S(1)} %pad_maximum_fusion.1), channel_id=1, source_target_pairs={{0,4},{1,5},{2,6},{3,7},{4,0},{5,1},{6,2},{7,3},{8,12},{9,13},{10,... | collective-permute-start | bytes 1572872 | tf_op jit(solution)/shard_map/ppermute | solution.py:259
  27.2 11.8 %collective-permute-start.17 = (bf16[2,2,256,128]{3,2,1,0:T(8,128)(2,1)S(1)}, bf16[2,2,256,128]{3,2,1,0:T(8,128)(2,1)S(1)}, u32[]{:S(2)}, u32[]{:S(2)}) collective-permute-start(bf16[2,2,256,128]{3,2,1,0:T(8,128)(2,1)S(1)} %pad_maximum_fusion.2), channel_id=1, source_target_pairs={{0,8},{1,9},{2,10},{3,11},{4,12},{5,13},{6,14},{7,15},{8,0},{9,1},... | collective-permute-start | bytes 786440 | tf_op jit(solution)/shard_map/ppermute | solution.py:259
  29.7 14.7 %collective-permute-start.18 = (bf16[2,2,256,128]{3,2,1,0:T(8,128)(2,1)S(1)}, bf16[2,2,256,128]{3,2,1,0:T(8,128)(2,1)S(1)}, u32[]{:S(2)}, u32[]{:S(2)}) collective-permute-start(bf16[2,2,256,128]{3,2,1,0:T(8,128)(2,1)S(1)} %pad_maximum_fusion.3), channel_id=1, source_target_pairs={{0,16},{1,17},{2,18},{3,19},{4,20},{5,21},{6,22},{7,23},{8,24},{9,... | collective-permute-start | bytes 786440 | tf_op jit(solution)/shard_map/ppermute | solution.py:259
  32.4 13.8 %collective-permute-start.19 = (bf16[2,2,256,128]{3,2,1,0:T(8,128)(2,1)S(1)}, bf16[2,2,256,128]{3,2,1,0:T(8,128)(2,1)S(1)}, u32[]{:S(2)}, u32[]{:S(2)}) collective-permute-start(bf16[2,2,256,128]{3,2,1,0:T(8,128)(2,1)S(1)} %pad_maximum_fusion.4), channel_id=1, source_target_pairs={{0,24},{1,25},{2,26},{3,27},{4,28},{5,29},{6,30},{7,31},{8,16},{9,... | collective-permute-start | bytes 786440 | tf_op jit(solution)/shard_map/ppermute | solution.py:259
  33.9 12.4 %collective-permute-start.16 = (bf16[2,5,64,128]{3,2,1,0:T(8,128)(2,1)S(1)}, bf16[2,5,64,128]{3,2,1,0:T(8,128)(2,1)S(1)}, u32[]{:S(2)}, u32[]{:S(2)}) collective-permute-start(bf16[2,5,64,128]{3,2,1,0:T(8,128)(2,1)S(1)} %get-tuple-element.20), channel_id=1, source_target_pairs={{0,1},{1,0},{2,3},{3,2},{4,5},{5,4},{6,7},{7,6},{8,9},{9,8},{10,11... | collective-permute-start | bytes 491528 | tf_op jit(solution)/shard_map/ppermute | solution.py:259
  37.7 12.4 %collective-permute-start.6 = (bf16[4,2,256,128]{3,2,1,0:T(8,128)(2,1)S(1)}, bf16[4,2,256,128]{3,2,1,0:T(8,128)(2,1)S(1)}, u32[]{:S(2)}, u32[]{:S(2)}) collective-permute-start(bf16[4,2,256,128]{3,2,1,0:T(8,128)(2,1)S(1)} %get-tuple-element.17), channel_id=1, source_target_pairs={{0,4},{1,5},{2,6},{3,7},{4,0},{5,1},{6,2},{7,3},{8,12},{9,13},{10,... | collective-permute-start | bytes 1572872 | tf_op jit(solution)/shard_map/ppermute | solution.py:259
  46.3 1.4 %collective-permute-start.23 = (bf16[2,256,128]{2,1,0:T(8,128)(2,1)S(1)}, bf16[2,256,128]{2,1,0:T(8,128)(2,1)S(1)}, u32[]{:S(2)}, u32[]{:S(2)}) collective-permute-start(bf16[2,256,128]{2,1,0:T(8,128)(2,1)S(1)} %fusion.17), channel_id=1, source_target_pairs={{0,4},{1,5},{2,6},{3,7},{4,0},{5,1},{6,2},{7,3},{8,12},{9,13},{10,... | collective-permute-start | bytes 393224 | tf_op jit(solution)/shard_map/ppermute | solution.py:259
  46.5 9.3 %collective-permute-start.5 = (bf16[2,5,64,128]{3,2,1,0:T(8,128)(2,1)S(1)}, bf16[2,5,64,128]{3,2,1,0:T(8,128)(2,1)S(1)}, u32[]{:S(2)}, u32[]{:S(2)}) collective-permute-start(bf16[2,5,64,128]{3,2,1,0:T(8,128)(2,1)S(1)} %get-tuple-element.15), channel_id=1, source_target_pairs={{0,1},{1,0},{2,3},{3,2},{4,5},{5,4},{6,7},{7,6},{8,9},{9,8},{10,11... | collective-permute-start | bytes 491528 | tf_op jit(solution)/shard_map/ppermute | solution.py:259
  47.8 9.1 %collective-permute-start.24 = (bf16[2,256,128]{2,1,0:T(8,128)(2,1)S(1)}, bf16[2,256,128]{2,1,0:T(8,128)(2,1)S(1)}, u32[]{:S(2)}, u32[]{:S(2)}) collective-permute-start(bf16[2,256,128]{2,1,0:T(8,128)(2,1)S(1)} %fusion.10), channel_id=1, source_target_pairs={{0,2},{1,3},{2,0},{3,1},{4,6},{5,7},{6,4},{7,5},{8,10},{9,11},{10,... | collective-permute-start | bytes 393224 | tf_op jit(solution)/shard_map/ppermute | solution.py:259
  50.4 6.6 %collective-permute-start.20 = (bf16[2,256,128]{2,1,0:T(8,128)(2,1)S(1)}, bf16[2,256,128]{2,1,0:T(8,128)(2,1)S(1)}, u32[]{:S(2)}, u32[]{:S(2)}) collective-permute-start(bf16[2,256,128]{2,1,0:T(8,128)(2,1)S(1)} %get-tuple-element.37), channel_id=1, source_target_pairs={{0,8},{1,9},{2,10},{3,11},{4,12},{5,13},{6,14},{7,15},{8,0},{9,1},... | collective-permute-start | bytes 393224 | tf_op jit(solution)/shard_map/ppermute | solution.py:259
  51.2 8.3 %collective-permute-start.21 = (bf16[2,256,128]{2,1,0:T(8,128)(2,1)S(1)}, bf16[2,256,128]{2,1,0:T(8,128)(2,1)S(1)}, u32[]{:S(2)}, u32[]{:S(2)}) collective-permute-start(bf16[2,256,128]{2,1,0:T(8,128)(2,1)S(1)} %get-tuple-element.35), channel_id=1, source_target_pairs={{0,16},{1,17},{2,18},{3,19},{4,20},{5,21},{6,22},{7,23},{8,24},{9,... | collective-permute-start | bytes 393224 | tf_op jit(solution)/shard_map/ppermute | solution.py:259
  53.4 6.1 %collective-permute-start.22 = (bf16[2,256,128]{2,1,0:T(8,128)(2,1)S(1)}, bf16[2,256,128]{2,1,0:T(8,128)(2,1)S(1)}, u32[]{:S(2)}, u32[]{:S(2)}) collective-permute-start(bf16[2,256,128]{2,1,0:T(8,128)(2,1)S(1)} %get-tuple-element.36), channel_id=1, source_target_pairs={{0,24},{1,25},{2,26},{3,27},{4,28},{5,29},{6,30},{7,31},{8,16},{9,... | collective-permute-start | bytes 393224 | tf_op jit(solution)/shard_map/ppermute | solution.py:259

commit v3 on v2

--- a/solution.py
+++ b/solution.py
@@ -69,13 +69,19 @@
             g_cols[:, n * pair : (n + 1) * pair] = g_rows[n].T
 
     def over_keys(step):
-        def two(i, _):
-            step(low + 2 * i, 2 * KEY_BLOCK)
+        count = high - low
+
+        def four(i, _):
+            step(low + 4 * i, 4 * KEY_BLOCK)
             return 0
 
-        lax.fori_loop(0, (high - low) // 2, two, 0)
-
-        @pl.when((high - low) % 2 == 1)
+        lax.fori_loop(0, count // 4, four, 0)
+
+        @pl.when(count % 4 >= 2)
+        def _():
+            step(low + count // 4 * 4, 2 * KEY_BLOCK)
+
+        @pl.when(count % 2 == 1)
         def _():
             step(high - 1, KEY_BLOCK)
 
@@ -273,8 +279,8 @@
     def piece(flip):
         return lax.dynamic_index_in_dim(both, z ^ flip, 0, keepdims=False)
 
+    far_chunks = (piece(2), swap(piece(3), 0, 1))
     near_chunks = (piece(0), swap(piece(1), 0, 1))
-    far_chunks = (piece(2), swap(piece(3), 0, 1))
 
     near_dq, near_dq_send, near_kept, near_sent = attention(
         "attention_near", doc_start, near_chunks, near, near_other

time: 59.2 us -> 57.9 us (0.978); the launches traced: 60.2 us -> 57.7 us
  starting transfers between devices: 30.2 us -> 28.7 us
  waiting for transfers between devices: 18.5 us -> 17.5 us
    ppermute x25, starting transfers between devices: 30.2 us -> 28.7 us  [swap(): return lax.ppermute(x, ('seq', 'head'), pairs)]
    ppermute x25, waiting for transfers between devices: 18.5 us -> 17.5 us  [swap(): return lax.ppermute(x, ('seq', 'head'), pairs)]
  transfers between devices with their start and end apart: 25 -> 25, of which waited for: 9 -> 9; matrix products, arithmetic and copies ran while one was open for 6% -> 6% of each run, Pallas kernels for 9% -> 10%
where the time goes in v3:
time: 57.9 us; the launch traced here: 57.7 us
  starting transfers between devices  28.7 us (50%)
  waiting for transfers between devices  17.5 us (30%)
  Pallas kernels  5.67 us (10%)
  other arithmetic  3.28 us (6%)
  local copies, waits for them, and re-layouts  1.69 us (3%)
  between operations  0.86 us (1%)
    ppermute x25, starting transfers between devices, swap(): return lax.ppermute(x, ('seq', 'head'), pairs)  28.7 us
    ppermute x25, waiting for transfers between devices, swap(): return lax.ppermute(x, ('seq', 'head'), pairs)  17.5 us
    pallas_call x2, Pallas kernels, attention(): pl.pallas_call(functools.partial(attention_kernel, column_count, group_la...  5.67 us
    squeeze x1, other arithmetic, piece(): return lax.dynamic_index_in_dim(both, z ^ flip, 0, keepdims=False)  1.51 us
  transfers between devices with their start and end apart: 25, of which 9 were waited for; matrix products, arithmetic and copies ran while one was open for 6% of the time, Pallas kernels for 10%

profile of v3, /device:TPU:0, one launch (start us, length us, event | category | flops | bytes accessed | tf_op | source)
XLA Modules:
  0.0 57.7 jit_solution(12997276020492681305)
XLA Ops:
  0.6 0.9 %fusion.18 = (bf16[1,2,256,128]{3,2,1,0:T(8,128)(2,1)S(1)}, bf16[2,256,128]{2,1,0:T(8,128)(2,1)S(1)}) fusion(bf16[1,256,128]{2,1,0:T(8,128)(2,1)} %bitcast.83, bf16[1,256,128]{2,1,0:T(8,128)(2,1)} %bitcast.84), kind=kLoop, calls=%fused_computation.50 | loop fusion | flops 65536 | bytes 393216 | tf_op jit(solution)/shard_map/stack | solution.py:273
  1.5 4.1 %collective-permute-start.8 = (bf16[2,256,128]{2,1,0:T(8,128)(2,1)S(1)}, bf16[2,256,128]{2,1,0:T(8,128)(2,1)S(1)}, u32[]{:S(2)}, u32[]{:S(2)}) collective-permute-start(bf16[2,256,128]{2,1,0:T(8,128)(2,1)S(1)} %get-tuple-element.47.refs_2_), channel_id=1, source_target_pairs={{0,2},{1,3},{2,0},{3,1},{4,6},{5,7},{6,4},{7,5},{8,10},{9,11},{10,... | collective-permute-start | bytes 393224 | tf_op jit(solution)/shard_map/ppermute | solution.py:265
  5.6 1.5 %collective-permute-start.1 = (bf16[2,256,128]{2,1,0:T(8,128)(2,1)S(1)}, bf16[2,256,128]{2,1,0:T(8,128)(2,1)S(1)}, u32[]{:S(2)}, u32[]{:S(2)}) collective-permute-start(bf16[2,256,128]{2,1,0:T(8,128)(2,1)S(1)} %get-tuple-element.47.refs_2_), channel_id=1, source_target_pairs={{0,8},{1,9},{2,10},{3,11},{4,12},{5,13},{6,14},{7,15},{8,0},{9,1},... | collective-permute-start | bytes 393224 | tf_op jit(solution)/shard_map/ppermute | solution.py:265
  7.1 1.5 %collective-permute-start.2 = (bf16[2,256,128]{2,1,0:T(8,128)(2,1)S(1)}, bf16[2,256,128]{2,1,0:T(8,128)(2,1)S(1)}, u32[]{:S(2)}, u32[]{:S(2)}) collective-permute-start(bf16[2,256,128]{2,1,0:T(8,128)(2,1)S(1)} %get-tuple-element.47.refs_2_), channel_id=1, source_target_pairs={{0,16},{1,17},{2,18},{3,19},{4,20},{5,21},{6,22},{7,23},{8,24},{9,... | collective-permute-start | bytes 393224 | tf_op jit(solution)/shard_map/ppermute | solution.py:265
  8.6 1.5 %fusion.5 = (bf16[2,2,5,64,128]{4,3,2,1,0:T(8,128)(2,1)S(1)}, bf16[2,2,5,64,128]{4,3,2,1,0:T(8,128)(2,1)S(1)}, bf16[2,2,5,64,128]{4,3,2,1,0:T(8,128)(2,1)S(1)}, bf16[2,2,5,64,128]{4,3,2,1,0:T(8,128)(2,1)S(1)}) fusion(s32[]{:T(128)S(6)} %select_n.19, bf16[1,2,64,4,5,128]{5,2,4,3,1,0:T(8,128)(2,1)} %bitcast.79, bf16[1,2,64,4,5,128]{5,2,4,3,1,0:T(8,128)(2,1)} %bitcast.80, ...), kind=kLoop, calls=%fused_computation.17 | loop fusion | flops 655360 | bytes 2621456 | tf_op jit(solution)/shard_map/jit(dynamic_index_in_dim)/squeeze | solution.py:280
  10.1 0.0 copy-start
  10.2 1.6 %collective-permute-start.7 = (bf16[2,2,5,64,128]{4,3,2,1,0:T(8,128)(2,1)S(1)}, bf16[2,2,5,64,128]{4,3,2,1,0:T(8,128)(2,1)S(1)}, u32[]{:S(2)}, u32[]{:S(2)}) collective-permute-start(bf16[2,2,5,64,128]{4,3,2,1,0:T(8,128)(2,1)S(1)} %get-tuple-element.30), channel_id=1, source_target_pairs={{0,1},{1,0},{2,3},{3,2},{4,5},{5,4},{6,7},{7,6},{8,9},{9,8},{10,11... | collective-permute-start | bytes 983048 | tf_op jit(solution)/shard_map/ppermute | solution.py:265
  11.8 0.5 collective-permute-start.3
  12.3 0.0 collective-permute-done.8.refs_2_
  12.3 1.5 %collective-permute-start.9 = (bf16[2,256,128]{2,1,0:T(8,128)(2,1)S(1)}, bf16[2,256,128]{2,1,0:T(8,128)(2,1)S(1)}, u32[]{:S(2)}, u32[]{:S(2)}) collective-permute-start(bf16[2,256,128]{2,1,0:T(8,128)(2,1)S(1)} %collective-permute-done.8.refs_2_), channel_id=1, source_target_pairs={{0,8},{1,9},{2,10},{3,11},{4,12},{5,13},{6,14},{7,15},{8,0},{9,1},... | collective-permute-start | bytes 393224 | tf_op jit(solution)/shard_map/ppermute | solution.py:265
  13.8 0.0 collective-permute-done.1.refs_3_
  13.8 1.5 %collective-permute-start.10 = (bf16[2,256,128]{2,1,0:T(8,128)(2,1)S(1)}, bf16[2,256,128]{2,1,0:T(8,128)(2,1)S(1)}, u32[]{:S(2)}, u32[]{:S(2)}) collective-permute-start(bf16[2,256,128]{2,1,0:T(8,128)(2,1)S(1)} %collective-permute-done.8.refs_2_), channel_id=1, source_target_pairs={{0,16},{1,17},{2,18},{3,19},{4,20},{5,21},{6,22},{7,23},{8,24},{9,... | collective-permute-start | bytes 393224 | tf_op jit(solution)/shard_map/ppermute | solution.py:265
  15.3 0.0 collective-permute-done.2.refs_4_
  15.3 0.5 collective-permute-start.11
  15.8 3.5 %collective-permute-done.3.refs_5_ = bf16[2,256,128]{2,1,0:T(8,128)(2,1)S(1)} collective-permute-done((bf16[2,256,128]{2,1,0:T(8,128)(2,1)S(1)}, bf16[2,256,128]{2,1,0:T(8,128)(2,1)S(1)}, u32[]{:S(2)}, u32[]{:S(2)}) %collective-permute-start.3) | collective-permute-done | bytes 131104 | tf_op jit(solution)/shard_map/ppermute | solution.py:265
  19.2 0.0 collective-permute-start.12
  19.2 0.9 %collective-permute-done.9.refs_3_ = bf16[2,256,128]{2,1,0:T(8,128)(2,1)S(1)} collective-permute-done((bf16[2,256,128]{2,1,0:T(8,128)(2,1)S(1)}, bf16[2,256,128]{2,1,0:T(8,128)(2,1)S(1)}, u32[]{:S(2)}, u32[]{:S(2)}) %collective-permute-start.9) | collective-permute-done | bytes 131104 | tf_op jit(solution)/shard_map/ppermute | solution.py:265
  20.1 0.0 collective-permute-start.13
  20.1 0.9 %collective-permute-done.10.refs_4_ = bf16[2,256,128]{2,1,0:T(8,128)(2,1)S(1)} collective-permute-done((bf16[2,256,128]{2,1,0:T(8,128)(2,1)S(1)}, bf16[2,256,128]{2,1,0:T(8,128)(2,1)S(1)}, u32[]{:S(2)}, u32[]{:S(2)}) %collective-permute-start.10) | collective-permute-done | bytes 131104 | tf_op jit(solution)/shard_map/ppermute | solution.py:265
  21.0 0.0 collective-permute-start.14
  21.0 1.4 %collective-permute-done.11.refs_5_ = bf16[2,256,128]{2,1,0:T(8,128)(2,1)S(1)} collective-permute-done((bf16[2,256,128]{2,1,0:T(8,128)(2,1)S(1)}, bf16[2,256,128]{2,1,0:T(8,128)(2,1)S(1)}, u32[]{:S(2)}, u32[]{:S(2)}) %collective-permute-start.11) | collective-permute-done | bytes 131104 | tf_op jit(solution)/shard_map/ppermute | solution.py:265
  22.5 0.0 collective-permute-start.15
  22.5 0.1 pad_maximum_fusion.1
  22.5 0.0 collective-permute-done.12.refs_6_
  22.6 1.7 %collective-permute-start = (bf16[2,2,5,64,128]{4,3,2,1,0:T(8,128)(2,1)S(1)}, bf16[2,2,5,64,128]{4,3,2,1,0:T(8,128)(2,1)S(1)}, u32[]{:S(2)}, u32[]{:S(2)}) collective-permute-start(bf16[2,2,5,64,128]{4,3,2,1,0:T(8,128)(2,1)S(1)} %get-tuple-element.27), channel_id=1, source_target_pairs={{0,1},{1,0},{2,3},{3,2},{4,5},{5,4},{6,7},{7,6},{8,9},{9,8},{10,11... | collective-permute-start | bytes 983048 | tf_op jit(solution)/shard_map/ppermute | solution.py:265
  24.2 0.0 collective-permute-done.7.refs_1_
  24.2 0.0 collective-permute-start.4
  24.2 0.0 collective-permute-done.13.refs_7_
  24.2 0.0 collective-permute-done.14.refs_8_
  24.2 0.0 collective-permute-done.15.refs_9_
  24.3 2.9 %attention_far.1 = (bf16[2,5,64,128]{3,2,1,0:T(8,128)(2,1)S(1)}, bf16[2,5,64,128]{3,2,1,0:T(8,128)(2,1)S(1)}, f32[4,2,256,128]{3,2,1,0:T(8,128)S(1)}, bf16[4,2,256,128]{3,2,1,0:T(8,128)(2,1)S(1)}) custom-call(s32[2048]{0:T(1024)S(1)} %copy-done, s32[16,128]{1,0:T(8,128)S(1)} %bitcast.76, bf16[2,2,5,64,128]{4,3,2,1,0:T(8,128)(2,1)S(1)} %get-tuple-element.29.refs_0_, ...), custom_call_target="tpu_custom_call" | custom-call | flops 3355443200 | bytes 4194304 | tf_op jit(solution)/shard_map/attention_far/pallas_call | solution.py:220
  27.2 0.1 convert.14
  27.4 2.5 %collective-permute-start.17 = (bf16[2,2,256,128]{3,2,1,0:T(8,128)(2,1)S(1)}, bf16[2,2,256,128]{3,2,1,0:T(8,128)(2,1)S(1)}, u32[]{:S(2)}, u32[]{:S(2)}) collective-permute-start(bf16[2,2,256,128]{3,2,1,0:T(8,128)(2,1)S(1)} %pad_maximum_fusion.2), channel_id=1, source_target_pairs={{0,8},{1,9},{2,10},{3,11},{4,12},{5,13},{6,14},{7,15},{8,0},{9,1},... | collective-permute-start | bytes 786440 | tf_op jit(solution)/shard_map/ppermute | solution.py:265
  29.9 2.3 %collective-permute-start.18 = (bf16[2,2,256,128]{3,2,1,0:T(8,128)(2,1)S(1)}, bf16[2,2,256,128]{3,2,1,0:T(8,128)(2,1)S(1)}, u32[]{:S(2)}, u32[]{:S(2)}) collective-permute-start(bf16[2,2,256,128]{3,2,1,0:T(8,128)(2,1)S(1)} %pad_maximum_fusion.3), channel_id=1, source_target_pairs={{0,16},{1,17},{2,18},{3,19},{4,20},{5,21},{6,22},{7,23},{8,24},{9,... | collective-permute-start | bytes 786440 | tf_op jit(solution)/shard_map/ppermute | solution.py:265
  32.2 1.5 %collective-permute-start.19 = (bf16[2,2,256,128]{3,2,1,0:T(8,128)(2,1)S(1)}, bf16[2,2,256,128]{3,2,1,0:T(8,128)(2,1)S(1)}, u32[]{:S(2)}, u32[]{:S(2)}) collective-permute-start(bf16[2,2,256,128]{3,2,1,0:T(8,128)(2,1)S(1)} %pad_maximum_fusion.4), channel_id=1, source_target_pairs={{0,24},{1,25},{2,26},{3,27},{4,28},{5,29},{6,30},{7,31},{8,16},{9,... | collective-permute-start | bytes 786440 | tf_op jit(solution)/shard_map/ppermute | solution.py:265
  33.8 0.0 collective-permute-done.refs_1_
  33.8 0.9 %collective-permute-start.16 = (bf16[2,5,64,128]{3,2,1,0:T(8,128)(2,1)S(1)}, bf16[2,5,64,128]{3,2,1,0:T(8,128)(2,1)S(1)}, u32[]{:S(2)}, u32[]{:S(2)}) collective-permute-start(bf16[2,5,64,128]{3,2,1,0:T(8,128)(2,1)S(1)} %get-tuple-element.20), channel_id=1, source_target_pairs={{0,1},{1,0},{2,3},{3,2},{4,5},{5,4},{6,7},{7,6},{8,9},{9,8},{10,11... | collective-permute-start | bytes 491528 | tf_op jit(solution)/shard_map/ppermute | solution.py:265
  34.6 0.0 collective-permute-done.4.refs_6_
  34.6 2.7 %attention_near.1 = (bf16[2,5,64,128]{3,2,1,0:T(8,128)(2,1)S(1)}, bf16[2,5,64,128]{3,2,1,0:T(8,128)(2,1)S(1)}, f32[4,2,256,128]{3,2,1,0:T(8,128)S(1)}, bf16[4,2,256,128]{3,2,1,0:T(8,128)(2,1)S(1)}) custom-call(s32[2048]{0:T(1024)S(1)} %copy-done, s32[16,128]{1,0:T(8,128)S(1)} %bitcast.77, bf16[2,2,5,64,128]{4,3,2,1,0:T(8,128)(2,1)S(1)} %get-tuple-element.28.refs_0_, ...), custom_call_target="tpu_custom_call" | custom-call | flops 3355443200 | bytes 4194304 | tf_op jit(solution)/shard_map/attention_near/pallas_call | solution.py:220
  37.4 0.1 collective-permute-start.6
  37.5 0.0 collective-permute-done.17
  37.5 6.8 %collective-permute-done.18 = bf16[2,2,256,128]{3,2,1,0:T(8,128)(2,1)S(1)} collective-permute-done((bf16[2,2,256,128]{3,2,1,0:T(8,128)(2,1)S(1)}, bf16[2,2,256,128]{3,2,1,0:T(8,128)(2,1)S(1)}, u32[]{:S(2)}, u32[]{:S(2)}) %collective-permute-start.18) | collective-permute-done | bytes 262176 | tf_op jit(solution)/shard_map/ppermute | solution.py:265
  44.4 0.0 collective-permute-done.19
  44.4 0.1 fusion.17
  44.5 0.1 collective-permute-start.23
  44.6 0.9 %collective-permute-start.5 = (bf16[2,5,64,128]{3,2,1,0:T(8,128)(2,1)S(1)}, bf16[2,5,64,128]{3,2,1,0:T(8,128)(2,1)S(1)}, u32[]{:S(2)}, u32[]{:S(2)}) collective-permute-start(bf16[2,5,64,128]{3,2,1,0:T(8,128)(2,1)S(1)} %get-tuple-element.15), channel_id=1, source_target_pairs={{0,1},{1,0},{2,3},{3,2},{4,5},{5,4},{6,7},{7,6},{8,9},{9,8},{10,11... | collective-permute-start | bytes 491528 | tf_op jit(solution)/shard_map/ppermute | solution.py:265
  45.5 0.4 collective-permute-done.23
  45.9 0.1 fusion.10
  46.0 2.6 %collective-permute-start.24 = (bf16[2,256,128]{2,1,0:T(8,128)(2,1)S(1)}, bf16[2,256,128]{2,1,0:T(8,128)(2,1)S(1)}, u32[]{:S(2)}, u32[]{:S(2)}) collective-permute-start(bf16[2,256,128]{2,1,0:T(8,128)(2,1)S(1)} %fusion.10), channel_id=1, source_target_pairs={{0,2},{1,3},{2,0},{3,1},{4,6},{5,7},{6,4},{7,5},{8,10},{9,11},{10,... | collective-permute-start | bytes 393224 | tf_op jit(solution)/shard_map/ppermute | solution.py:265
  48.5 0.2 fusion.19
  48.7 0.4 collective-permute-start.20
  49.1 1.7 %collective-permute-start.21 = (bf16[2,256,128]{2,1,0:T(8,128)(2,1)S(1)}, bf16[2,256,128]{2,1,0:T(8,128)(2,1)S(1)}, u32[]{:S(2)}, u32[]{:S(2)}) collective-permute-start(bf16[2,256,128]{2,1,0:T(8,128)(2,1)S(1)} %get-tuple-element.35), channel_id=1, source_target_pairs={{0,16},{1,17},{2,18},{3,19},{4,20},{5,21},{6,22},{7,23},{8,24},{9,... | collective-permute-start | bytes 393224 | tf_op jit(solution)/shard_map/ppermute | solution.py:265
  50.8 1.5 %collective-permute-start.22 = (bf16[2,256,128]{2,1,0:T(8,128)(2,1)S(1)}, bf16[2,256,128]{2,1,0:T(8,128)(2,1)S(1)}, u32[]{:S(2)}, u32[]{:S(2)}) collective-permute-start(bf16[2,256,128]{2,1,0:T(8,128)(2,1)S(1)} %get-tuple-element.36), channel_id=1, source_target_pairs={{0,24},{1,25},{2,26},{3,27},{4,28},{5,29},{6,30},{7,31},{8,16},{9,... | collective-permute-start | bytes 393224 | tf_op jit(solution)/shard_map/ppermute | solution.py:265
  52.3 1.7 %collective-permute-done.5 = bf16[2,5,64,128]{3,2,1,0:T(8,128)(2,1)S(1)} collective-permute-done((bf16[2,5,64,128]{3,2,1,0:T(8,128)(2,1)S(1)}, bf16[2,5,64,128]{3,2,1,0:T(8,128)(2,1)S(1)}, u32[]{:S(2)}, u32[]{:S(2)}) %collective-permute-start.5) | collective-permute-done | bytes 163872 | tf_op jit(solution)/shard_map/ppermute | solution.py:265
  54.0 0.1 pad_maximum_fusion
  54.1 0.1 constant_dynamic-slice_fusion.3
  54.1 0.1 maximum_bitcast_fusion
  54.2 0.9 %copy.10 = bf16[2,64,4,5,128]{4,1,3,2,0:T(8,128)(2,1)} copy(bf16[2,64,4,5,128]{4,1,3,0,2:T(8,128)(2,1)S(1)} %maximum_bitcast_fusion) | data formatting | bytes 1310720 | tf_op jit(solution)/shard_map/transpose | solution.py:323
  55.1 0.0 collective-permute-done.24
  55.1 0.1 collective-permute-done.20
  55.2 1.8 %collective-permute-done.21 = bf16[2,256,128]{2,1,0:T(8,128)(2,1)S(1)} collective-permute-done((bf16[2,256,128]{2,1,0:T(8,128)(2,1)S(1)}, bf16[2,256,128]{2,1,0:T(8,128)(2,1)S(1)}, u32[]{:S(2)}, u32[]{:S(2)}) %collective-permute-start.21) | collective-permute-done | bytes 131104 | tf_op jit(solution)/shard_map/ppermute | solution.py:265
  57.0 0.0 collective-permute-done.22
  57.0 0.1 fusion.15
  57.1 0.7 %slice_bitcast_fusion.4 = (bf16[256,1,128]{2,0,1:T(8,128)(2,1)}, bf16[256,1,128]{2,0,1:T(8,128)(2,1)}) fusion(bf16[2,256,128]{2,1,0:T(8,128)(2,1)S(1)} %fusion.15), kind=kLoop, calls=%fused_computation.44 | loop fusion | bytes 262144 | tf_op jit(solution)/shard_map/squeeze | solution.py:325
  (12 shorter events, 0.3 us)
Async XLA Ops:
  1.5 10.8 %collective-permute-start.8 = (bf16[2,256,128]{2,1,0:T(8,128)(2,1)S(1)}, bf16[2,256,128]{2,1,0:T(8,128)(2,1)S(1)}, u32[]{:S(2)}, u32[]{:S(2)}) collective-permute-start(bf16[2,256,128]{2,1,0:T(8,128)(2,1)S(1)} %get-tuple-element.47.refs_2_), channel_id=1, source_target_pairs={{0,2},{1,3},{2,0},{3,1},{4,6},{5,7},{6,4},{7,5},{8,10},{9,11},{10,... | collective-permute-start | bytes 393224 | tf_op jit(solution)/shard_map/ppermute | solution.py:265
  5.6 8.2 %collective-permute-start.1 = (bf16[2,256,128]{2,1,0:T(8,128)(2,1)S(1)}, bf16[2,256,128]{2,1,0:T(8,128)(2,1)S(1)}, u32[]{:S(2)}, u32[]{:S(2)}) collective-permute-start(bf16[2,256,128]{2,1,0:T(8,128)(2,1)S(1)} %get-tuple-element.47.refs_2_), channel_id=1, source_target_pairs={{0,8},{1,9},{2,10},{3,11},{4,12},{5,13},{6,14},{7,15},{8,0},{9,1},... | collective-permute-start | bytes 393224 | tf_op jit(solution)/shard_map/ppermute | solution.py:265
  7.1 8.2 %collective-permute-start.2 = (bf16[2,256,128]{2,1,0:T(8,128)(2,1)S(1)}, bf16[2,256,128]{2,1,0:T(8,128)(2,1)S(1)}, u32[]{:S(2)}, u32[]{:S(2)}) collective-permute-start(bf16[2,256,128]{2,1,0:T(8,128)(2,1)S(1)} %get-tuple-element.47.refs_2_), channel_id=1, source_target_pairs={{0,16},{1,17},{2,18},{3,19},{4,20},{5,21},{6,22},{7,23},{8,24},{9,... | collective-permute-start | bytes 393224 | tf_op jit(solution)/shard_map/ppermute | solution.py:265
  10.1 14.1 %copy-start = (s32[2048]{0:T(1024)S(1)}, s32[2048]{0:T(1024)}, u32[]{:S(2)}) copy-start(s32[2048]{0:T(1024)} %doc_ref.3) | copy-start | bytes 24580
  10.2 14.1 %collective-permute-start.7 = (bf16[2,2,5,64,128]{4,3,2,1,0:T(8,128)(2,1)S(1)}, bf16[2,2,5,64,128]{4,3,2,1,0:T(8,128)(2,1)S(1)}, u32[]{:S(2)}, u32[]{:S(2)}) collective-permute-start(bf16[2,2,5,64,128]{4,3,2,1,0:T(8,128)(2,1)S(1)} %get-tuple-element.30), channel_id=1, source_target_pairs={{0,1},{1,0},{2,3},{3,2},{4,5},{5,4},{6,7},{7,6},{8,9},{9,8},{10,11... | collective-permute-start | bytes 983048 | tf_op jit(solution)/shard_map/ppermute | solution.py:265
  11.8 7.4 %collective-permute-start.3 = (bf16[2,256,128]{2,1,0:T(8,128)(2,1)S(1)}, bf16[2,256,128]{2,1,0:T(8,128)(2,1)S(1)}, u32[]{:S(2)}, u32[]{:S(2)}) collective-permute-start(bf16[2,256,128]{2,1,0:T(8,128)(2,1)S(1)} %get-tuple-element.47.refs_2_), channel_id=1, source_target_pairs={{0,24},{1,25},{2,26},{3,27},{4,28},{5,29},{6,30},{7,31},{8,16},{9,... | collective-permute-start | bytes 393224 | tf_op jit(solution)/shard_map/ppermute | solution.py:265
  12.3 7.8 %collective-permute-start.9 = (bf16[2,256,128]{2,1,0:T(8,128)(2,1)S(1)}, bf16[2,256,128]{2,1,0:T(8,128)(2,1)S(1)}, u32[]{:S(2)}, u32[]{:S(2)}) collective-permute-start(bf16[2,256,128]{2,1,0:T(8,128)(2,1)S(1)} %collective-permute-done.8.refs_2_), channel_id=1, source_target_pairs={{0,8},{1,9},{2,10},{3,11},{4,12},{5,13},{6,14},{7,15},{8,0},{9,1},... | collective-permute-start | bytes 393224 | tf_op jit(solution)/shard_map/ppermute | solution.py:265
  13.8 7.3 %collective-permute-start.10 = (bf16[2,256,128]{2,1,0:T(8,128)(2,1)S(1)}, bf16[2,256,128]{2,1,0:T(8,128)(2,1)S(1)}, u32[]{:S(2)}, u32[]{:S(2)}) collective-permute-start(bf16[2,256,128]{2,1,0:T(8,128)(2,1)S(1)} %collective-permute-done.8.refs_2_), channel_id=1, source_target_pairs={{0,16},{1,17},{2,18},{3,19},{4,20},{5,21},{6,22},{7,23},{8,24},{9,... | collective-permute-start | bytes 393224 | tf_op jit(solution)/shard_map/ppermute | solution.py:265
  15.3 7.2 %collective-permute-start.11 = (bf16[2,256,128]{2,1,0:T(8,128)(2,1)S(1)}, bf16[2,256,128]{2,1,0:T(8,128)(2,1)S(1)}, u32[]{:S(2)}, u32[]{:S(2)}) collective-permute-start(bf16[2,256,128]{2,1,0:T(8,128)(2,1)S(1)} %collective-permute-done.8.refs_2_), channel_id=1, source_target_pairs={{0,24},{1,25},{2,26},{3,27},{4,28},{5,29},{6,30},{7,31},{8,16},{9,... | collective-permute-start | bytes 393224 | tf_op jit(solution)/shard_map/ppermute | solution.py:265
  19.2 3.3 %collective-permute-start.12 = (bf16[2,256,128]{2,1,0:T(8,128)(2,1)S(1)}, bf16[2,256,128]{2,1,0:T(8,128)(2,1)S(1)}, u32[]{:S(2)}, u32[]{:S(2)}) collective-permute-start(bf16[2,256,128]{2,1,0:T(8,128)(2,1)S(1)} %collective-permute-done.8.refs_2_), channel_id=1, source_target_pairs={{0,4},{1,5},{2,6},{3,7},{4,0},{5,1},{6,2},{7,3},{8,12},{9,13},{10,... | collective-permute-start | bytes 393224 | tf_op jit(solution)/shard_map/ppermute | solution.py:265
  20.1 4.1 %collective-permute-start.13 = (bf16[2,256,128]{2,1,0:T(8,128)(2,1)S(1)}, bf16[2,256,128]{2,1,0:T(8,128)(2,1)S(1)}, u32[]{:S(2)}, u32[]{:S(2)}) collective-permute-start(bf16[2,256,128]{2,1,0:T(8,128)(2,1)S(1)} %collective-permute-done.9.refs_3_), channel_id=1, source_target_pairs={{0,4},{1,5},{2,6},{3,7},{4,0},{5,1},{6,2},{7,3},{8,12},{9,13},{10,... | collective-permute-start | bytes 393224 | tf_op jit(solution)/shard_map/ppermute | solution.py:265
  21.0 3.2 %collective-permute-start.14 = (bf16[2,256,128]{2,1,0:T(8,128)(2,1)S(1)}, bf16[2,256,128]{2,1,0:T(8,128)(2,1)S(1)}, u32[]{:S(2)}, u32[]{:S(2)}) collective-permute-start(bf16[2,256,128]{2,1,0:T(8,128)(2,1)S(1)} %collective-permute-done.10.refs_4_), channel_id=1, source_target_pairs={{0,4},{1,5},{2,6},{3,7},{4,0},{5,1},{6,2},{7,3},{8,12},{9,13},{10,... | collective-permute-start | bytes 393224 | tf_op jit(solution)/shard_map/ppermute | solution.py:265
  22.5 1.8 %collective-permute-start.15 = (bf16[2,256,128]{2,1,0:T(8,128)(2,1)S(1)}, bf16[2,256,128]{2,1,0:T(8,128)(2,1)S(1)}, u32[]{:S(2)}, u32[]{:S(2)}) collective-permute-start(bf16[2,256,128]{2,1,0:T(8,128)(2,1)S(1)} %collective-permute-done.11.refs_5_), channel_id=1, source_target_pairs={{0,4},{1,5},{2,6},{3,7},{4,0},{5,1},{6,2},{7,3},{8,12},{9,13},{10,... | collective-permute-start | bytes 393224 | tf_op jit(solution)/shard_map/ppermute | solution.py:265
  22.6 11.2 %collective-permute-start = (bf16[2,2,5,64,128]{4,3,2,1,0:T(8,128)(2,1)S(1)}, bf16[2,2,5,64,128]{4,3,2,1,0:T(8,128)(2,1)S(1)}, u32[]{:S(2)}, u32[]{:S(2)}) collective-permute-start(bf16[2,2,5,64,128]{4,3,2,1,0:T(8,128)(2,1)S(1)} %get-tuple-element.27), channel_id=1, source_target_pairs={{0,1},{1,0},{2,3},{3,2},{4,5},{5,4},{6,7},{7,6},{8,9},{9,8},{10,11... | collective-permute-start | bytes 983048 | tf_op jit(solution)/shard_map/ppermute | solution.py:265
  24.2 10.4 %collective-permute-start.4 = (bf16[4,2,256,128]{3,2,1,0:T(8,128)(2,1)S(1)}, bf16[4,2,256,128]{3,2,1,0:T(8,128)(2,1)S(1)}, u32[]{:S(2)}, u32[]{:S(2)}) collective-permute-start(bf16[4,2,256,128]{3,2,1,0:T(8,128)(2,1)S(1)} %pad_maximum_fusion.1), channel_id=1, source_target_pairs={{0,4},{1,5},{2,6},{3,7},{4,0},{5,1},{6,2},{7,3},{8,12},{9,13},{10,... | collective-permute-start | bytes 1572872 | tf_op jit(solution)/shard_map/ppermute | solution.py:265
  27.4 10.1 %collective-permute-start.17 = (bf16[2,2,256,128]{3,2,1,0:T(8,128)(2,1)S(1)}, bf16[2,2,256,128]{3,2,1,0:T(8,128)(2,1)S(1)}, u32[]{:S(2)}, u32[]{:S(2)}) collective-permute-start(bf16[2,2,256,128]{3,2,1,0:T(8,128)(2,1)S(1)} %pad_maximum_fusion.2), channel_id=1, source_target_pairs={{0,8},{1,9},{2,10},{3,11},{4,12},{5,13},{6,14},{7,15},{8,0},{9,1},... | collective-permute-start | bytes 786440 | tf_op jit(solution)/shard_map/ppermute | solution.py:265
  29.9 14.4 %collective-permute-start.18 = (bf16[2,2,256,128]{3,2,1,0:T(8,128)(2,1)S(1)}, bf16[2,2,256,128]{3,2,1,0:T(8,128)(2,1)S(1)}, u32[]{:S(2)}, u32[]{:S(2)}) collective-permute-start(bf16[2,2,256,128]{3,2,1,0:T(8,128)(2,1)S(1)} %pad_maximum_fusion.3), channel_id=1, source_target_pairs={{0,16},{1,17},{2,18},{3,19},{4,20},{5,21},{6,22},{7,23},{8,24},{9,... | collective-permute-start | bytes 786440 | tf_op jit(solution)/shard_map/ppermute | solution.py:265
  32.2 12.1 %collective-permute-start.19 = (bf16[2,2,256,128]{3,2,1,0:T(8,128)(2,1)S(1)}, bf16[2,2,256,128]{3,2,1,0:T(8,128)(2,1)S(1)}, u32[]{:S(2)}, u32[]{:S(2)}) collective-permute-start(bf16[2,2,256,128]{3,2,1,0:T(8,128)(2,1)S(1)} %pad_maximum_fusion.4), channel_id=1, source_target_pairs={{0,24},{1,25},{2,26},{3,27},{4,28},{5,29},{6,30},{7,31},{8,16},{9,... | collective-permute-start | bytes 786440 | tf_op jit(solution)/shard_map/ppermute | solution.py:265
  33.8 10.7 %collective-permute-start.16 = (bf16[2,5,64,128]{3,2,1,0:T(8,128)(2,1)S(1)}, bf16[2,5,64,128]{3,2,1,0:T(8,128)(2,1)S(1)}, u32[]{:S(2)}, u32[]{:S(2)}) collective-permute-start(bf16[2,5,64,128]{3,2,1,0:T(8,128)(2,1)S(1)} %get-tuple-element.20), channel_id=1, source_target_pairs={{0,1},{1,0},{2,3},{3,2},{4,5},{5,4},{6,7},{7,6},{8,9},{9,8},{10,11... | collective-permute-start | bytes 491528 | tf_op jit(solution)/shard_map/ppermute | solution.py:265
  37.4 11.2 %collective-permute-start.6 = (bf16[4,2,256,128]{3,2,1,0:T(8,128)(2,1)S(1)}, bf16[4,2,256,128]{3,2,1,0:T(8,128)(2,1)S(1)}, u32[]{:S(2)}, u32[]{:S(2)}) collective-permute-start(bf16[4,2,256,128]{3,2,1,0:T(8,128)(2,1)S(1)} %get-tuple-element.17), channel_id=1, source_target_pairs={{0,4},{1,5},{2,6},{3,7},{4,0},{5,1},{6,2},{7,3},{8,12},{9,13},{10,... | collective-permute-start | bytes 1572872 | tf_op jit(solution)/shard_map/ppermute | solution.py:265
  44.5 1.4 %collective-permute-start.23 = (bf16[2,256,128]{2,1,0:T(8,128)(2,1)S(1)}, bf16[2,256,128]{2,1,0:T(8,128)(2,1)S(1)}, u32[]{:S(2)}, u32[]{:S(2)}) collective-permute-start(bf16[2,256,128]{2,1,0:T(8,128)(2,1)S(1)} %fusion.17), channel_id=1, source_target_pairs={{0,4},{1,5},{2,6},{3,7},{4,0},{5,1},{6,2},{7,3},{8,12},{9,13},{10,... | collective-permute-start | bytes 393224 | tf_op jit(solution)/shard_map/ppermute | solution.py:265
  44.6 9.4 %collective-permute-start.5 = (bf16[2,5,64,128]{3,2,1,0:T(8,128)(2,1)S(1)}, bf16[2,5,64,128]{3,2,1,0:T(8,128)(2,1)S(1)}, u32[]{:S(2)}, u32[]{:S(2)}) collective-permute-start(bf16[2,5,64,128]{3,2,1,0:T(8,128)(2,1)S(1)} %get-tuple-element.15), channel_id=1, source_target_pairs={{0,1},{1,0},{2,3},{3,2},{4,5},{5,4},{6,7},{7,6},{8,9},{9,8},{10,11... | collective-permute-start | bytes 491528 | tf_op jit(solution)/shard_map/ppermute | solution.py:265
  46.0 9.2 %collective-permute-start.24 = (bf16[2,256,128]{2,1,0:T(8,128)(2,1)S(1)}, bf16[2,256,128]{2,1,0:T(8,128)(2,1)S(1)}, u32[]{:S(2)}, u32[]{:S(2)}) collective-permute-start(bf16[2,256,128]{2,1,0:T(8,128)(2,1)S(1)} %fusion.10), channel_id=1, source_target_pairs={{0,2},{1,3},{2,0},{3,1},{4,6},{5,7},{6,4},{7,5},{8,10},{9,11},{10,... | collective-permute-start | bytes 393224 | tf_op jit(solution)/shard_map/ppermute | solution.py:265
  48.7 6.4 %collective-permute-start.20 = (bf16[2,256,128]{2,1,0:T(8,128)(2,1)S(1)}, bf16[2,256,128]{2,1,0:T(8,128)(2,1)S(1)}, u32[]{:S(2)}, u32[]{:S(2)}) collective-permute-start(bf16[2,256,128]{2,1,0:T(8,128)(2,1)S(1)} %get-tuple-element.37), channel_id=1, source_target_pairs={{0,8},{1,9},{2,10},{3,11},{4,12},{5,13},{6,14},{7,15},{8,0},{9,1},... | collective-permute-start | bytes 393224 | tf_op jit(solution)/shard_map/ppermute | solution.py:265
  49.1 7.9 %collective-permute-start.21 = (bf16[2,256,128]{2,1,0:T(8,128)(2,1)S(1)}, bf16[2,256,128]{2,1,0:T(8,128)(2,1)S(1)}, u32[]{:S(2)}, u32[]{:S(2)}) collective-permute-start(bf16[2,256,128]{2,1,0:T(8,128)(2,1)S(1)} %get-tuple-element.35), channel_id=1, source_target_pairs={{0,16},{1,17},{2,18},{3,19},{4,20},{5,21},{6,22},{7,23},{8,24},{9,... | collective-permute-start | bytes 393224 | tf_op jit(solution)/shard_map/ppermute | solution.py:265
  50.8 6.2 %collective-permute-start.22 = (bf16[2,256,128]{2,1,0:T(8,128)(2,1)S(1)}, bf16[2,256,128]{2,1,0:T(8,128)(2,1)S(1)}, u32[]{:S(2)}, u32[]{:S(2)}) collective-permute-start(bf16[2,256,128]{2,1,0:T(8,128)(2,1)S(1)} %get-tuple-element.36), channel_id=1, source_target_pairs={{0,24},{1,25},{2,26},{3,27},{4,28},{5,29},{6,30},{7,31},{8,16},{9,... | collective-permute-start | bytes 393224 | tf_op jit(solution)/shard_map/ppermute | solution.py:265

commit v4 on v3

--- a/solution.py
+++ b/solution.py
@@ -294,12 +294,12 @@
         return sums[0], [sums[d].astype(jnp.bfloat16) for d in columns[1:]]
 
     def add_columns(mine, parts):
-        for d, part in zip(columns[1:], parts):
+        for d, part in reversed(list(zip(columns[1:], parts))):
             mine = mine + swap(part, 2 * d, 0).astype(jnp.float32)
         return mine
 
     far_kept_total, far_sent_total = far_kept[0], far_sent[0].astype(jnp.float32)
-    for d in columns[1:]:
+    for d in reversed(columns[1:]):
         both_cores = swap(jnp.stack([far_kept[d].astype(jnp.bfloat16), far_sent[d]]), 2 * d, 0)
         both_cores = both_cores.astype(jnp.float32)
         far_kept_total = far_kept_total + both_cores[0]

time: 57.9 us -> 58.2 us (level)
  waiting for transfers between devices: 17.5 us -> 18.7 us
  starting transfers between devices: 28.7 us -> 27.8 us
    ppermute x25, waiting for transfers between devices: 17.5 us -> 18.7 us  [swap(): return lax.ppermute(x, ('seq', 'head'), pairs)]
    ppermute x25, starting transfers between devices: 28.7 us -> 27.8 us  [swap(): return lax.ppermute(x, ('seq', 'head'), pairs)]
  transfers between devices with their start and end apart: 25 -> 25, of which waited for: 9 -> 10; matrix products, arithmetic and copies ran while one was open for 6% -> 6% of each run, Pallas kernels for 10% -> 10%
where the time goes in v4:
time: 58.2 us; the launch traced here: 58 us
  starting transfers between devices  27.8 us (48%)
  waiting for transfers between devices  18.7 us (32%)
  Pallas kernels  5.67 us (10%)
  other arithmetic  3.28 us (6%)
  local copies, waits for them, and re-layouts  1.69 us (3%)
  between operations  0.84 us (1%)
    ppermute x25, starting transfers between devices, swap(): return lax.ppermute(x, ('seq', 'head'), pairs)  27.8 us
    ppermute x25, waiting for transfers between devices, swap(): return lax.ppermute(x, ('seq', 'head'), pairs)  18.7 us
    pallas_call x2, Pallas kernels, attention(): pl.pallas_call(functools.partial(attention_kernel, column_count, group_la...  5.67 us
    squeeze x1, other arithmetic, piece(): return lax.dynamic_index_in_dim(both, z ^ flip, 0, keepdims=False)  1.51 us
  transfers between devices with their start and end apart: 25, of which 10 were waited for; matrix products, arithmetic and copies ran while one was open for 6% of the time, Pallas kernels for 10%

profile of v4, /device:TPU:0, one launch (start us, length us, event | category | flops | bytes accessed | tf_op | source)
XLA Modules:
  0.0 58.0 jit_solution(12457125735553076842)
XLA Ops:
  0.6 0.9 %fusion.18 = (bf16[1,2,256,128]{3,2,1,0:T(8,128)(2,1)S(1)}, bf16[2,256,128]{2,1,0:T(8,128)(2,1)S(1)}) fusion(bf16[1,256,128]{2,1,0:T(8,128)(2,1)} %bitcast.83, bf16[1,256,128]{2,1,0:T(8,128)(2,1)} %bitcast.84), kind=kLoop, calls=%fused_computation.50 | loop fusion | flops 65536 | bytes 393216 | tf_op jit(solution)/shard_map/stack | solution.py:273
  1.5 4.1 %collective-permute-start.8 = (bf16[2,256,128]{2,1,0:T(8,128)(2,1)S(1)}, bf16[2,256,128]{2,1,0:T(8,128)(2,1)S(1)}, u32[]{:S(2)}, u32[]{:S(2)}) collective-permute-start(bf16[2,256,128]{2,1,0:T(8,128)(2,1)S(1)} %get-tuple-element.47.refs_2_), channel_id=1, source_target_pairs={{0,2},{1,3},{2,0},{3,1},{4,6},{5,7},{6,4},{7,5},{8,10},{9,11},{10,... | collective-permute-start | bytes 393224 | tf_op jit(solution)/shard_map/ppermute | solution.py:265
  5.6 1.5 %collective-permute-start.1 = (bf16[2,256,128]{2,1,0:T(8,128)(2,1)S(1)}, bf16[2,256,128]{2,1,0:T(8,128)(2,1)S(1)}, u32[]{:S(2)}, u32[]{:S(2)}) collective-permute-start(bf16[2,256,128]{2,1,0:T(8,128)(2,1)S(1)} %get-tuple-element.47.refs_2_), channel_id=1, source_target_pairs={{0,8},{1,9},{2,10},{3,11},{4,12},{5,13},{6,14},{7,15},{8,0},{9,1},... | collective-permute-start | bytes 393224 | tf_op jit(solution)/shard_map/ppermute | solution.py:265
  7.1 1.5 %collective-permute-start.2 = (bf16[2,256,128]{2,1,0:T(8,128)(2,1)S(1)}, bf16[2,256,128]{2,1,0:T(8,128)(2,1)S(1)}, u32[]{:S(2)}, u32[]{:S(2)}) collective-permute-start(bf16[2,256,128]{2,1,0:T(8,128)(2,1)S(1)} %get-tuple-element.47.refs_2_), channel_id=1, source_target_pairs={{0,16},{1,17},{2,18},{3,19},{4,20},{5,21},{6,22},{7,23},{8,24},{9,... | collective-permute-start | bytes 393224 | tf_op jit(solution)/shard_map/ppermute | solution.py:265
  8.6 1.5 %fusion.5 = (bf16[2,2,5,64,128]{4,3,2,1,0:T(8,128)(2,1)S(1)}, bf16[2,2,5,64,128]{4,3,2,1,0:T(8,128)(2,1)S(1)}, bf16[2,2,5,64,128]{4,3,2,1,0:T(8,128)(2,1)S(1)}, bf16[2,2,5,64,128]{4,3,2,1,0:T(8,128)(2,1)S(1)}) fusion(s32[]{:T(128)S(6)} %select_n.19, bf16[1,2,64,4,5,128]{5,2,4,3,1,0:T(8,128)(2,1)} %bitcast.79, bf16[1,2,64,4,5,128]{5,2,4,3,1,0:T(8,128)(2,1)} %bitcast.80, ...), kind=kLoop, calls=%fused_computation.17 | loop fusion | flops 655360 | bytes 2621456 | tf_op jit(solution)/shard_map/jit(dynamic_index_in_dim)/squeeze | solution.py:280
  10.1 0.0 copy-start
  10.2 1.6 %collective-permute-start.7 = (bf16[2,2,5,64,128]{4,3,2,1,0:T(8,128)(2,1)S(1)}, bf16[2,2,5,64,128]{4,3,2,1,0:T(8,128)(2,1)S(1)}, u32[]{:S(2)}, u32[]{:S(2)}) collective-permute-start(bf16[2,2,5,64,128]{4,3,2,1,0:T(8,128)(2,1)S(1)} %get-tuple-element.30), channel_id=1, source_target_pairs={{0,1},{1,0},{2,3},{3,2},{4,5},{5,4},{6,7},{7,6},{8,9},{9,8},{10,11... | collective-permute-start | bytes 983048 | tf_op jit(solution)/shard_map/ppermute | solution.py:265
  11.8 0.5 collective-permute-start.3
  12.3 0.0 collective-permute-done.8.refs_2_
  12.3 1.5 %collective-permute-start.9 = (bf16[2,256,128]{2,1,0:T(8,128)(2,1)S(1)}, bf16[2,256,128]{2,1,0:T(8,128)(2,1)S(1)}, u32[]{:S(2)}, u32[]{:S(2)}) collective-permute-start(bf16[2,256,128]{2,1,0:T(8,128)(2,1)S(1)} %collective-permute-done.8.refs_2_), channel_id=1, source_target_pairs={{0,8},{1,9},{2,10},{3,11},{4,12},{5,13},{6,14},{7,15},{8,0},{9,1},... | collective-permute-start | bytes 393224 | tf_op jit(solution)/shard_map/ppermute | solution.py:265
  13.8 0.0 collective-permute-done.1.refs_3_
  13.8 1.5 %collective-permute-start.10 = (bf16[2,256,128]{2,1,0:T(8,128)(2,1)S(1)}, bf16[2,256,128]{2,1,0:T(8,128)(2,1)S(1)}, u32[]{:S(2)}, u32[]{:S(2)}) collective-permute-start(bf16[2,256,128]{2,1,0:T(8,128)(2,1)S(1)} %collective-permute-done.8.refs_2_), channel_id=1, source_target_pairs={{0,16},{1,17},{2,18},{3,19},{4,20},{5,21},{6,22},{7,23},{8,24},{9,... | collective-permute-start | bytes 393224 | tf_op jit(solution)/shard_map/ppermute | solution.py:265
  15.3 0.0 collective-permute-done.2.refs_4_
  15.3 0.5 collective-permute-start.11
  15.8 3.5 %collective-permute-done.3.refs_5_ = bf16[2,256,128]{2,1,0:T(8,128)(2,1)S(1)} collective-permute-done((bf16[2,256,128]{2,1,0:T(8,128)(2,1)S(1)}, bf16[2,256,128]{2,1,0:T(8,128)(2,1)S(1)}, u32[]{:S(2)}, u32[]{:S(2)}) %collective-permute-start.3) | collective-permute-done | bytes 131104 | tf_op jit(solution)/shard_map/ppermute | solution.py:265
  19.2 0.0 collective-permute-start.12
  19.2 0.9 %collective-permute-done.9.refs_3_ = bf16[2,256,128]{2,1,0:T(8,128)(2,1)S(1)} collective-permute-done((bf16[2,256,128]{2,1,0:T(8,128)(2,1)S(1)}, bf16[2,256,128]{2,1,0:T(8,128)(2,1)S(1)}, u32[]{:S(2)}, u32[]{:S(2)}) %collective-permute-start.9) | collective-permute-done | bytes 131104 | tf_op jit(solution)/shard_map/ppermute | solution.py:265
  20.1 0.0 collective-permute-start.13
  20.1 0.9 %collective-permute-done.10.refs_4_ = bf16[2,256,128]{2,1,0:T(8,128)(2,1)S(1)} collective-permute-done((bf16[2,256,128]{2,1,0:T(8,128)(2,1)S(1)}, bf16[2,256,128]{2,1,0:T(8,128)(2,1)S(1)}, u32[]{:S(2)}, u32[]{:S(2)}) %collective-permute-start.10) | collective-permute-done | bytes 131104 | tf_op jit(solution)/shard_map/ppermute | solution.py:265
  21.0 0.0 collective-permute-start.14
  21.0 1.4 %collective-permute-done.11.refs_5_ = bf16[2,256,128]{2,1,0:T(8,128)(2,1)S(1)} collective-permute-done((bf16[2,256,128]{2,1,0:T(8,128)(2,1)S(1)}, bf16[2,256,128]{2,1,0:T(8,128)(2,1)S(1)}, u32[]{:S(2)}, u32[]{:S(2)}) %collective-permute-start.11) | collective-permute-done | bytes 131104 | tf_op jit(solution)/shard_map/ppermute | solution.py:265
  22.5 0.0 collective-permute-start.15
  22.5 0.1 pad_maximum_fusion.1
  22.5 0.0 collective-permute-done.12.refs_6_
  22.6 1.7 %collective-permute-start = (bf16[2,2,5,64,128]{4,3,2,1,0:T(8,128)(2,1)S(1)}, bf16[2,2,5,64,128]{4,3,2,1,0:T(8,128)(2,1)S(1)}, u32[]{:S(2)}, u32[]{:S(2)}) collective-permute-start(bf16[2,2,5,64,128]{4,3,2,1,0:T(8,128)(2,1)S(1)} %get-tuple-element.27), channel_id=1, source_target_pairs={{0,1},{1,0},{2,3},{3,2},{4,5},{5,4},{6,7},{7,6},{8,9},{9,8},{10,11... | collective-permute-start | bytes 983048 | tf_op jit(solution)/shard_map/ppermute | solution.py:265
  24.2 0.0 collective-permute-done.7.refs_1_
  24.2 0.0 collective-permute-start.4
  24.2 0.0 collective-permute-done.13.refs_7_
  24.2 0.0 collective-permute-done.14.refs_8_
  24.2 0.0 collective-permute-done.15.refs_9_
  24.3 2.9 %attention_far.1 = (bf16[2,5,64,128]{3,2,1,0:T(8,128)(2,1)S(1)}, bf16[2,5,64,128]{3,2,1,0:T(8,128)(2,1)S(1)}, f32[4,2,256,128]{3,2,1,0:T(8,128)S(1)}, bf16[4,2,256,128]{3,2,1,0:T(8,128)(2,1)S(1)}) custom-call(s32[2048]{0:T(1024)S(1)} %copy-done, s32[16,128]{1,0:T(8,128)S(1)} %bitcast.76, bf16[2,2,5,64,128]{4,3,2,1,0:T(8,128)(2,1)S(1)} %get-tuple-element.29.refs_0_, ...), custom_call_target="tpu_custom_call" | custom-call | flops 3355443200 | bytes 4194304 | tf_op jit(solution)/shard_map/attention_far/pallas_call | solution.py:220
  27.2 0.1 convert.14
  27.4 1.8 %collective-permute-start.17 = (bf16[2,2,256,128]{3,2,1,0:T(8,128)(2,1)S(1)}, bf16[2,2,256,128]{3,2,1,0:T(8,128)(2,1)S(1)}, u32[]{:S(2)}, u32[]{:S(2)}) collective-permute-start(bf16[2,2,256,128]{3,2,1,0:T(8,128)(2,1)S(1)} %pad_maximum_fusion.2), channel_id=1, source_target_pairs={{0,24},{1,25},{2,26},{3,27},{4,28},{5,29},{6,30},{7,31},{8,16},{9,... | collective-permute-start | bytes 786440 | tf_op jit(solution)/shard_map/ppermute | solution.py:265
  29.2 3.0 %collective-permute-start.18 = (bf16[2,2,256,128]{3,2,1,0:T(8,128)(2,1)S(1)}, bf16[2,2,256,128]{3,2,1,0:T(8,128)(2,1)S(1)}, u32[]{:S(2)}, u32[]{:S(2)}) collective-permute-start(bf16[2,2,256,128]{3,2,1,0:T(8,128)(2,1)S(1)} %pad_maximum_fusion.3), channel_id=1, source_target_pairs={{0,16},{1,17},{2,18},{3,19},{4,20},{5,21},{6,22},{7,23},{8,24},{9,... | collective-permute-start | bytes 786440 | tf_op jit(solution)/shard_map/ppermute | solution.py:265
  32.2 1.5 %collective-permute-start.19 = (bf16[2,2,256,128]{3,2,1,0:T(8,128)(2,1)S(1)}, bf16[2,2,256,128]{3,2,1,0:T(8,128)(2,1)S(1)}, u32[]{:S(2)}, u32[]{:S(2)}) collective-permute-start(bf16[2,2,256,128]{3,2,1,0:T(8,128)(2,1)S(1)} %pad_maximum_fusion.4), channel_id=1, source_target_pairs={{0,8},{1,9},{2,10},{3,11},{4,12},{5,13},{6,14},{7,15},{8,0},{9,1},... | collective-permute-start | bytes 786440 | tf_op jit(solution)/shard_map/ppermute | solution.py:265
  33.8 0.0 collective-permute-done.refs_1_
  33.8 0.9 %collective-permute-start.16 = (bf16[2,5,64,128]{3,2,1,0:T(8,128)(2,1)S(1)}, bf16[2,5,64,128]{3,2,1,0:T(8,128)(2,1)S(1)}, u32[]{:S(2)}, u32[]{:S(2)}) collective-permute-start(bf16[2,5,64,128]{3,2,1,0:T(8,128)(2,1)S(1)} %get-tuple-element.20), channel_id=1, source_target_pairs={{0,1},{1,0},{2,3},{3,2},{4,5},{5,4},{6,7},{7,6},{8,9},{9,8},{10,11... | collective-permute-start | bytes 491528 | tf_op jit(solution)/shard_map/ppermute | solution.py:265
  34.6 0.0 collective-permute-done.4.refs_6_
  34.6 2.7 %attention_near.1 = (bf16[2,5,64,128]{3,2,1,0:T(8,128)(2,1)S(1)}, bf16[2,5,64,128]{3,2,1,0:T(8,128)(2,1)S(1)}, f32[4,2,256,128]{3,2,1,0:T(8,128)S(1)}, bf16[4,2,256,128]{3,2,1,0:T(8,128)(2,1)S(1)}) custom-call(s32[2048]{0:T(1024)S(1)} %copy-done, s32[16,128]{1,0:T(8,128)S(1)} %bitcast.77, bf16[2,2,5,64,128]{4,3,2,1,0:T(8,128)(2,1)S(1)} %get-tuple-element.28.refs_0_, ...), custom_call_target="tpu_custom_call" | custom-call | flops 3355443200 | bytes 4194304 | tf_op jit(solution)/shard_map/attention_near/pallas_call | solution.py:220
  37.4 1.4 %collective-permute-start.6 = (bf16[4,2,256,128]{3,2,1,0:T(8,128)(2,1)S(1)}, bf16[4,2,256,128]{3,2,1,0:T(8,128)(2,1)S(1)}, u32[]{:S(2)}, u32[]{:S(2)}) collective-permute-start(bf16[4,2,256,128]{3,2,1,0:T(8,128)(2,1)S(1)} %get-tuple-element.17), channel_id=1, source_target_pairs={{0,4},{1,5},{2,6},{3,7},{4,0},{5,1},{6,2},{7,3},{8,12},{9,13},{10,... | collective-permute-start | bytes 1572872 | tf_op jit(solution)/shard_map/ppermute | solution.py:265
  38.8 0.0 collective-permute-done.17
  38.9 5.2 %collective-permute-done.18 = bf16[2,2,256,128]{3,2,1,0:T(8,128)(2,1)S(1)} collective-permute-done((bf16[2,2,256,128]{3,2,1,0:T(8,128)(2,1)S(1)}, bf16[2,2,256,128]{3,2,1,0:T(8,128)(2,1)S(1)}, u32[]{:S(2)}, u32[]{:S(2)}) %collective-permute-start.18) | collective-permute-done | bytes 262176 | tf_op jit(solution)/shard_map/ppermute | solution.py:265
  44.1 1.8 %collective-permute-done.19 = bf16[2,2,256,128]{3,2,1,0:T(8,128)(2,1)S(1)} collective-permute-done((bf16[2,2,256,128]{3,2,1,0:T(8,128)(2,1)S(1)}, bf16[2,2,256,128]{3,2,1,0:T(8,128)(2,1)S(1)}, u32[]{:S(2)}, u32[]{:S(2)}) %collective-permute-start.19) | collective-permute-done | bytes 262176 | tf_op jit(solution)/shard_map/ppermute | solution.py:265
  46.0 0.1 fusion.17
  46.1 0.0 collective-permute-done.16
  46.1 0.3 collective-permute-start.23
  46.4 0.9 %collective-permute-start.5 = (bf16[2,5,64,128]{3,2,1,0:T(8,128)(2,1)S(1)}, bf16[2,5,64,128]{3,2,1,0:T(8,128)(2,1)S(1)}, u32[]{:S(2)}, u32[]{:S(2)}) collective-permute-start(bf16[2,5,64,128]{3,2,1,0:T(8,128)(2,1)S(1)} %get-tuple-element.15), channel_id=1, source_target_pairs={{0,1},{1,0},{2,3},{3,2},{4,5},{5,4},{6,7},{7,6},{8,9},{9,8},{10,11... | collective-permute-start | bytes 491528 | tf_op jit(solution)/shard_map/ppermute | solution.py:265
  47.2 0.2 collective-permute-done.23
  47.5 0.1 fusion.10
  47.5 0.1 collective-permute-start.24
  47.6 0.0 collective-permute-done.6
  47.6 0.2 fusion.19
  47.9 2.0 %collective-permute-start.20 = (bf16[2,256,128]{2,1,0:T(8,128)(2,1)S(1)}, bf16[2,256,128]{2,1,0:T(8,128)(2,1)S(1)}, u32[]{:S(2)}, u32[]{:S(2)}) collective-permute-start(bf16[2,256,128]{2,1,0:T(8,128)(2,1)S(1)} %get-tuple-element.35), channel_id=1, source_target_pairs={{0,24},{1,25},{2,26},{3,27},{4,28},{5,29},{6,30},{7,31},{8,16},{9,... | collective-permute-start | bytes 393224 | tf_op jit(solution)/shard_map/ppermute | solution.py:265
  49.9 0.7 %collective-permute-start.21 = (bf16[2,256,128]{2,1,0:T(8,128)(2,1)S(1)}, bf16[2,256,128]{2,1,0:T(8,128)(2,1)S(1)}, u32[]{:S(2)}, u32[]{:S(2)}) collective-permute-start(bf16[2,256,128]{2,1,0:T(8,128)(2,1)S(1)} %get-tuple-element.36), channel_id=1, source_target_pairs={{0,16},{1,17},{2,18},{3,19},{4,20},{5,21},{6,22},{7,23},{8,24},{9,... | collective-permute-start | bytes 393224 | tf_op jit(solution)/shard_map/ppermute | solution.py:265
  50.6 0.8 %collective-permute-start.22 = (bf16[2,256,128]{2,1,0:T(8,128)(2,1)S(1)}, bf16[2,256,128]{2,1,0:T(8,128)(2,1)S(1)}, u32[]{:S(2)}, u32[]{:S(2)}) collective-permute-start(bf16[2,256,128]{2,1,0:T(8,128)(2,1)S(1)} %get-tuple-element.37), channel_id=1, source_target_pairs={{0,8},{1,9},{2,10},{3,11},{4,12},{5,13},{6,14},{7,15},{8,0},{9,1},... | collective-permute-start | bytes 393224 | tf_op jit(solution)/shard_map/ppermute | solution.py:265
  51.4 1.7 %collective-permute-done.5 = bf16[2,5,64,128]{3,2,1,0:T(8,128)(2,1)S(1)} collective-permute-done((bf16[2,5,64,128]{3,2,1,0:T(8,128)(2,1)S(1)}, bf16[2,5,64,128]{3,2,1,0:T(8,128)(2,1)S(1)}, u32[]{:S(2)}, u32[]{:S(2)}) %collective-permute-start.5) | collective-permute-done | bytes 163872 | tf_op jit(solution)/shard_map/ppermute | solution.py:265
  53.2 0.1 pad_maximum_fusion
  53.2 0.1 constant_dynamic-slice_fusion.3
  53.3 0.1 maximum_bitcast_fusion
  53.4 0.9 %copy.10 = bf16[2,64,4,5,128]{4,1,3,2,0:T(8,128)(2,1)} copy(bf16[2,64,4,5,128]{4,1,3,0,2:T(8,128)(2,1)S(1)} %maximum_bitcast_fusion) | data formatting | bytes 1310720 | tf_op jit(solution)/shard_map/transpose | solution.py:323
  54.3 2.7 %collective-permute-done.24 = bf16[2,256,128]{2,1,0:T(8,128)(2,1)S(1)} collective-permute-done((bf16[2,256,128]{2,1,0:T(8,128)(2,1)S(1)}, bf16[2,256,128]{2,1,0:T(8,128)(2,1)S(1)}, u32[]{:S(2)}, u32[]{:S(2)}) %collective-permute-start.24) | collective-permute-done | bytes 131104 | tf_op jit(solution)/shard_map/ppermute | solution.py:265
  57.0 0.3 collective-permute-done.21
  57.3 0.1 fusion.15
  57.4 0.7 %slice_bitcast_fusion.4 = (bf16[256,1,128]{2,0,1:T(8,128)(2,1)}, bf16[256,1,128]{2,0,1:T(8,128)(2,1)}) fusion(bf16[2,256,128]{2,1,0:T(8,128)(2,1)S(1)} %fusion.15), kind=kLoop, calls=%fused_computation.44 | loop fusion | bytes 262144 | tf_op jit(solution)/shard_map/squeeze | solution.py:325
  (12 shorter events, 0.3 us)
Async XLA Ops:
  1.5 10.8 %collective-permute-start.8 = (bf16[2,256,128]{2,1,0:T(8,128)(2,1)S(1)}, bf16[2,256,128]{2,1,0:T(8,128)(2,1)S(1)}, u32[]{:S(2)}, u32[]{:S(2)}) collective-permute-start(bf16[2,256,128]{2,1,0:T(8,128)(2,1)S(1)} %get-tuple-element.47.refs_2_), channel_id=1, source_target_pairs={{0,2},{1,3},{2,0},{3,1},{4,6},{5,7},{6,4},{7,5},{8,10},{9,11},{10,... | collective-permute-start | bytes 393224 | tf_op jit(solution)/shard_map/ppermute | solution.py:265
  5.6 8.2 %collective-permute-start.1 = (bf16[2,256,128]{2,1,0:T(8,128)(2,1)S(1)}, bf16[2,256,128]{2,1,0:T(8,128)(2,1)S(1)}, u32[]{:S(2)}, u32[]{:S(2)}) collective-permute-start(bf16[2,256,128]{2,1,0:T(8,128)(2,1)S(1)} %get-tuple-element.47.refs_2_), channel_id=1, source_target_pairs={{0,8},{1,9},{2,10},{3,11},{4,12},{5,13},{6,14},{7,15},{8,0},{9,1},... | collective-permute-start | bytes 393224 | tf_op jit(solution)/shard_map/ppermute | solution.py:265
  7.1 8.2 %collective-permute-start.2 = (bf16[2,256,128]{2,1,0:T(8,128)(2,1)S(1)}, bf16[2,256,128]{2,1,0:T(8,128)(2,1)S(1)}, u32[]{:S(2)}, u32[]{:S(2)}) collective-permute-start(bf16[2,256,128]{2,1,0:T(8,128)(2,1)S(1)} %get-tuple-element.47.refs_2_), channel_id=1, source_target_pairs={{0,16},{1,17},{2,18},{3,19},{4,20},{5,21},{6,22},{7,23},{8,24},{9,... | collective-permute-start | bytes 393224 | tf_op jit(solution)/shard_map/ppermute | solution.py:265
  10.1 14.1 %copy-start = (s32[2048]{0:T(1024)S(1)}, s32[2048]{0:T(1024)}, u32[]{:S(2)}) copy-start(s32[2048]{0:T(1024)} %doc_ref.3) | copy-start | bytes 24580
  10.2 14.1 %collective-permute-start.7 = (bf16[2,2,5,64,128]{4,3,2,1,0:T(8,128)(2,1)S(1)}, bf16[2,2,5,64,128]{4,3,2,1,0:T(8,128)(2,1)S(1)}, u32[]{:S(2)}, u32[]{:S(2)}) collective-permute-start(bf16[2,2,5,64,128]{4,3,2,1,0:T(8,128)(2,1)S(1)} %get-tuple-element.30), channel_id=1, source_target_pairs={{0,1},{1,0},{2,3},{3,2},{4,5},{5,4},{6,7},{7,6},{8,9},{9,8},{10,11... | collective-permute-start | bytes 983048 | tf_op jit(solution)/shard_map/ppermute | solution.py:265
  11.8 7.4 %collective-permute-start.3 = (bf16[2,256,128]{2,1,0:T(8,128)(2,1)S(1)}, bf16[2,256,128]{2,1,0:T(8,128)(2,1)S(1)}, u32[]{:S(2)}, u32[]{:S(2)}) collective-permute-start(bf16[2,256,128]{2,1,0:T(8,128)(2,1)S(1)} %get-tuple-element.47.refs_2_), channel_id=1, source_target_pairs={{0,24},{1,25},{2,26},{3,27},{4,28},{5,29},{6,30},{7,31},{8,16},{9,... | collective-permute-start | bytes 393224 | tf_op jit(solution)/shard_map/ppermute | solution.py:265
  12.3 7.8 %collective-permute-start.9 = (bf16[2,256,128]{2,1,0:T(8,128)(2,1)S(1)}, bf16[2,256,128]{2,1,0:T(8,128)(2,1)S(1)}, u32[]{:S(2)}, u32[]{:S(2)}) collective-permute-start(bf16[2,256,128]{2,1,0:T(8,128)(2,1)S(1)} %collective-permute-done.8.refs_2_), channel_id=1, source_target_pairs={{0,8},{1,9},{2,10},{3,11},{4,12},{5,13},{6,14},{7,15},{8,0},{9,1},... | collective-permute-start | bytes 393224 | tf_op jit(solution)/shard_map/ppermute | solution.py:265
  13.8 7.3 %collective-permute-start.10 = (bf16[2,256,128]{2,1,0:T(8,128)(2,1)S(1)}, bf16[2,256,128]{2,1,0:T(8,128)(2,1)S(1)}, u32[]{:S(2)}, u32[]{:S(2)}) collective-permute-start(bf16[2,256,128]{2,1,0:T(8,128)(2,1)S(1)} %collective-permute-done.8.refs_2_), channel_id=1, source_target_pairs={{0,16},{1,17},{2,18},{3,19},{4,20},{5,21},{6,22},{7,23},{8,24},{9,... | collective-permute-start | bytes 393224 | tf_op jit(solution)/shard_map/ppermute | solution.py:265
  15.3 7.2 %collective-permute-start.11 = (bf16[2,256,128]{2,1,0:T(8,128)(2,1)S(1)}, bf16[2,256,128]{2,1,0:T(8,128)(2,1)S(1)}, u32[]{:S(2)}, u32[]{:S(2)}) collective-permute-start(bf16[2,256,128]{2,1,0:T(8,128)(2,1)S(1)} %collective-permute-done.8.refs_2_), channel_id=1, source_target_pairs={{0,24},{1,25},{2,26},{3,27},{4,28},{5,29},{6,30},{7,31},{8,16},{9,... | collective-permute-start | bytes 393224 | tf_op jit(solution)/shard_map/ppermute | solution.py:265
  19.2 3.3 %collective-permute-start.12 = (bf16[2,256,128]{2,1,0:T(8,128)(2,1)S(1)}, bf16[2,256,128]{2,1,0:T(8,128)(2,1)S(1)}, u32[]{:S(2)}, u32[]{:S(2)}) collective-permute-start(bf16[2,256,128]{2,1,0:T(8,128)(2,1)S(1)} %collective-permute-done.8.refs_2_), channel_id=1, source_target_pairs={{0,4},{1,5},{2,6},{3,7},{4,0},{5,1},{6,2},{7,3},{8,12},{9,13},{10,... | collective-permute-start | bytes 393224 | tf_op jit(solution)/shard_map/ppermute | solution.py:265
  20.1 4.1 %collective-permute-start.13 = (bf16[2,256,128]{2,1,0:T(8,128)(2,1)S(1)}, bf16[2,256,128]{2,1,0:T(8,128)(2,1)S(1)}, u32[]{:S(2)}, u32[]{:S(2)}) collective-permute-start(bf16[2,256,128]{2,1,0:T(8,128)(2,1)S(1)} %collective-permute-done.9.refs_3_), channel_id=1, source_target_pairs={{0,4},{1,5},{2,6},{3,7},{4,0},{5,1},{6,2},{7,3},{8,12},{9,13},{10,... | collective-permute-start | bytes 393224 | tf_op jit(solution)/shard_map/ppermute | solution.py:265
  21.0 3.2 %collective-permute-start.14 = (bf16[2,256,128]{2,1,0:T(8,128)(2,1)S(1)}, bf16[2,256,128]{2,1,0:T(8,128)(2,1)S(1)}, u32[]{:S(2)}, u32[]{:S(2)}) collective-permute-start(bf16[2,256,128]{2,1,0:T(8,128)(2,1)S(1)} %collective-permute-done.10.refs_4_), channel_id=1, source_target_pairs={{0,4},{1,5},{2,6},{3,7},{4,0},{5,1},{6,2},{7,3},{8,12},{9,13},{10,... | collective-permute-start | bytes 393224 | tf_op jit(solution)/shard_map/ppermute | solution.py:265
  22.5 1.8 %collective-permute-start.15 = (bf16[2,256,128]{2,1,0:T(8,128)(2,1)S(1)}, bf16[2,256,128]{2,1,0:T(8,128)(2,1)S(1)}, u32[]{:S(2)}, u32[]{:S(2)}) collective-permute-start(bf16[2,256,128]{2,1,0:T(8,128)(2,1)S(1)} %collective-permute-done.11.refs_5_), channel_id=1, source_target_pairs={{0,4},{1,5},{2,6},{3,7},{4,0},{5,1},{6,2},{7,3},{8,12},{9,13},{10,... | collective-permute-start | bytes 393224 | tf_op jit(solution)/shard_map/ppermute | solution.py:265
  22.6 11.2 %collective-permute-start = (bf16[2,2,5,64,128]{4,3,2,1,0:T(8,128)(2,1)S(1)}, bf16[2,2,5,64,128]{4,3,2,1,0:T(8,128)(2,1)S(1)}, u32[]{:S(2)}, u32[]{:S(2)}) collective-permute-start(bf16[2,2,5,64,128]{4,3,2,1,0:T(8,128)(2,1)S(1)} %get-tuple-element.27), channel_id=1, source_target_pairs={{0,1},{1,0},{2,3},{3,2},{4,5},{5,4},{6,7},{7,6},{8,9},{9,8},{10,11... | collective-permute-start | bytes 983048 | tf_op jit(solution)/shard_map/ppermute | solution.py:265
  24.2 10.4 %collective-permute-start.4 = (bf16[4,2,256,128]{3,2,1,0:T(8,128)(2,1)S(1)}, bf16[4,2,256,128]{3,2,1,0:T(8,128)(2,1)S(1)}, u32[]{:S(2)}, u32[]{:S(2)}) collective-permute-start(bf16[4,2,256,128]{3,2,1,0:T(8,128)(2,1)S(1)} %pad_maximum_fusion.1), channel_id=1, source_target_pairs={{0,4},{1,5},{2,6},{3,7},{4,0},{5,1},{6,2},{7,3},{8,12},{9,13},{10,... | collective-permute-start | bytes 1572872 | tf_op jit(solution)/shard_map/ppermute | solution.py:265
  27.4 11.4 %collective-permute-start.17 = (bf16[2,2,256,128]{3,2,1,0:T(8,128)(2,1)S(1)}, bf16[2,2,256,128]{3,2,1,0:T(8,128)(2,1)S(1)}, u32[]{:S(2)}, u32[]{:S(2)}) collective-permute-start(bf16[2,2,256,128]{3,2,1,0:T(8,128)(2,1)S(1)} %pad_maximum_fusion.2), channel_id=1, source_target_pairs={{0,24},{1,25},{2,26},{3,27},{4,28},{5,29},{6,30},{7,31},{8,16},{9,... | collective-permute-start | bytes 786440 | tf_op jit(solution)/shard_map/ppermute | solution.py:265
  29.2 14.9 %collective-permute-start.18 = (bf16[2,2,256,128]{3,2,1,0:T(8,128)(2,1)S(1)}, bf16[2,2,256,128]{3,2,1,0:T(8,128)(2,1)S(1)}, u32[]{:S(2)}, u32[]{:S(2)}) collective-permute-start(bf16[2,2,256,128]{3,2,1,0:T(8,128)(2,1)S(1)} %pad_maximum_fusion.3), channel_id=1, source_target_pairs={{0,16},{1,17},{2,18},{3,19},{4,20},{5,21},{6,22},{7,23},{8,24},{9,... | collective-permute-start | bytes 786440 | tf_op jit(solution)/shard_map/ppermute | solution.py:265
  32.2 13.7 %collective-permute-start.19 = (bf16[2,2,256,128]{3,2,1,0:T(8,128)(2,1)S(1)}, bf16[2,2,256,128]{3,2,1,0:T(8,128)(2,1)S(1)}, u32[]{:S(2)}, u32[]{:S(2)}) collective-permute-start(bf16[2,2,256,128]{3,2,1,0:T(8,128)(2,1)S(1)} %pad_maximum_fusion.4), channel_id=1, source_target_pairs={{0,8},{1,9},{2,10},{3,11},{4,12},{5,13},{6,14},{7,15},{8,0},{9,1},... | collective-permute-start | bytes 786440 | tf_op jit(solution)/shard_map/ppermute | solution.py:265
  33.8 12.3 %collective-permute-start.16 = (bf16[2,5,64,128]{3,2,1,0:T(8,128)(2,1)S(1)}, bf16[2,5,64,128]{3,2,1,0:T(8,128)(2,1)S(1)}, u32[]{:S(2)}, u32[]{:S(2)}) collective-permute-start(bf16[2,5,64,128]{3,2,1,0:T(8,128)(2,1)S(1)} %get-tuple-element.20), channel_id=1, source_target_pairs={{0,1},{1,0},{2,3},{3,2},{4,5},{5,4},{6,7},{7,6},{8,9},{9,8},{10,11... | collective-permute-start | bytes 491528 | tf_op jit(solution)/shard_map/ppermute | solution.py:265
  37.4 10.3 %collective-permute-start.6 = (bf16[4,2,256,128]{3,2,1,0:T(8,128)(2,1)S(1)}, bf16[4,2,256,128]{3,2,1,0:T(8,128)(2,1)S(1)}, u32[]{:S(2)}, u32[]{:S(2)}) collective-permute-start(bf16[4,2,256,128]{3,2,1,0:T(8,128)(2,1)S(1)} %get-tuple-element.17), channel_id=1, source_target_pairs={{0,4},{1,5},{2,6},{3,7},{4,0},{5,1},{6,2},{7,3},{8,12},{9,13},{10,... | collective-permute-start | bytes 1572872 | tf_op jit(solution)/shard_map/ppermute | solution.py:265
  46.1 1.4 %collective-permute-start.23 = (bf16[2,256,128]{2,1,0:T(8,128)(2,1)S(1)}, bf16[2,256,128]{2,1,0:T(8,128)(2,1)S(1)}, u32[]{:S(2)}, u32[]{:S(2)}) collective-permute-start(bf16[2,256,128]{2,1,0:T(8,128)(2,1)S(1)} %fusion.17), channel_id=1, source_target_pairs={{0,4},{1,5},{2,6},{3,7},{4,0},{5,1},{6,2},{7,3},{8,12},{9,13},{10,... | collective-permute-start | bytes 393224 | tf_op jit(solution)/shard_map/ppermute | solution.py:265
  46.4 6.8 %collective-permute-start.5 = (bf16[2,5,64,128]{3,2,1,0:T(8,128)(2,1)S(1)}, bf16[2,5,64,128]{3,2,1,0:T(8,128)(2,1)S(1)}, u32[]{:S(2)}, u32[]{:S(2)}) collective-permute-start(bf16[2,5,64,128]{3,2,1,0:T(8,128)(2,1)S(1)} %get-tuple-element.15), channel_id=1, source_target_pairs={{0,1},{1,0},{2,3},{3,2},{4,5},{5,4},{6,7},{7,6},{8,9},{9,8},{10,11... | collective-permute-start | bytes 491528 | tf_op jit(solution)/shard_map/ppermute | solution.py:265
  47.5 9.4 %collective-permute-start.24 = (bf16[2,256,128]{2,1,0:T(8,128)(2,1)S(1)}, bf16[2,256,128]{2,1,0:T(8,128)(2,1)S(1)}, u32[]{:S(2)}, u32[]{:S(2)}) collective-permute-start(bf16[2,256,128]{2,1,0:T(8,128)(2,1)S(1)} %fusion.10), channel_id=1, source_target_pairs={{0,2},{1,3},{2,0},{3,1},{4,6},{5,7},{6,4},{7,5},{8,10},{9,11},{10,... | collective-permute-start | bytes 393224 | tf_op jit(solution)/shard_map/ppermute | solution.py:265
  47.9 9.1 %collective-permute-start.20 = (bf16[2,256,128]{2,1,0:T(8,128)(2,1)S(1)}, bf16[2,256,128]{2,1,0:T(8,128)(2,1)S(1)}, u32[]{:S(2)}, u32[]{:S(2)}) collective-permute-start(bf16[2,256,128]{2,1,0:T(8,128)(2,1)S(1)} %get-tuple-element.35), channel_id=1, source_target_pairs={{0,24},{1,25},{2,26},{3,27},{4,28},{5,29},{6,30},{7,31},{8,16},{9,... | collective-permute-start | bytes 393224 | tf_op jit(solution)/shard_map/ppermute | solution.py:265
  49.9 7.4 %collective-permute-start.21 = (bf16[2,256,128]{2,1,0:T(8,128)(2,1)S(1)}, bf16[2,256,128]{2,1,0:T(8,128)(2,1)S(1)}, u32[]{:S(2)}, u32[]{:S(2)}) collective-permute-start(bf16[2,256,128]{2,1,0:T(8,128)(2,1)S(1)} %get-tuple-element.36), channel_id=1, source_target_pairs={{0,16},{1,17},{2,18},{3,19},{4,20},{5,21},{6,22},{7,23},{8,24},{9,... | collective-permute-start | bytes 393224 | tf_op jit(solution)/shard_map/ppermute | solution.py:265
  50.6 6.7 %collective-permute-start.22 = (bf16[2,256,128]{2,1,0:T(8,128)(2,1)S(1)}, bf16[2,256,128]{2,1,0:T(8,128)(2,1)S(1)}, u32[]{:S(2)}, u32[]{:S(2)}) collective-permute-start(bf16[2,256,128]{2,1,0:T(8,128)(2,1)S(1)} %get-tuple-element.37), channel_id=1, source_target_pairs={{0,8},{1,9},{2,10},{3,11},{4,12},{5,13},{6,14},{7,15},{8,0},{9,1},... | collective-permute-start | bytes 393224 | tf_op jit(solution)/shard_map/ppermute | solution.py:265

commit v5 on v3

--- a/solution.py
+++ b/solution.py
@@ -14,17 +14,19 @@
 SCORE_BYTES = 24 * 1024 * 1024
 
 
-def attention_kernel(column_count, group_lanes, merged, doc_ref, doc_rows_ref, *refs):
+def attention_kernel(column_count, group_lanes, merged, direct, doc_ref, doc_rows_ref, *refs):
     chunk_refs = refs[:2]
     kv_refs = refs[2 : 2 + column_count]
     kv_other = refs[2 + column_count : 2 + 2 * column_count]
     if merged:
         kv_other = [refs[2 + column_count].at[d] for d in range(column_count)]
+    part_count = column_count - 1 if direct else 0
+    dq_own, dq_send, kept_ref, sent_ref = refs[-19 - part_count : -15 - part_count]
+    part_refs = refs[-15 - part_count : -15]
     (
-        dq_own, dq_send, kept_ref, sent_ref,
         q_rows, g_rows, q_cols, g_cols, keys, values,
         e_scr, d_scr, m_scr, max_scr, sum_scr, weight_scr, dqt, dk_acc, dv_acc,
-    ) = refs[-19:]
+    ) = refs[-15:]
     layers, group, tokens, width = dq_own.shape
     block_tokens = kv_refs[0].shape[1]
     pair = 2 * tokens
@@ -184,22 +186,26 @@
             out[n // group, n % group] = q_rows[n, pl.ds(at, tokens), :]
 
     for d in range(column_count):
-        for b, out in enumerate((kept_ref, sent_ref)):
+        for b, near_ref in enumerate((kept_ref, sent_ref)):
+            if direct:
+                out = part_refs[d - 1].at[b] if d else near_ref
+            else:
+                out = near_ref.at[d]
             start = pl.multiple_of(((column ^ d) * 2 + (core ^ b)) * block_tokens, block_tokens)
             rows = pl.ds(start, block_tokens)
             seen = (start >= low * KEY_BLOCK) & (start < high * KEY_BLOCK)
 
             @pl.when(seen)
             def _():
-                out[d, 0] = (dk_acc[rows, :] * scale).astype(out.dtype)
-                out[d, 1] = dv_acc[rows, :].astype(out.dtype)
+                out[0] = (dk_acc[rows, :] * scale).astype(out.dtype)
+                out[1] = dv_acc[rows, :].astype(out.dtype)
 
             @pl.when(jnp.logical_not(seen))
             def _():
-                out[d] = jnp.zeros(out.shape[1:], out.dtype)
-
-
-def attention(name, doc_start, chunks, kv_own, kv_other, after=()):
+                out[...] = jnp.zeros(out.shape, out.dtype)
+
+
+def attention(name, doc_start, chunks, kv_own, kv_other, direct=False, after=()):
     _, layers, group, tokens, width = chunks[0].shape
     column_count = len(kv_own)
     merged = len(kv_other) == 1
@@ -215,10 +221,15 @@
     vmem = pl.BlockSpec(memory_space=pltpu.VMEM)
     f32, bf16 = jnp.float32, jnp.bfloat16
     outs = [jax.ShapeDtypeStruct((layers, group, tokens, width), bf16)] * 2
-    outs.append(jax.ShapeDtypeStruct((column_count, 2, block_tokens, width), f32))
-    outs.append(jax.ShapeDtypeStruct((column_count, 2, block_tokens, width), bf16))
+    block = (2, block_tokens, width)
+    if direct:
+        outs += [jax.ShapeDtypeStruct(block, f32), jax.ShapeDtypeStruct(block, bf16)]
+        outs += [jax.ShapeDtypeStruct((2,) + block, bf16)] * (column_count - 1)
+    else:
+        outs.append(jax.ShapeDtypeStruct((column_count,) + block, f32))
+        outs.append(jax.ShapeDtypeStruct((column_count,) + block, bf16))
     return pl.pallas_call(
-        functools.partial(attention_kernel, column_count, group_lanes, merged),
+        functools.partial(attention_kernel, column_count, group_lanes, merged, direct),
         out_shape=outs,
         in_specs=[smem] + [vmem] * (1 + 2 + column_count + len(kv_other))
         + [pl.BlockSpec(memory_space=pl.ANY)] * len(after),
@@ -285,8 +296,8 @@
     near_dq, near_dq_send, near_kept, near_sent = attention(
         "attention_near", doc_start, near_chunks, near, near_other
     )
-    far_dq, far_dq_send, far_kept, far_sent = attention(
-        "attention_far", doc_start, far_chunks, far, far_other
+    far_dq, far_dq_send, far_kept, far_sent, *far_parts = attention(
+        "attention_far", doc_start, far_chunks, far, far_other, True
     )
 
     def add_cores(kept, sent):
@@ -298,9 +309,9 @@
             mine = mine + swap(part, 2 * d, 0).astype(jnp.float32)
         return mine
 
-    far_kept_total, far_sent_total = far_kept[0], far_sent[0].astype(jnp.float32)
+    far_kept_total, far_sent_total = far_kept, far_sent.astype(jnp.float32)
     for d in columns[1:]:
-        both_cores = swap(jnp.stack([far_kept[d].astype(jnp.bfloat16), far_sent[d]]), 2 * d, 0)
+        both_cores = swap(far_parts[d - 1], 2 * d, 0)
         both_cores = both_cores.astype(jnp.float32)
         far_kept_total = far_kept_total + both_cores[0]
         far_sent_total = far_sent_total + both_cores[1]

time: 57.9 us -> 57.6 us (level)
  waiting for transfers between devices: 17.5 us -> 15.4 us
  starting transfers between devices: 28.7 us -> 30.7 us
    ppermute x25, waiting for transfers between devices: 17.5 us -> 15.4 us  [swap(): return lax.ppermute(x, ('seq', 'head'), pairs)]
    ppermute x25, starting transfers between devices: 28.7 us -> 30.7 us  [swap(): return lax.ppermute(x, ('seq', 'head'), pairs)]
  transfers between devices with their start and end apart: 25 -> 25, of which waited for: 9 -> 7; matrix products, arithmetic and copies ran while one was open for 6% -> 5% of each run, Pallas kernels for 10% -> 10%
where the time goes in v5:
time: 57.6 us; the launch traced here: 57.4 us
  starting transfers between devices  30.7 us (53%)
  waiting for transfers between devices  15.4 us (27%)
  Pallas kernels  5.66 us (10%)
  other arithmetic  3.13 us (5%)
  local copies, waits for them, and re-layouts  1.64 us (3%)
  between operations  0.79 us (1%)
    ppermute x25, starting transfers between devices, swap(): return lax.ppermute(x, ('seq', 'head'), pairs)  30.7 us
    ppermute x25, waiting for transfers between devices, swap(): return lax.ppermute(x, ('seq', 'head'), pairs)  15.4 us
    pallas_call x2, Pallas kernels, attention(): pl.pallas_call(functools.partial(attention_kernel, column_count, group_la...  5.66 us
    squeeze x1, other arithmetic, piece(): return lax.dynamic_index_in_dim(both, z ^ flip, 0, keepdims=False)  1.51 us
  transfers between devices with their start and end apart: 25, of which 7 were waited for; matrix products, arithmetic and copies ran while one was open for 5% of the time, Pallas kernels for 10%

profile of v5, /device:TPU:0, one launch (start us, length us, event | category | flops | bytes accessed | tf_op | source)
XLA Modules:
  0.0 57.4 jit_solution(12222636354540996009)
XLA Ops:
  0.6 0.9 %fusion.22 = (bf16[1,2,256,128]{3,2,1,0:T(8,128)(2,1)S(1)}, bf16[2,256,128]{2,1,0:T(8,128)(2,1)S(1)}) fusion(bf16[1,256,128]{2,1,0:T(8,128)(2,1)} %bitcast.113, bf16[1,256,128]{2,1,0:T(8,128)(2,1)} %bitcast.114), kind=kLoop, calls=%fused_computation.51 | loop fusion | flops 65536 | bytes 393216 | tf_op jit(solution)/shard_map/stack | solution.py:284
  1.5 4.1 %collective-permute-start.8 = (bf16[2,256,128]{2,1,0:T(8,128)(2,1)S(1)}, bf16[2,256,128]{2,1,0:T(8,128)(2,1)S(1)}, u32[]{:S(2)}, u32[]{:S(2)}) collective-permute-start(bf16[2,256,128]{2,1,0:T(8,128)(2,1)S(1)} %get-tuple-element.47.refs_2_), channel_id=1, source_target_pairs={{0,2},{1,3},{2,0},{3,1},{4,6},{5,7},{6,4},{7,5},{8,10},{9,11},{10,... | collective-permute-start | bytes 393224 | tf_op jit(solution)/shard_map/ppermute | solution.py:276
  5.6 1.5 %collective-permute-start.1 = (bf16[2,256,128]{2,1,0:T(8,128)(2,1)S(1)}, bf16[2,256,128]{2,1,0:T(8,128)(2,1)S(1)}, u32[]{:S(2)}, u32[]{:S(2)}) collective-permute-start(bf16[2,256,128]{2,1,0:T(8,128)(2,1)S(1)} %get-tuple-element.47.refs_2_), channel_id=1, source_target_pairs={{0,8},{1,9},{2,10},{3,11},{4,12},{5,13},{6,14},{7,15},{8,0},{9,1},... | collective-permute-start | bytes 393224 | tf_op jit(solution)/shard_map/ppermute | solution.py:276
  7.1 1.5 %collective-permute-start.2 = (bf16[2,256,128]{2,1,0:T(8,128)(2,1)S(1)}, bf16[2,256,128]{2,1,0:T(8,128)(2,1)S(1)}, u32[]{:S(2)}, u32[]{:S(2)}) collective-permute-start(bf16[2,256,128]{2,1,0:T(8,128)(2,1)S(1)} %get-tuple-element.47.refs_2_), channel_id=1, source_target_pairs={{0,16},{1,17},{2,18},{3,19},{4,20},{5,21},{6,22},{7,23},{8,24},{9,... | collective-permute-start | bytes 393224 | tf_op jit(solution)/shard_map/ppermute | solution.py:276
  8.6 0.5 collective-permute-start.3
  9.1 1.5 %fusion.5 = (bf16[2,2,5,64,128]{4,3,2,1,0:T(8,128)(2,1)S(1)}, bf16[2,2,5,64,128]{4,3,2,1,0:T(8,128)(2,1)S(1)}, bf16[2,2,5,64,128]{4,3,2,1,0:T(8,128)(2,1)S(1)}, bf16[2,2,5,64,128]{4,3,2,1,0:T(8,128)(2,1)S(1)}) fusion(s32[]{:T(128)S(6)} %select_n.19, bf16[1,2,64,4,5,128]{5,2,4,3,1,0:T(8,128)(2,1)} %bitcast.109, bf16[1,2,64,4,5,128]{5,2,4,3,1,0:T(8,128)(2,1)} %bitcast.110, ...), kind=kLoop, calls=%fused_computation.17 | loop fusion | flops 655360 | bytes 2621456 | tf_op jit(solution)/shard_map/jit(dynamic_index_in_dim)/squeeze | solution.py:291
  10.6 0.0 copy-start
  10.6 1.6 %collective-permute-start.7 = (bf16[2,2,5,64,128]{4,3,2,1,0:T(8,128)(2,1)S(1)}, bf16[2,2,5,64,128]{4,3,2,1,0:T(8,128)(2,1)S(1)}, u32[]{:S(2)}, u32[]{:S(2)}) collective-permute-start(bf16[2,2,5,64,128]{4,3,2,1,0:T(8,128)(2,1)S(1)} %get-tuple-element.36), channel_id=1, source_target_pairs={{0,1},{1,0},{2,3},{3,2},{4,5},{5,4},{6,7},{7,6},{8,9},{9,8},{10,11... | collective-permute-start | bytes 983048 | tf_op jit(solution)/shard_map/ppermute | solution.py:276
  12.3 0.0 collective-permute-done.8.refs_2_
  12.3 1.5 %collective-permute-start.9 = (bf16[2,256,128]{2,1,0:T(8,128)(2,1)S(1)}, bf16[2,256,128]{2,1,0:T(8,128)(2,1)S(1)}, u32[]{:S(2)}, u32[]{:S(2)}) collective-permute-start(bf16[2,256,128]{2,1,0:T(8,128)(2,1)S(1)} %collective-permute-done.8.refs_2_), channel_id=1, source_target_pairs={{0,8},{1,9},{2,10},{3,11},{4,12},{5,13},{6,14},{7,15},{8,0},{9,1},... | collective-permute-start | bytes 393224 | tf_op jit(solution)/shard_map/ppermute | solution.py:276
  13.8 0.0 collective-permute-done.1.refs_3_
  13.8 1.5 %collective-permute-start.10 = (bf16[2,256,128]{2,1,0:T(8,128)(2,1)S(1)}, bf16[2,256,128]{2,1,0:T(8,128)(2,1)S(1)}, u32[]{:S(2)}, u32[]{:S(2)}) collective-permute-start(bf16[2,256,128]{2,1,0:T(8,128)(2,1)S(1)} %collective-permute-done.8.refs_2_), channel_id=1, source_target_pairs={{0,16},{1,17},{2,18},{3,19},{4,20},{5,21},{6,22},{7,23},{8,24},{9,... | collective-permute-start | bytes 393224 | tf_op jit(solution)/shard_map/ppermute | solution.py:276
  15.3 0.0 collective-permute-done.2.refs_4_
  15.3 0.8 %collective-permute-start.11 = (bf16[2,256,128]{2,1,0:T(8,128)(2,1)S(1)}, bf16[2,256,128]{2,1,0:T(8,128)(2,1)S(1)}, u32[]{:S(2)}, u32[]{:S(2)}) collective-permute-start(bf16[2,256,128]{2,1,0:T(8,128)(2,1)S(1)} %collective-permute-done.8.refs_2_), channel_id=1, source_target_pairs={{0,24},{1,25},{2,26},{3,27},{4,28},{5,29},{6,30},{7,31},{8,16},{9,... | collective-permute-start | bytes 393224 | tf_op jit(solution)/shard_map/ppermute | solution.py:276
  16.1 0.0 collective-permute-done.3.refs_5_
  16.1 0.0 collective-permute-start.12
  16.1 0.1 pad_maximum_fusion.1
  16.2 2.4 %collective-permute-done.9.refs_3_ = bf16[2,256,128]{2,1,0:T(8,128)(2,1)S(1)} collective-permute-done((bf16[2,256,128]{2,1,0:T(8,128)(2,1)S(1)}, bf16[2,256,128]{2,1,0:T(8,128)(2,1)S(1)}, u32[]{:S(2)}, u32[]{:S(2)}) %collective-permute-start.9) | collective-permute-done | bytes 131104 | tf_op jit(solution)/shard_map/ppermute | solution.py:276
  18.5 0.0 collective-permute-start.4
  18.5 2.8 %collective-permute-done.10.refs_4_ = bf16[2,256,128]{2,1,0:T(8,128)(2,1)S(1)} collective-permute-done((bf16[2,256,128]{2,1,0:T(8,128)(2,1)S(1)}, bf16[2,256,128]{2,1,0:T(8,128)(2,1)S(1)}, u32[]{:S(2)}, u32[]{:S(2)}) %collective-permute-start.10) | collective-permute-done | bytes 131104 | tf_op jit(solution)/shard_map/ppermute | solution.py:276
  21.3 0.0 collective-permute-start.13
  21.3 0.0 collective-permute-done.11.refs_5_
  21.4 0.5 collective-permute-start.14
  21.9 0.0 collective-permute-done.12.refs_6_
  21.9 0.1 collective-permute-start.15
  21.9 0.0 collective-permute-done.7.refs_1_
  21.9 0.9 %collective-permute-start = (bf16[2,2,5,64,128]{4,3,2,1,0:T(8,128)(2,1)S(1)}, bf16[2,2,5,64,128]{4,3,2,1,0:T(8,128)(2,1)S(1)}, u32[]{:S(2)}, u32[]{:S(2)}) collective-permute-start(bf16[2,2,5,64,128]{4,3,2,1,0:T(8,128)(2,1)S(1)} %get-tuple-element.33), channel_id=1, source_target_pairs={{0,1},{1,0},{2,3},{3,2},{4,5},{5,4},{6,7},{7,6},{8,9},{9,8},{10,11... | collective-permute-start | bytes 983048 | tf_op jit(solution)/shard_map/ppermute | solution.py:276
  22.9 0.0 collective-permute-done.13.refs_7_
  22.9 0.0 collective-permute-done.14.refs_8_
  22.9 0.3 collective-permute-done.15.refs_9_
  23.2 2.9 %attention_far.1 = (bf16[2,5,64,128]{3,2,1,0:T(8,128)(2,1)S(1)}, bf16[2,5,64,128]{3,2,1,0:T(8,128)(2,1)S(1)}, f32[2,256,128]{2,1,0:T(8,128)S(1)}, bf16[2,256,128...) custom-call(s32[2048]{0:T(1024)S(1)} %copy-done, ...), custom_call_target="tpu_custom_call" | custom-call | flops 3355443200 | bytes 4194304 | tf_op jit(solution)/shard_map/attention_far/pallas_call | solution.py:231
  26.1 2.8 %collective-permute-start.17 = (bf16[2,2,256,128]{3,2,1,0:T(8,128)(2,1)S(1)}, bf16[2,2,256,128]{3,2,1,0:T(8,128)(2,1)S(1)}, u32[]{:S(2)}, u32[]{:S(2)}) collective-permute-start(bf16[2,2,256,128]{3,2,1,0:T(8,128)(2,1)S(1)} %get-tuple-element.25), channel_id=1, source_target_pairs={{0,8},{1,9},{2,10},{3,11},{4,12},{5,13},{6,14},{7,15},{8,0},{9,1},... | collective-permute-start | bytes 786440 | tf_op jit(solution)/shard_map/ppermute | solution.py:276
  28.9 2.0 %collective-permute-start.18 = (bf16[2,2,256,128]{3,2,1,0:T(8,128)(2,1)S(1)}, bf16[2,2,256,128]{3,2,1,0:T(8,128)(2,1)S(1)}, u32[]{:S(2)}, u32[]{:S(2)}) collective-permute-start(bf16[2,2,256,128]{3,2,1,0:T(8,128)(2,1)S(1)} %get-tuple-element.26), channel_id=1, source_target_pairs={{0,16},{1,17},{2,18},{3,19},{4,20},{5,21},{6,22},{7,23},{8,24},{9,... | collective-permute-start | bytes 786440 | tf_op jit(solution)/shard_map/ppermute | solution.py:276
  30.9 1.4 %collective-permute-start.19 = (bf16[2,2,256,128]{3,2,1,0:T(8,128)(2,1)S(1)}, bf16[2,2,256,128]{3,2,1,0:T(8,128)(2,1)S(1)}, u32[]{:S(2)}, u32[]{:S(2)}) collective-permute-start(bf16[2,2,256,128]{3,2,1,0:T(8,128)(2,1)S(1)} %get-tuple-element.27), channel_id=1, source_target_pairs={{0,24},{1,25},{2,26},{3,27},{4,28},{5,29},{6,30},{7,31},{8,16},{9,... | collective-permute-start | bytes 786440 | tf_op jit(solution)/shard_map/ppermute | solution.py:276
  32.3 0.0 collective-permute-done.refs_1_
  32.3 1.3 %collective-permute-start.16 = (bf16[2,5,64,128]{3,2,1,0:T(8,128)(2,1)S(1)}, bf16[2,5,64,128]{3,2,1,0:T(8,128)(2,1)S(1)}, u32[]{:S(2)}, u32[]{:S(2)}) collective-permute-start(bf16[2,5,64,128]{3,2,1,0:T(8,128)(2,1)S(1)} %get-tuple-element.23), channel_id=1, source_target_pairs={{0,1},{1,0},{2,3},{3,2},{4,5},{5,4},{6,7},{7,6},{8,9},{9,8},{10,11... | collective-permute-start | bytes 491528 | tf_op jit(solution)/shard_map/ppermute | solution.py:276
  33.6 0.0 collective-permute-done.4.refs_6_
  33.6 2.7 %attention_near.1 = (bf16[2,5,64,128]{3,2,1,0:T(8,128)(2,1)S(1)}, bf16[2,5,64,128]{3,2,1,0:T(8,128)(2,1)S(1)}, f32[4,2,256,128]{3,2,1,0:T(8,128)S(1)}, bf16[4,2,256,128]{3,2,1,0:T(8,128)(2,1)S(1)}) custom-call(s32[2048]{0:T(1024)S(1)} %copy-done, s32[16,128]{1,0:T(8,128)S(1)} %bitcast.107, bf16[2,2,5,64,128]{4,3,2,1,0:T(8,128)(2,1)S(1)} %get-tuple-element.34.refs_0_, ...), custom_call_target="tpu_custom_call" | custom-call | flops 3355443200 | bytes 4194304 | tf_op jit(solution)/shard_map/attention_near/pallas_call | solution.py:231
  36.4 0.1 collective-permute-start.6
  36.4 0.0 collective-permute-done.17
  36.5 6.3 %collective-permute-done.18 = bf16[2,2,256,128]{3,2,1,0:T(8,128)(2,1)S(1)} collective-permute-done((bf16[2,2,256,128]{3,2,1,0:T(8,128)(2,1)S(1)}, bf16[2,2,256,128]{3,2,1,0:T(8,128)(2,1)S(1)}, u32[]{:S(2)}, u32[]{:S(2)}) %collective-permute-start.18) | collective-permute-done | bytes 262176 | tf_op jit(solution)/shard_map/ppermute | solution.py:276
  42.9 0.1 fusion.19
  42.9 0.0 collective-permute-done.16
  43.0 0.1 collective-permute-start.23
  43.0 1.6 %collective-permute-start.5 = (bf16[2,5,64,128]{3,2,1,0:T(8,128)(2,1)S(1)}, bf16[2,5,64,128]{3,2,1,0:T(8,128)(2,1)S(1)}, u32[]{:S(2)}, u32[]{:S(2)}) collective-permute-start(bf16[2,5,64,128]{3,2,1,0:T(8,128)(2,1)S(1)} %get-tuple-element.18), channel_id=1, source_target_pairs={{0,1},{1,0},{2,3},{3,2},{4,5},{5,4},{6,7},{7,6},{8,9},{9,8},{10,11... | collective-permute-start | bytes 491528 | tf_op jit(solution)/shard_map/ppermute | solution.py:276
  44.6 0.0 collective-permute-done.23
  44.6 0.1 fusion.10
  44.7 3.4 %collective-permute-start.24 = (bf16[2,256,128]{2,1,0:T(8,128)(2,1)S(1)}, bf16[2,256,128]{2,1,0:T(8,128)(2,1)S(1)}, u32[]{:S(2)}, u32[]{:S(2)}) collective-permute-start(bf16[2,256,128]{2,1,0:T(8,128)(2,1)S(1)} %fusion.10), channel_id=1, source_target_pairs={{0,2},{1,3},{2,0},{3,1},{4,6},{5,7},{6,4},{7,5},{8,10},{9,11},{10,... | collective-permute-start | bytes 393224 | tf_op jit(solution)/shard_map/ppermute | solution.py:276
  48.2 0.0 collective-permute-done.6
  48.2 0.2 fusion.23
  48.4 0.4 collective-permute-start.20
  48.8 1.6 %collective-permute-start.21 = (bf16[2,256,128]{2,1,0:T(8,128)(2,1)S(1)}, bf16[2,256,128]{2,1,0:T(8,128)(2,1)S(1)}, u32[]{:S(2)}, u32[]{:S(2)}) collective-permute-start(bf16[2,256,128]{2,1,0:T(8,128)(2,1)S(1)} %get-tuple-element.41), channel_id=1, source_target_pairs={{0,16},{1,17},{2,18},{3,19},{4,20},{5,21},{6,22},{7,23},{8,24},{9,... | collective-permute-start | bytes 393224 | tf_op jit(solution)/shard_map/ppermute | solution.py:276
  50.4 1.5 %collective-permute-start.22 = (bf16[2,256,128]{2,1,0:T(8,128)(2,1)S(1)}, bf16[2,256,128]{2,1,0:T(8,128)(2,1)S(1)}, u32[]{:S(2)}, u32[]{:S(2)}) collective-permute-start(bf16[2,256,128]{2,1,0:T(8,128)(2,1)S(1)} %get-tuple-element.42), channel_id=1, source_target_pairs={{0,24},{1,25},{2,26},{3,27},{4,28},{5,29},{6,30},{7,31},{8,16},{9,... | collective-permute-start | bytes 393224 | tf_op jit(solution)/shard_map/ppermute | solution.py:276
  51.9 0.5 collective-permute-done.5
  52.5 0.1 pad_maximum_fusion
  52.5 0.1 constant_dynamic-slice_fusion.3
  52.6 0.1 maximum_bitcast_fusion
  52.7 0.9 %copy.10 = bf16[2,64,4,5,128]{4,1,3,2,0:T(8,128)(2,1)} copy(bf16[2,64,4,5,128]{4,1,3,0,2:T(8,128)(2,1)S(1)} %maximum_bitcast_fusion) | data formatting | bytes 1310720 | tf_op jit(solution)/shard_map/transpose | solution.py:334
  53.6 0.0 collective-permute-done.24
  53.6 1.2 %collective-permute-done.20 = bf16[2,256,128]{2,1,0:T(8,128)(2,1)S(1)} collective-permute-done((bf16[2,256,128]{2,1,0:T(8,128)(2,1)S(1)}, bf16[2,256,128]{2,1,0:T(8,128)(2,1)S(1)}, u32[]{:S(2)}, u32[]{:S(2)}) %collective-permute-start.20) | collective-permute-done | bytes 131104 | tf_op jit(solution)/shard_map/ppermute | solution.py:276
  54.8 1.8 %collective-permute-done.21 = bf16[2,256,128]{2,1,0:T(8,128)(2,1)S(1)} collective-permute-done((bf16[2,256,128]{2,1,0:T(8,128)(2,1)S(1)}, bf16[2,256,128]{2,1,0:T(8,128)(2,1)S(1)}, u32[]{:S(2)}, u32[]{:S(2)}) %collective-permute-start.21) | collective-permute-done | bytes 131104 | tf_op jit(solution)/shard_map/ppermute | solution.py:276
  56.6 0.0 collective-permute-done.22
  56.6 0.1 fusion.17
  56.7 0.7 %slice_bitcast_fusion.10 = (bf16[256,1,128]{2,0,1:T(8,128)(2,1)}, bf16[256,1,128]{2,0,1:T(8,128)(2,1)}) fusion(bf16[2,256,128]{2,1,0:T(8,128)(2,1)S(1)} %fusion.17), kind=kLoop, calls=%fused_computation.45 | loop fusion | bytes 262144 | tf_op jit(solution)/shard_map/squeeze | solution.py:336
  (6 shorter events, 0.1 us)
Async XLA Ops:
  1.5 10.8 %collective-permute-start.8 = (bf16[2,256,128]{2,1,0:T(8,128)(2,1)S(1)}, bf16[2,256,128]{2,1,0:T(8,128)(2,1)S(1)}, u32[]{:S(2)}, u32[]{:S(2)}) collective-permute-start(bf16[2,256,128]{2,1,0:T(8,128)(2,1)S(1)} %get-tuple-element.47.refs_2_), channel_id=1, source_target_pairs={{0,2},{1,3},{2,0},{3,1},{4,6},{5,7},{6,4},{7,5},{8,10},{9,11},{10,... | collective-permute-start | bytes 393224 | tf_op jit(solution)/shard_map/ppermute | solution.py:276
  5.6 8.2 %collective-permute-start.1 = (bf16[2,256,128]{2,1,0:T(8,128)(2,1)S(1)}, bf16[2,256,128]{2,1,0:T(8,128)(2,1)S(1)}, u32[]{:S(2)}, u32[]{:S(2)}) collective-permute-start(bf16[2,256,128]{2,1,0:T(8,128)(2,1)S(1)} %get-tuple-element.47.refs_2_), channel_id=1, source_target_pairs={{0,8},{1,9},{2,10},{3,11},{4,12},{5,13},{6,14},{7,15},{8,0},{9,1},... | collective-permute-start | bytes 393224 | tf_op jit(solution)/shard_map/ppermute | solution.py:276
  7.1 8.2 %collective-permute-start.2 = (bf16[2,256,128]{2,1,0:T(8,128)(2,1)S(1)}, bf16[2,256,128]{2,1,0:T(8,128)(2,1)S(1)}, u32[]{:S(2)}, u32[]{:S(2)}) collective-permute-start(bf16[2,256,128]{2,1,0:T(8,128)(2,1)S(1)} %get-tuple-element.47.refs_2_), channel_id=1, source_target_pairs={{0,16},{1,17},{2,18},{3,19},{4,20},{5,21},{6,22},{7,23},{8,24},{9,... | collective-permute-start | bytes 393224 | tf_op jit(solution)/shard_map/ppermute | solution.py:276
  8.6 7.5 %collective-permute-start.3 = (bf16[2,256,128]{2,1,0:T(8,128)(2,1)S(1)}, bf16[2,256,128]{2,1,0:T(8,128)(2,1)S(1)}, u32[]{:S(2)}, u32[]{:S(2)}) collective-permute-start(bf16[2,256,128]{2,1,0:T(8,128)(2,1)S(1)} %get-tuple-element.47.refs_2_), channel_id=1, source_target_pairs={{0,24},{1,25},{2,26},{3,27},{4,28},{5,29},{6,30},{7,31},{8,16},{9,... | collective-permute-start | bytes 393224 | tf_op jit(solution)/shard_map/ppermute | solution.py:276
  10.6 12.6 %copy-start = (s32[2048]{0:T(1024)S(1)}, s32[2048]{0:T(1024)}, u32[]{:S(2)}) copy-start(s32[2048]{0:T(1024)} %doc_ref.3) | copy-start | bytes 24580
  10.6 11.3 %collective-permute-start.7 = (bf16[2,2,5,64,128]{4,3,2,1,0:T(8,128)(2,1)S(1)}, bf16[2,2,5,64,128]{4,3,2,1,0:T(8,128)(2,1)S(1)}, u32[]{:S(2)}, u32[]{:S(2)}) collective-permute-start(bf16[2,2,5,64,128]{4,3,2,1,0:T(8,128)(2,1)S(1)} %get-tuple-element.36), channel_id=1, source_target_pairs={{0,1},{1,0},{2,3},{3,2},{4,5},{5,4},{6,7},{7,6},{8,9},{9,8},{10,11... | collective-permute-start | bytes 983048 | tf_op jit(solution)/shard_map/ppermute | solution.py:276
  12.3 6.3 %collective-permute-start.9 = (bf16[2,256,128]{2,1,0:T(8,128)(2,1)S(1)}, bf16[2,256,128]{2,1,0:T(8,128)(2,1)S(1)}, u32[]{:S(2)}, u32[]{:S(2)}) collective-permute-start(bf16[2,256,128]{2,1,0:T(8,128)(2,1)S(1)} %collective-permute-done.8.refs_2_), channel_id=1, source_target_pairs={{0,8},{1,9},{2,10},{3,11},{4,12},{5,13},{6,14},{7,15},{8,0},{9,1},... | collective-permute-start | bytes 393224 | tf_op jit(solution)/shard_map/ppermute | solution.py:276
  13.8 7.6 %collective-permute-start.10 = (bf16[2,256,128]{2,1,0:T(8,128)(2,1)S(1)}, bf16[2,256,128]{2,1,0:T(8,128)(2,1)S(1)}, u32[]{:S(2)}, u32[]{:S(2)}) collective-permute-start(bf16[2,256,128]{2,1,0:T(8,128)(2,1)S(1)} %collective-permute-done.8.refs_2_), channel_id=1, source_target_pairs={{0,16},{1,17},{2,18},{3,19},{4,20},{5,21},{6,22},{7,23},{8,24},{9,... | collective-permute-start | bytes 393224 | tf_op jit(solution)/shard_map/ppermute | solution.py:276
  15.3 6.0 %collective-permute-start.11 = (bf16[2,256,128]{2,1,0:T(8,128)(2,1)S(1)}, bf16[2,256,128]{2,1,0:T(8,128)(2,1)S(1)}, u32[]{:S(2)}, u32[]{:S(2)}) collective-permute-start(bf16[2,256,128]{2,1,0:T(8,128)(2,1)S(1)} %collective-permute-done.8.refs_2_), channel_id=1, source_target_pairs={{0,24},{1,25},{2,26},{3,27},{4,28},{5,29},{6,30},{7,31},{8,16},{9,... | collective-permute-start | bytes 393224 | tf_op jit(solution)/shard_map/ppermute | solution.py:276
  16.1 5.8 %collective-permute-start.12 = (bf16[2,256,128]{2,1,0:T(8,128)(2,1)S(1)}, bf16[2,256,128]{2,1,0:T(8,128)(2,1)S(1)}, u32[]{:S(2)}, u32[]{:S(2)}) collective-permute-start(bf16[2,256,128]{2,1,0:T(8,128)(2,1)S(1)} %collective-permute-done.8.refs_2_), channel_id=1, source_target_pairs={{0,4},{1,5},{2,6},{3,7},{4,0},{5,1},{6,2},{7,3},{8,12},{9,13},{10,... | collective-permute-start | bytes 393224 | tf_op jit(solution)/shard_map/ppermute | solution.py:276
  18.5 15.1 %collective-permute-start.4 = (bf16[4,2,256,128]{3,2,1,0:T(8,128)(2,1)S(1)}, bf16[4,2,256,128]{3,2,1,0:T(8,128)(2,1)S(1)}, u32[]{:S(2)}, u32[]{:S(2)}) collective-permute-start(bf16[4,2,256,128]{3,2,1,0:T(8,128)(2,1)S(1)} %pad_maximum_fusion.1), channel_id=1, source_target_pairs={{0,4},{1,5},{2,6},{3,7},{4,0},{5,1},{6,2},{7,3},{8,12},{9,13},{10,... | collective-permute-start | bytes 1572872 | tf_op jit(solution)/shard_map/ppermute | solution.py:276
  21.3 1.5 %collective-permute-start.13 = (bf16[2,256,128]{2,1,0:T(8,128)(2,1)S(1)}, bf16[2,256,128]{2,1,0:T(8,128)(2,1)S(1)}, u32[]{:S(2)}, u32[]{:S(2)}) collective-permute-start(bf16[2,256,128]{2,1,0:T(8,128)(2,1)S(1)} %collective-permute-done.9.refs_3_), channel_id=1, source_target_pairs={{0,4},{1,5},{2,6},{3,7},{4,0},{5,1},{6,2},{7,3},{8,12},{9,13},{10,... | collective-permute-start | bytes 393224 | tf_op jit(solution)/shard_map/ppermute | solution.py:276
  21.4 1.5 %collective-permute-start.14 = (bf16[2,256,128]{2,1,0:T(8,128)(2,1)S(1)}, bf16[2,256,128]{2,1,0:T(8,128)(2,1)S(1)}, u32[]{:S(2)}, u32[]{:S(2)}) collective-permute-start(bf16[2,256,128]{2,1,0:T(8,128)(2,1)S(1)} %collective-permute-done.10.refs_4_), channel_id=1, source_target_pairs={{0,4},{1,5},{2,6},{3,7},{4,0},{5,1},{6,2},{7,3},{8,12},{9,13},{10,... | collective-permute-start | bytes 393224 | tf_op jit(solution)/shard_map/ppermute | solution.py:276
  21.9 1.3 %collective-permute-start.15 = (bf16[2,256,128]{2,1,0:T(8,128)(2,1)S(1)}, bf16[2,256,128]{2,1,0:T(8,128)(2,1)S(1)}, u32[]{:S(2)}, u32[]{:S(2)}) collective-permute-start(bf16[2,256,128]{2,1,0:T(8,128)(2,1)S(1)} %collective-permute-done.11.refs_5_), channel_id=1, source_target_pairs={{0,4},{1,5},{2,6},{3,7},{4,0},{5,1},{6,2},{7,3},{8,12},{9,13},{10,... | collective-permute-start | bytes 393224 | tf_op jit(solution)/shard_map/ppermute | solution.py:276
  21.9 10.4 %collective-permute-start = (bf16[2,2,5,64,128]{4,3,2,1,0:T(8,128)(2,1)S(1)}, bf16[2,2,5,64,128]{4,3,2,1,0:T(8,128)(2,1)S(1)}, u32[]{:S(2)}, u32[]{:S(2)}) collective-permute-start(bf16[2,2,5,64,128]{4,3,2,1,0:T(8,128)(2,1)S(1)} %get-tuple-element.33), channel_id=1, source_target_pairs={{0,1},{1,0},{2,3},{3,2},{4,5},{5,4},{6,7},{7,6},{8,9},{9,8},{10,11... | collective-permute-start | bytes 983048 | tf_op jit(solution)/shard_map/ppermute | solution.py:276
  26.1 10.3 %collective-permute-start.17 = (bf16[2,2,256,128]{3,2,1,0:T(8,128)(2,1)S(1)}, bf16[2,2,256,128]{3,2,1,0:T(8,128)(2,1)S(1)}, u32[]{:S(2)}, u32[]{:S(2)}) collective-permute-start(bf16[2,2,256,128]{3,2,1,0:T(8,128)(2,1)S(1)} %get-tuple-element.25), channel_id=1, source_target_pairs={{0,8},{1,9},{2,10},{3,11},{4,12},{5,13},{6,14},{7,15},{8,0},{9,1},... | collective-permute-start | bytes 786440 | tf_op jit(solution)/shard_map/ppermute | solution.py:276
  28.9 13.9 %collective-permute-start.18 = (bf16[2,2,256,128]{3,2,1,0:T(8,128)(2,1)S(1)}, bf16[2,2,256,128]{3,2,1,0:T(8,128)(2,1)S(1)}, u32[]{:S(2)}, u32[]{:S(2)}) collective-permute-start(bf16[2,2,256,128]{3,2,1,0:T(8,128)(2,1)S(1)} %get-tuple-element.26), channel_id=1, source_target_pairs={{0,16},{1,17},{2,18},{3,19},{4,20},{5,21},{6,22},{7,23},{8,24},{9,... | collective-permute-start | bytes 786440 | tf_op jit(solution)/shard_map/ppermute | solution.py:276
  30.9 11.9 %collective-permute-start.19 = (bf16[2,2,256,128]{3,2,1,0:T(8,128)(2,1)S(1)}, bf16[2,2,256,128]{3,2,1,0:T(8,128)(2,1)S(1)}, u32[]{:S(2)}, u32[]{:S(2)}) collective-permute-start(bf16[2,2,256,128]{3,2,1,0:T(8,128)(2,1)S(1)} %get-tuple-element.27), channel_id=1, source_target_pairs={{0,24},{1,25},{2,26},{3,27},{4,28},{5,29},{6,30},{7,31},{8,16},{9,... | collective-permute-start | bytes 786440 | tf_op jit(solution)/shard_map/ppermute | solution.py:276
  32.3 10.6 %collective-permute-start.16 = (bf16[2,5,64,128]{3,2,1,0:T(8,128)(2,1)S(1)}, bf16[2,5,64,128]{3,2,1,0:T(8,128)(2,1)S(1)}, u32[]{:S(2)}, u32[]{:S(2)}) collective-permute-start(bf16[2,5,64,128]{3,2,1,0:T(8,128)(2,1)S(1)} %get-tuple-element.23), channel_id=1, source_target_pairs={{0,1},{1,0},{2,3},{3,2},{4,5},{5,4},{6,7},{7,6},{8,9},{9,8},{10,11... | collective-permute-start | bytes 491528 | tf_op jit(solution)/shard_map/ppermute | solution.py:276
  36.4 11.8 %collective-permute-start.6 = (bf16[4,2,256,128]{3,2,1,0:T(8,128)(2,1)S(1)}, bf16[4,2,256,128]{3,2,1,0:T(8,128)(2,1)S(1)}, u32[]{:S(2)}, u32[]{:S(2)}) collective-permute-start(bf16[4,2,256,128]{3,2,1,0:T(8,128)(2,1)S(1)} %get-tuple-element.20), channel_id=1, source_target_pairs={{0,4},{1,5},{2,6},{3,7},{4,0},{5,1},{6,2},{7,3},{8,12},{9,13},{10,... | collective-permute-start | bytes 1572872 | tf_op jit(solution)/shard_map/ppermute | solution.py:276
  43.0 1.7 %collective-permute-start.23 = (bf16[2,256,128]{2,1,0:T(8,128)(2,1)S(1)}, bf16[2,256,128]{2,1,0:T(8,128)(2,1)S(1)}, u32[]{:S(2)}, u32[]{:S(2)}) collective-permute-start(bf16[2,256,128]{2,1,0:T(8,128)(2,1)S(1)} %fusion.19), channel_id=1, source_target_pairs={{0,4},{1,5},{2,6},{3,7},{4,0},{5,1},{6,2},{7,3},{8,12},{9,13},{10,... | collective-permute-start | bytes 393224 | tf_op jit(solution)/shard_map/ppermute | solution.py:276
  43.0 9.4 %collective-permute-start.5 = (bf16[2,5,64,128]{3,2,1,0:T(8,128)(2,1)S(1)}, bf16[2,5,64,128]{3,2,1,0:T(8,128)(2,1)S(1)}, u32[]{:S(2)}, u32[]{:S(2)}) collective-permute-start(bf16[2,5,64,128]{3,2,1,0:T(8,128)(2,1)S(1)} %get-tuple-element.18), channel_id=1, source_target_pairs={{0,1},{1,0},{2,3},{3,2},{4,5},{5,4},{6,7},{7,6},{8,9},{9,8},{10,11... | collective-permute-start | bytes 491528 | tf_op jit(solution)/shard_map/ppermute | solution.py:276
  44.7 8.9 %collective-permute-start.24 = (bf16[2,256,128]{2,1,0:T(8,128)(2,1)S(1)}, bf16[2,256,128]{2,1,0:T(8,128)(2,1)S(1)}, u32[]{:S(2)}, u32[]{:S(2)}) collective-permute-start(bf16[2,256,128]{2,1,0:T(8,128)(2,1)S(1)} %fusion.10), channel_id=1, source_target_pairs={{0,2},{1,3},{2,0},{3,1},{4,6},{5,7},{6,4},{7,5},{8,10},{9,11},{10,... | collective-permute-start | bytes 393224 | tf_op jit(solution)/shard_map/ppermute | solution.py:276
  48.4 6.4 %collective-permute-start.20 = (bf16[2,256,128]{2,1,0:T(8,128)(2,1)S(1)}, bf16[2,256,128]{2,1,0:T(8,128)(2,1)S(1)}, u32[]{:S(2)}, u32[]{:S(2)}) collective-permute-start(bf16[2,256,128]{2,1,0:T(8,128)(2,1)S(1)} %get-tuple-element.43), channel_id=1, source_target_pairs={{0,8},{1,9},{2,10},{3,11},{4,12},{5,13},{6,14},{7,15},{8,0},{9,1},... | collective-permute-start | bytes 393224 | tf_op jit(solution)/shard_map/ppermute | solution.py:276
  48.8 7.8 %collective-permute-start.21 = (bf16[2,256,128]{2,1,0:T(8,128)(2,1)S(1)}, bf16[2,256,128]{2,1,0:T(8,128)(2,1)S(1)}, u32[]{:S(2)}, u32[]{:S(2)}) collective-permute-start(bf16[2,256,128]{2,1,0:T(8,128)(2,1)S(1)} %get-tuple-element.41), channel_id=1, source_target_pairs={{0,16},{1,17},{2,18},{3,19},{4,20},{5,21},{6,22},{7,23},{8,24},{9,... | collective-permute-start | bytes 393224 | tf_op jit(solution)/shard_map/ppermute | solution.py:276
  50.4 6.2 %collective-permute-start.22 = (bf16[2,256,128]{2,1,0:T(8,128)(2,1)S(1)}, bf16[2,256,128]{2,1,0:T(8,128)(2,1)S(1)}, u32[]{:S(2)}, u32[]{:S(2)}) collective-permute-start(bf16[2,256,128]{2,1,0:T(8,128)(2,1)S(1)} %get-tuple-element.42), channel_id=1, source_target_pairs={{0,24},{1,25},{2,26},{3,27},{4,28},{5,29},{6,30},{7,31},{8,16},{9,... | collective-permute-start | bytes 393224 | tf_op jit(solution)/shard_map/ppermute | solution.py:276
